TPU v7x, 32 devices: a whole 2x2x4 slice. The times are simulated.
32 devices in a mesh: board: 16 (over z, y, core), seq: 2 (over x).
Axes of the slice: x: 2, y: 2, z: 4, core: 2. Of those that a mesh axis runs over, the one named last changes fastest.
Arguments:
- board_cards: int32 [16, 6, 5], P('board'), may hold values from 0 to 51, as said below
- hand_ranks: int32 [16, 6, 1326], P('board'), may hold values from 0 to 7461
- river_count: int32 [16], P('board'), may hold values from 1 to 6, as said below
- reach_in: bfloat16 [16, 24, 1326], P('board', 'seq'), may hold values from 0 to 1
- strategy: bfloat16 [16, 6, 96, 1326], P('board', None, 'seq'), may hold values from 0.049804688 to 1
- parent_node: int32 [96], P('seq'), may hold values from 0 to 23, as said below
- pot_size: float32 [96], P('seq'), may hold values from 0.5 to 4
- flop_weight: float32 [16], P('board'), may hold values from 0.1 to 10
Outputs:
- turn_value: float32 [16, 24, 1326], P('board', 'seq')
- root_value: float32 [24, 1326], P('seq')
Inputs may be any that keep to these rules, and one draw needn't show every extreme that they name: `board_cards`: the five cards of a river board are distinct; the first three are the flop group's and the same on all of its river boards. `river_count`: some flop group has 6 live river boards; slots at or past the count hold unused data. `parent_node`: each river root is the parent of exactly 4 leaves.
All inputs are finite; a program needn't handle non-finite values.
Results may differ from a plain program's by a relative error of at most 0.0003.
Values may be sent and summed in bfloat16 or wider, within the bound.
No kernel may reach another device: no remote copies, remote signals or barrier semaphores. Data moves between devices by JAX's collectives and lax.ppermute only.
A program may use at most 64 MiB of HBM per device.

v0:
```python
import functools

import jax
import jax.numpy as jnp
from jax import lax
from jax.experimental import pallas as pl
from jax.experimental.pallas import tpu as pltpu
from jax.sharding import PartitionSpec as P

DECK = 52
LANES = 128
MIB = 1024 * 1024


def round_up(value, step):
    return -(-value // step) * step


def hand_cards(padded):
    hand = lax.broadcasted_iota(jnp.int32, (1, padded), 1)
    low = jnp.zeros((1, padded), jnp.int32)
    start = jnp.zeros((1, padded), jnp.int32)
    first = 0
    for card in range(DECK - 1):
        if card:
            low = jnp.where(hand >= first, card, low)
            start = jnp.where(hand >= first, first, start)
        first += DECK - 1 - card
    high = hand - start + low + 1
    real = hand < first
    return jnp.where(real, low, -1), jnp.where(real, high, -1)


def pad_rows(rows):
    return 1 << max(rows - 1, 0).bit_length()


def tile_count(rows, hands):
    full, rest = divmod(rows, 8)
    whole, tail = divmod(hands, LANES)
    count = full * whole
    if rest:
        count += -(-whole // (8 // pad_rows(rest)))
    groups = full + (rest > 0)
    if tail:
        count += -(-groups // 2) if tail <= LANES // 2 else groups
    return count


def pack_tiles(value, rows, hands):
    full, rest = divmod(rows, 8)
    whole, tail = divmod(hands, LANES)
    tiles = [
        value[8 * group : 8 * group + 8, LANES * at : LANES * (at + 1)]
        for group in range(full)
        for at in range(whole)
    ]
    if rest:
        part = pad_rows(rest)
        each = 8 // part
        for start in range(0, whole, each):
            pieces = [
                value[8 * full : 8 * full + part, LANES * at : LANES * (at + 1)]
                for at in range(start, min(start + each, whole))
            ]
            if len(pieces) < each:
                pieces.append(jnp.zeros((8 - part * len(pieces), LANES), value.dtype))
            tiles.append(jnp.concatenate(pieces, axis=0) if len(pieces) > 1 else pieces[0])
    if tail:
        groups = full + (rest > 0)
        tails = [value[8 * group : 8 * group + 8, LANES * whole :] for group in range(groups)]
        if tail <= LANES // 2:
            for at in range(0, groups, 2):
                tile = tails[at]
                if at + 1 < groups:
                    tile = tile + pltpu.roll(tails[at + 1], LANES // 2, 1)
                tiles.append(tile)
        else:
            tiles.extend(tails)
    return tiles


def unpack_tiles(tiles, rows, hands):
    full, rest = divmod(rows, 8)
    whole, tail = divmod(hands, LANES)
    groups = [[tiles[group * whole + at] for at in range(whole)] for group in range(full)]
    used = full * whole
    if rest:
        part = pad_rows(rest)
        each = 8 // part
        last = []
        for at in range(whole):
            tile = tiles[used + at // each]
            begin = part * (at % each)
            last.append(pltpu.roll(tile, (8 - begin) % 8, 0) if begin else tile)
        used += -(-whole // each)
        groups.append(last)
    if tail:
        for at, group in enumerate(groups):
            if tail <= LANES // 2:
                tile = tiles[used + at // 2]
                if at % 2:
                    tile = pltpu.roll(tile, LANES // 2, 1)
            else:
                tile = tiles[used + at]
            group.append(tile[:, :tail])
    return [jnp.concatenate(group, axis=1) for group in groups]


def copy_all(pairs, sems):
    copies = [
        pltpu.make_async_copy(source, target, sems.at[at])
        for at, (source, target) in enumerate(pairs)
    ]
    for copy in copies:
        copy.start()
    return copies


def pack_kernel(
    rounds,
    seq_count,
    strat_ref,
    reach_ref,
    parent_ref,
    pot_ref,
    rank_ref,
    board_ref,
    *refs,
):
    packs, info_ref = refs[:seq_count], refs[seq_count]
    strat_tmp, reach_tmp, parent_tmp, pot_tmp, rank_tmp, board_tmp, small, info = refs[
        seq_count + 1 : -2
    ]
    in_sems, out_sems = refs[-2:]
    rivers, leaves, hands = strat_ref.shape[1:]
    padded = info.shape[-1]
    here = lax.axis_index("seq")
    loads = [
        (reach_ref, reach_tmp),
        (parent_ref, parent_tmp),
        (pot_ref, pot_tmp),
        (rank_ref, rank_tmp),
        (board_ref, board_tmp),
    ]
    first = len(loads)
    stores = []
    order = [step % seq_count for step in range(1, seq_count + 1)]
    for step in order:
        owner = lax.rem(here + step, seq_count)
        for at in range(rounds):
            river = jnp.minimum(at * seq_count + owner, rivers - 1)
            held = strat_tmp.at[step, pl.ds(at * leaves, leaves)]
            loads.append((strat_ref.at[0, river], held))
            stores.append((held, packs[step].at[pl.ds(at * leaves, leaves)]))
    loads = copy_all(loads, in_sems)

    low, high = hand_cards(padded)
    for copy in loads[:3]:
        copy.wait()
    pot = pot_tmp[...]
    top = pot.astype(jnp.bfloat16).astype(jnp.float32)
    middle = (pot - top).astype(jnp.bfloat16).astype(jnp.float32)
    labels = jnp.concatenate(
        [parent_tmp[...].astype(jnp.float32), top, middle, pot - top - middle], axis=0
    )
    extra, nodes = small.shape[0], reach_tmp.shape[1]
    wide = jnp.concatenate([labels, jnp.zeros((4, hands - leaves), jnp.float32)], axis=1)
    rows = [reach_tmp[0].astype(jnp.float32), wide]
    if extra > nodes + 4:
        rows.append(jnp.zeros((extra - nodes - 4, hands), jnp.float32))
    small[...] = jnp.concatenate(rows, axis=0).astype(jnp.bfloat16)
    stores += [(small, pack.at[pl.ds(rounds * leaves, extra)]) for pack in packs]
    stores += [(info, info_ref)]
    stores = [
        pltpu.make_async_copy(source, target, out_sems.at[at])
        for at, (source, target) in enumerate(stores)
    ]
    for copy in stores[-1 - seq_count : -1]:
        copy.start()
    for at in range((seq_count - 1) * rounds):
        loads[first + at].wait()
        stores[at].start()

    for copy in loads[3:first]:
        copy.wait()
    info[...] = jnp.zeros_like(info)
    for at in range(rounds):
        river = jnp.minimum(at * seq_count + here, rivers - 1)
        info[at : at + 1, :hands] = rank_tmp[river].astype(jnp.float32)
        live = jnp.where(low >= 0, 1.0, 0.0)
        for slot in range(board_tmp.shape[0]):
            card = board_tmp[slot, 0, river]
            live = jnp.where((low == card) | (high == card), 0.0, live)
        info[rounds + at : rounds + at + 1, :] = live
    stores[-1].start()
    for at in range((seq_count - 1) * rounds, seq_count * rounds):
        loads[first + at].wait()
        stores[at].start()
    for copy in stores:
        copy.wait()


def build_kernel(
    rounds,
    seq_count,
    count_ref,
    weight_ref,
    info_ref,
    pack_ref,
    payoff_ref,
    own_ref,
    live_ref,
    holds,
    apart,
    sem,
):
    padded = payoff_ref.shape[-1]
    hands = pack_ref.shape[-1]
    here = lax.axis_index("seq")
    handed = pltpu.make_async_copy(pack_ref, own_ref, sem)
    handed.start()
    live_count = count_ref[0]
    live_rounds = lax.div(live_count - here + seq_count - 1, seq_count)
    live_ref[...] = jnp.zeros_like(live_ref)
    live_ref[:rounds, :] = info_ref[rounds : 2 * rounds, :]
    live_ref[rounds : rounds + 1, :] = 1.0 / (
        hands * jnp.full((1, padded), live_count.astype(jnp.float32))
    )
    live_ref[rounds + 1 : rounds + 2, :] = jnp.full(
        (1, padded), live_rounds.astype(jnp.float32)
    )
    live_ref[rounds + 2 : rounds + 3, :] = jnp.full(
        (1, padded), weight_ref[0] / lax.axis_size("board")
    )

    low, high = hand_cards(padded)
    card = lax.broadcasted_iota(jnp.int32, (holds.shape[0], padded), 0)
    holds[...] = jnp.where((card == low) | (card == high), 1.0, 0.0).astype(jnp.bfloat16)

    def mask_rows(start):
        shared = lax.dot_general(
            holds[:, start : start + LANES],
            holds[...],
            (((0,), (0,)), ((), ())),
            preferred_element_type=jnp.float32,
        )
        apart[start : start + LANES, :] = jnp.maximum(1.0 - shared, 0.0).astype(jnp.bfloat16)

    mask_rows(0)
    for start in range(0, padded, LANES):
        if start + LANES < padded:
            mask_rows(start + LANES)
        rows = slice(start, start + LANES)
        columns = [
            jnp.broadcast_to(info_ref[at : at + 1, rows], (LANES, LANES)).T
            for at in range(rounds)
        ]
        for lane in range(0, padded, LANES):
            here_lanes = slice(lane, lane + LANES)
            mask = apart[rows, here_lanes]
            for at in range(rounds):
                gap = (info_ref[at : at + 1, here_lanes] - columns[at]).astype(jnp.bfloat16)
                payoff_ref[at, rows, here_lanes] = jnp.maximum(jnp.minimum(gap, mask), -mask)
    handed.wait()


def value_kernel(rounds, seq_count, nodes, leaves, *refs):
    payoff_ref, own_ref, live_ref = refs[:3]
    came = refs[3 : 3 + seq_count - 1]
    outs, (total, reach_all) = refs[3 + seq_count - 1 : -2], refs[-2:]
    hands = own_ref.shape[-1]
    padded = payoff_ref.shape[-1]
    local_leaves, local_nodes = leaves // seq_count, nodes // seq_count
    here = lax.axis_index("seq")
    packs = (own_ref,) + tuple(came)
    base = rounds * local_leaves

    reach, places, pots = [], [], []
    for pack in packs:
        small = pack[base:, :].astype(jnp.float32)
        reach.append(small[:local_nodes])
        labels = small[local_nodes : local_nodes + 4, :LANES]
        parent = labels[0:1]
        place = parent
        for owner in range(seq_count):
            inside = (parent >= owner * local_nodes) & (parent < (owner + 1) * local_nodes)
            move = (lax.rem(here - owner + seq_count, seq_count) - owner) * local_nodes
            place = jnp.where(inside, parent + move.astype(jnp.float32), place)
        lane = lax.broadcasted_iota(jnp.int32, (1, LANES), 1)
        places.append(jnp.where(lane < local_leaves, place, -1.0))
        pots.append(labels[1:2] + labels[2:3] + labels[3:4])

    sub = lax.broadcasted_iota(jnp.int32, (LANES, LANES), 0)
    lane = lax.broadcasted_iota(jnp.int32, (LANES, LANES), 1)
    columns = [jnp.broadcast_to(place, (LANES, LANES)).T for place in places]
    picks = []
    pot_sorted = jnp.zeros((leaves, 1), jnp.float32)
    target = lax.broadcasted_iota(jnp.int32, (leaves, LANES), 0).astype(jnp.float32)
    for at in range(seq_count):
        nth = jnp.sum(
            jnp.where((columns[at] == places[at]) & (sub < lane), 1.0, 0.0), axis=0, keepdims=True
        )
        for before in range(at):
            nth = nth + jnp.sum(
                jnp.where(columns[before] == places[at], 1.0, 0.0), axis=0, keepdims=True
            )
        slot = jnp.where(places[at] >= 0.0, nth * nodes + places[at], -1.0)
        pick = jnp.where(target == slot, 1.0, 0.0)
        pot_sorted = pot_sorted + jnp.sum(pick * pots[at], axis=1, keepdims=True)
        picks.append(pick.astype(jnp.bfloat16)[:, :local_leaves])
    lookup = jnp.concatenate(reach * (leaves // nodes), axis=0)

    reach_all[...] = jnp.zeros_like(reach_all)
    total[...] = jnp.zeros_like(total)
    live_rounds = jnp.max(live_ref[rounds + 1 : rounds + 2, :LANES])
    for at in range(rounds):

        @pl.when(live_rounds > at)
        def _():
            rows = slice(at * local_leaves, (at + 1) * local_leaves)
            live = live_ref[at : at + 1, :]
            strat = jnp.dot(picks[0], own_ref[rows, :], preferred_element_type=jnp.float32)
            for pick, pack in zip(picks[1:], came):
                strat = strat + jnp.dot(pick, pack[rows, :], preferred_element_type=jnp.float32)
            reach_all[:, :hands] = (lookup * strat * live[:, :hands]).astype(jnp.bfloat16)
            shown = jnp.dot(reach_all[...], payoff_ref[at], preferred_element_type=jnp.float32)
            value = shown * pot_sorted
            best = value[:nodes]
            for row in range(nodes, leaves, nodes):
                best = jnp.maximum(best, value[row : row + nodes])
            gain = best * (live * live_ref[rounds : rounds + 1, :])
            total[...] += gain

    outs[-1][...] = jnp.broadcast_to(live_ref[rounds + 2 : rounds + 3, :LANES], (8, LANES))
    short = round_up(local_nodes, 8) - local_nodes
    for step in range(seq_count):
        rows = total[step * local_nodes : (step + 1) * local_nodes, :]
        if short:
            rows = jnp.concatenate([rows, jnp.zeros((short, padded), jnp.float32)], axis=0)
        for at, tile in enumerate(pack_tiles(rows, local_nodes, hands)):
            outs[step][at] = tile


def share_kernel(rows, hands, tiles_ref, out_ref, tmp, sem):
    tiles = [tiles_ref[at] for at in range(tile_count(rows, hands))]
    for at, group in enumerate(unpack_tiles(tiles, rows, hands)):
        for row in range(8 * at, min(8 * at + 8, rows)):
            tmp[row] = group[row - 8 * at : row - 8 * at + 1]
    copy = pltpu.make_async_copy(tmp, out_ref, sem)
    copy.start()
    copy.wait()


def root_kernel(rows, hands, mine_ref, came_ref, out_ref, tmp, sem):
    tiles = [mine_ref[at] + came_ref[at] for at in range(tile_count(rows, hands))]
    for at, group in enumerate(unpack_tiles(tiles, rows, hands)):
        height = min(8, rows - 8 * at)
        tmp[8 * at : 8 * at + height, :] = group[:height]
    copy = pltpu.make_async_copy(tmp, out_ref, sem)
    copy.start()
    copy.wait()


def body(
    board_cards, hand_ranks, river_count, reach_in, strategy, parent_node, pot_size, flop_weight
):
    seq_count = lax.axis_size("seq")
    board_count = lax.axis_size("board")
    rivers, local_leaves, hands = strategy.shape[1:]
    local_nodes = reach_in.shape[1]
    nodes, leaves = local_nodes * seq_count, local_leaves * seq_count
    rounds = -(-rivers // seq_count)
    padded = round_up(hands, LANES)
    anywhere = pl.BlockSpec(memory_space=pltpu.HBM)
    vmem = pl.BlockSpec(memory_space=pltpu.VMEM)
    params = pltpu.CompilerParams(vmem_limit_bytes=16 * MIB)

    def shift(array, step):
        return lax.ppermute(
            array, "seq", [(at, (at + step) % seq_count) for at in range(seq_count)]
        )

    small_rows = round_up(local_nodes + 4, 16)
    pack_rows = rounds * local_leaves + small_rows
    info_rows = round_up(2 * rounds, 8)
    own_pack, *packs, info = pl.pallas_call(
        functools.partial(pack_kernel, rounds, seq_count),
        out_shape=[jax.ShapeDtypeStruct((pack_rows, hands), jnp.bfloat16)] * seq_count
        + [jax.ShapeDtypeStruct((info_rows, padded), jnp.float32)],
        in_specs=[anywhere] * 6,
        out_specs=[anywhere] * (seq_count + 1),
        scratch_shapes=[
            pltpu.VMEM((seq_count, rounds * local_leaves, hands), jnp.bfloat16),
            pltpu.VMEM(reach_in.shape, jnp.bfloat16),
            pltpu.VMEM((1, local_leaves), jnp.int32),
            pltpu.VMEM((1, local_leaves), jnp.float32),
            pltpu.VMEM((rivers, 1, hands), jnp.int32),
            pltpu.SMEM((board_cards.shape[2], 1, rivers), jnp.int32),
            pltpu.VMEM((small_rows, hands), jnp.bfloat16),
            pltpu.VMEM((info_rows, padded), jnp.float32),
            pltpu.SemaphoreType.DMA((5 + rounds * seq_count,)),
            pltpu.SemaphoreType.DMA((1 + (1 + rounds) * seq_count,)),
        ],
        compiler_params=pltpu.CompilerParams(vmem_limit_bytes=60 * MIB),
        name="pack",
    )(
        strategy,
        reach_in,
        parent_node[None],
        pot_size[None],
        hand_ranks.transpose(1, 0, 2),
        board_cards.transpose(2, 0, 1),
    )
    came = [shift(pack, step) for step, pack in enumerate(packs, 1)]

    smem = pl.BlockSpec(memory_space=pltpu.SMEM)
    payoff, own, live = pl.pallas_call(
        functools.partial(build_kernel, rounds, seq_count),
        out_shape=[
            jax.ShapeDtypeStruct((rounds, padded, padded), jnp.bfloat16),
            jax.ShapeDtypeStruct((pack_rows, hands), jnp.bfloat16),
            jax.ShapeDtypeStruct((round_up(rounds + 3, 8), padded), jnp.float32),
        ],
        in_specs=[smem, smem, vmem, vmem],
        out_specs=[vmem] * 3,
        scratch_shapes=[
            pltpu.VMEM((round_up(DECK, 16), padded), jnp.bfloat16),
            pltpu.VMEM((padded, padded), jnp.bfloat16),
            pltpu.SemaphoreType.DMA,
        ],
        compiler_params=pltpu.CompilerParams(vmem_limit_bytes=30 * MIB),
        cost_estimate=pl.CostEstimate(
            flops=10 * rounds * padded * padded, bytes_accessed=4 * padded * padded, transcendentals=0
        ),
        name="build",
    )(river_count, flop_weight, info, own_pack)

    count = tile_count(local_nodes, hands)
    *shares, weight = pl.pallas_call(
        functools.partial(value_kernel, rounds, seq_count, nodes, leaves),
        out_shape=[jax.ShapeDtypeStruct((count, 8, LANES), jnp.float32)] * seq_count
        + [jax.ShapeDtypeStruct((8, LANES), jnp.float32)],
        in_specs=[vmem] * (3 + seq_count - 1),
        out_specs=[vmem] * (seq_count + 1),
        scratch_shapes=[
            pltpu.VMEM((nodes, padded), jnp.float32),
            pltpu.VMEM((leaves, padded), jnp.bfloat16),
        ],
        compiler_params=params,
        name="value",
    )(payoff, own, live, *came)

    share = shares[0]
    for step in range(1, seq_count):
        share = share + shift(shares[step], -step)
    root = share * weight[None]
    step = 1
    while True:
        came = lax.ppermute(root, "board", [(at, at ^ step) for at in range(board_count)])
        step *= 2
        if step >= board_count:
            break
        root = root + came

    turn_value = pl.pallas_call(
        functools.partial(share_kernel, local_nodes, hands),
        out_shape=jax.ShapeDtypeStruct((local_nodes, 1, hands), jnp.float32),
        in_specs=[vmem],
        out_specs=anywhere,
        scratch_shapes=[
            pltpu.VMEM((local_nodes, 1, hands), jnp.float32),
            pltpu.SemaphoreType.DMA,
        ],
        compiler_params=params,
        name="share",
    )(share)
    root_value = pl.pallas_call(
        functools.partial(root_kernel, local_nodes, hands),
        out_shape=jax.ShapeDtypeStruct((local_nodes, hands), jnp.float32),
        in_specs=[vmem] * 2,
        out_specs=anywhere,
        scratch_shapes=[pltpu.VMEM((local_nodes, hands), jnp.float32), pltpu.SemaphoreType.DMA],
        compiler_params=params,
        name="root",
    )(root, came)
    return (turn_value.transpose(1, 0, 2), root_value)


def solution(mesh):
    return jax.shard_map(
        body,
        mesh=mesh,
        in_specs=(
            P("board", None, None),
            P("board", None, None),
            P("board"),
            P("board", "seq", None),
            P("board", None, "seq", None),
            P("seq"),
            P("seq"),
            P("board"),
        ),
        out_specs=(P("board", "seq", None), P("seq", None)),
        check_vma=False,
    )
```

profile of v0, /device:TPU:0, one launch (start us, length us, event | category | flops | bytes accessed | tf_op | source)
XLA Modules:
  0.0 39.5 jit_solution(5414924445320742670)
XLA Ops:
  0.6 2.2 %pack.1 = (bf16[160,1326]{1,0:T(8,128)(2,1)}, bf16[160,1326]{1,0:T(8,128)(2,1)}, f32[8,1408]{1,0:T(8,128)}) custom-call(bf16[1,6,48,1326]{3,2,1,0:T(8,128)(2,1)} %strat_ref.1, bf16[1,12,1326]{2,1,0:T(8,128)(2,1)} %reach_ref.1, s32[1,48]{1,0:T(1,128)} %bitcast.8, f32[1,48]{1,0:T(1,128)} %bitcast.9, s32[6,1,1326]{2,1,0:T(1,128)} %bitcast.6, s32[5,1,6]{2,1,0:T(1,128)} %bitcast.7), custom_call_target="tpu_custom_call" | custom-call | tf_op jit(solution)/shard_map/pack/pallas_call | solution.py:387
  2.8 3.0 %collective-permute-start = (bf16[160,1326]{1,0:T(8,128)(2,1)}, bf16[160,1326]{1,0:T(8,128)(2,1)S(1)}, u32[]{:S(2)}, u32[]{:S(2)}) collective-permute-start(bf16[160,1326]{1,0:T(8,128)(2,1)} %get-tuple-element.16), channel_id=1, source_target_pairs={{0,1},{1,0},{2,3},{3,2},{4,5},{5,4},{6,7},{7,6},{8,9},{9,8},{10,11... | collective-permute-start | bytes 1272968 | tf_op jit(solution)/shard_map/ppermute | solution.py:380
  7.1 0.0 copy-start
  7.1 1.0 %copy-done = bf16[160,1326]{1,0:T(8,128)(2,1)S(1)} copy-done((bf16[160,1326]{1,0:T(8,128)(2,1)S(1)}, bf16[160,1326]{1,0:T(8,128)(2,1)}, u32[]{:S(2)}) %copy-start) | copy-done | bytes 424344
  8.2 0.0 copy-start.1
  8.2 0.8 %copy-done.1 = f32[8,1408]{1,0:T(8,128)S(1)} copy-done((f32[8,1408]{1,0:T(8,128)S(1)}, f32[8,1408]{1,0:T(8,128)}, u32[]{:S(2)}) %copy-start.1) | copy-done | bytes 45080
  8.9 5.5 %build.1 = (bf16[3,1408,1408]{2,1,0:T(8,128)(2,1)S(1)}, bf16[160,1326]{1,0:T(8,128)(2,1)S(1)}, f32[8,1408]{1,0:T(8,128)S(1)}) custom-call(s32[1]{0:T(128)S(6)} %copy.10.count_ref, f32[1]{0:T(128)S(6)} %copy.11.weight_ref, f32[8,1408]{1,0:T(8,128)S(1)} %copy-done.1, bf16[160,1326]{1,0:T(8,128)(2,1)S(1)} %copy-done), custom_call_target="tpu_custom_call" | custom-call | flops 59473920 | bytes 7929856 | tf_op jit(solution)/shard_map/build/pallas_call | solution.py:418
  14.4 2.0 %collective-permute-done.refs_3_ = bf16[160,1326]{1,0:T(8,128)(2,1)S(1)} collective-permute-done((bf16[160,1326]{1,0:T(8,128)(2,1)}, bf16[160,1326]{1,0:T(8,128)(2,1)S(1)}, u32[]{:S(2)}, u32[]{:S(2)}) %collective-permute-start) | collective-permute-done | bytes 424352 | tf_op jit(solution)/shard_map/ppermute | solution.py:380
  16.4 1.3 %value.1 = (f32[16,8,128]{2,1,0:T(8,128)S(1)}, f32[16,8,128]{2,1,0:T(8,128)S(1)}, f32[8,128]{1,0:T(8,128)S(1)}) custom-call(bf16[3,1408,1408]{2,1,0:T(8,128)(2,1)S(1)} %get-tuple-element.13.refs_0_, bf16[160,1326]{1,0:T(8,128)(2,1)S(1)} %get-tuple-element.14.refs_1_, f32[8,1408]{1,0:T(8,128)S(1)} %get-tuple-element.15.refs_2_, ...), custom_call_target="tpu_custom_call" | custom-call | tf_op jit(solution)/shard_map/value/pallas_call | solution.py:440
  17.7 1.8 %collective-permute-start.1 = (f32[16,8,128]{2,1,0:T(8,128)S(1)}, f32[16,8,128]{2,1,0:T(8,128)S(1)}, u32[]{:S(2)}, u32[]{:S(2)}) collective-permute-start(f32[16,8,128]{2,1,0:T(8,128)S(1)} %get-tuple-element.18), channel_id=1, source_target_pairs={{0,1},{1,0},{2,3},{3,2},{4,5},{5,4},{6,7},{7,6},{8,9},{9,8},{10,11... | collective-permute-start | bytes 196616 | tf_op jit(solution)/shard_map/ppermute | solution.py:380
  19.5 2.5 %collective-permute-done.1 = f32[16,8,128]{2,1,0:T(8,128)S(1)} collective-permute-done((f32[16,8,128]{2,1,0:T(8,128)S(1)}, f32[16,8,128]{2,1,0:T(8,128)S(1)}, u32[]{:S(2)}, u32[]{:S(2)}) %collective-permute-start.1) | collective-permute-done | bytes 65568 | tf_op jit(solution)/shard_map/ppermute | solution.py:380
  22.0 0.1 collective-permute-start.2
  22.1 1.2 %collective-permute-done.2 = f32[16,8,128]{2,1,0:T(8,128)S(1)} collective-permute-done((f32[16,8,128]{2,1,0:T(8,128)S(1)}, f32[16,8,128]{2,1,0:T(8,128)S(1)}, u32[]{:S(2)}, u32[]{:S(2)}) %collective-permute-start.2) | collective-permute-done | bytes 65568 | tf_op jit(solution)/shard_map/ppermute | solution.py:460
  23.4 2.8 %collective-permute-start.3 = (f32[16,8,128]{2,1,0:T(8,128)S(1)}, f32[16,8,128]{2,1,0:T(8,128)S(1)}, u32[]{:S(2)}, u32[]{:S(2)}) collective-permute-start(f32[16,8,128]{2,1,0:T(8,128)S(1)} %add.13), channel_id=1, source_target_pairs={{0,4},{2,6},{4,0},{6,2},{8,12},{10,14},{12,8},{14,10},{16,20},{18,... | collective-permute-start | bytes 196616 | tf_op jit(solution)/shard_map/ppermute | solution.py:460
  26.2 2.4 %collective-permute-done.3 = f32[16,8,128]{2,1,0:T(8,128)S(1)} collective-permute-done((f32[16,8,128]{2,1,0:T(8,128)S(1)}, f32[16,8,128]{2,1,0:T(8,128)S(1)}, u32[]{:S(2)}, u32[]{:S(2)}) %collective-permute-start.3) | collective-permute-done | bytes 65568 | tf_op jit(solution)/shard_map/ppermute | solution.py:460
  28.6 2.7 %collective-permute-start.4 = (f32[16,8,128]{2,1,0:T(8,128)S(1)}, f32[16,8,128]{2,1,0:T(8,128)S(1)}, u32[]{:S(2)}, u32[]{:S(2)}) collective-permute-start(f32[16,8,128]{2,1,0:T(8,128)S(1)} %add.14), channel_id=1, source_target_pairs={{0,8},{2,10},{4,12},{6,14},{8,0},{10,2},{12,4},{14,6},{16,24},{18,... | collective-permute-start | bytes 196616 | tf_op jit(solution)/shard_map/ppermute | solution.py:460
  31.3 2.2 %collective-permute-done.4 = f32[16,8,128]{2,1,0:T(8,128)S(1)} collective-permute-done((f32[16,8,128]{2,1,0:T(8,128)S(1)}, f32[16,8,128]{2,1,0:T(8,128)S(1)}, u32[]{:S(2)}, u32[]{:S(2)}) %collective-permute-start.4) | collective-permute-done | bytes 65568 | tf_op jit(solution)/shard_map/ppermute | solution.py:460
  33.5 2.4 %collective-permute-start.5 = (f32[16,8,128]{2,1,0:T(8,128)S(1)}, f32[16,8,128]{2,1,0:T(8,128)S(1)}, u32[]{:S(2)}, u32[]{:S(2)}) collective-permute-start(f32[16,8,128]{2,1,0:T(8,128)S(1)} %add.15.mine_ref), channel_id=1, source_target_pairs={{0,16},{2,18},{4,20},{6,22},{8,24},{10,26},{12,28},{14,30},{16,0},... | collective-permute-start | bytes 196616 | tf_op jit(solution)/shard_map/ppermute | solution.py:460
  35.9 0.7 %share.1 = f32[12,1,1326]{2,1,0:T(1,128)} custom-call(f32[16,8,128]{2,1,0:T(8,128)S(1)} %get-tuple-element.21.tiles_ref), custom_call_target="tpu_custom_call" | custom-call | tf_op jit(solution)/shard_map/share/pallas_call | solution.py:466
  36.7 2.1 %collective-permute-done.5.came_ref = f32[16,8,128]{2,1,0:T(8,128)S(1)} collective-permute-done((f32[16,8,128]{2,1,0:T(8,128)S(1)}, f32[16,8,128]{2,1,0:T(8,128)S(1)}, u32[]{:S(2)}, u32[]{:S(2)}) %collective-permute-start.5) | collective-permute-done | bytes 65568 | tf_op jit(solution)/shard_map/ppermute | solution.py:460
  38.8 0.7 %root.1 = f32[12,1326]{1,0:T(8,128)} custom-call(f32[16,8,128]{2,1,0:T(8,128)S(1)} %add.15.mine_ref, f32[16,8,128]{2,1,0:T(8,128)S(1)} %collective-permute-done.5.came_ref), custom_call_target="tpu_custom_call" | custom-call | tf_op jit(solution)/shard_map/root/pallas_call | solution.py:478
  (4 shorter events, 0.0 us)
Async XLA Ops:
  2.8 13.6 %collective-permute-start = (bf16[160,1326]{1,0:T(8,128)(2,1)}, bf16[160,1326]{1,0:T(8,128)(2,1)S(1)}, u32[]{:S(2)}, u32[]{:S(2)}) collective-permute-start(bf16[160,1326]{1,0:T(8,128)(2,1)} %get-tuple-element.16), channel_id=1, source_target_pairs={{0,1},{1,0},{2,3},{3,2},{4,5},{5,4},{6,7},{7,6},{8,9},{9,8},{10,11... | collective-permute-start | bytes 1272968 | tf_op jit(solution)/shard_map/ppermute | solution.py:380
  7.1 1.0 %copy-start = (bf16[160,1326]{1,0:T(8,128)(2,1)S(1)}, bf16[160,1326]{1,0:T(8,128)(2,1)}, u32[]{:S(2)}) copy-start(bf16[160,1326]{1,0:T(8,128)(2,1)} %get-tuple-element.12.pack_ref) | copy-start | bytes 1272964
  8.2 0.8 %copy-start.1 = (f32[8,1408]{1,0:T(8,128)S(1)}, f32[8,1408]{1,0:T(8,128)}, u32[]{:S(2)}) copy-start(f32[8,1408]{1,0:T(8,128)} %get-tuple-element.11.info_ref) | copy-start | bytes 135172
  17.7 4.3 %collective-permute-start.1 = (f32[16,8,128]{2,1,0:T(8,128)S(1)}, f32[16,8,128]{2,1,0:T(8,128)S(1)}, u32[]{:S(2)}, u32[]{:S(2)}) collective-permute-start(f32[16,8,128]{2,1,0:T(8,128)S(1)} %get-tuple-element.18), channel_id=1, source_target_pairs={{0,1},{1,0},{2,3},{3,2},{4,5},{5,4},{6,7},{7,6},{8,9},{9,8},{10,11... | collective-permute-start | bytes 196616 | tf_op jit(solution)/shard_map/ppermute | solution.py:380
  22.0 1.3 %collective-permute-start.2 = (f32[16,8,128]{2,1,0:T(8,128)S(1)}, f32[16,8,128]{2,1,0:T(8,128)S(1)}, u32[]{:S(2)}, u32[]{:S(2)}) collective-permute-start(f32[16,8,128]{2,1,0:T(8,128)S(1)} %get-tuple-element.20), channel_id=1, source_target_pairs={{0,2},{2,0},{4,6},{6,4},{8,10},{10,8},{12,14},{14,12},{16,18},{18,... | collective-permute-start | bytes 196616 | tf_op jit(solution)/shard_map/ppermute | solution.py:460
  23.4 5.2 %collective-permute-start.3 = (f32[16,8,128]{2,1,0:T(8,128)S(1)}, f32[16,8,128]{2,1,0:T(8,128)S(1)}, u32[]{:S(2)}, u32[]{:S(2)}) collective-permute-start(f32[16,8,128]{2,1,0:T(8,128)S(1)} %add.13), channel_id=1, source_target_pairs={{0,4},{2,6},{4,0},{6,2},{8,12},{10,14},{12,8},{14,10},{16,20},{18,... | collective-permute-start | bytes 196616 | tf_op jit(solution)/shard_map/ppermute | solution.py:460
  28.6 4.9 %collective-permute-start.4 = (f32[16,8,128]{2,1,0:T(8,128)S(1)}, f32[16,8,128]{2,1,0:T(8,128)S(1)}, u32[]{:S(2)}, u32[]{:S(2)}) collective-permute-start(f32[16,8,128]{2,1,0:T(8,128)S(1)} %add.14), channel_id=1, source_target_pairs={{0,8},{2,10},{4,12},{6,14},{8,0},{10,2},{12,4},{14,6},{16,24},{18,... | collective-permute-start | bytes 196616 | tf_op jit(solution)/shard_map/ppermute | solution.py:460
  33.5 5.2 %collective-permute-start.5 = (f32[16,8,128]{2,1,0:T(8,128)S(1)}, f32[16,8,128]{2,1,0:T(8,128)S(1)}, u32[]{:S(2)}, u32[]{:S(2)}) collective-permute-start(f32[16,8,128]{2,1,0:T(8,128)S(1)} %add.15.mine_ref), channel_id=1, source_target_pairs={{0,16},{2,18},{4,20},{6,22},{8,24},{10,26},{12,28},{14,30},{16,0},... | collective-permute-start | bytes 196616 | tf_op jit(solution)/shard_map/ppermute | solution.py:460
where the time goes:
time: 39.9 us; the launch traced here: 39.5 us
  starting transfers between devices  12.7 us (32%)
  waiting for transfers between devices  12.5 us (31%)
  Pallas kernels  10.4 us (26%)
  between operations  1.99 us (5%)
  local copies, waits for them, and re-layouts  1.8 us (5%)
    ppermute x4, waiting for transfers between devices, body(): lax.ppermute(root, 'board', [(at, at ^ step) for at in range(board_count)])  8.01 us
    ppermute x4, starting transfers between devices, body(): lax.ppermute(root, 'board', [(at, at ^ step) for at in range(board_count)])  7.97 us
    pallas_call x1, Pallas kernels, body(): pl.pallas_call(functools.partial(build_kernel, rounds, seq_count), out_sh...  5.45 us
    ppermute x2, starting transfers between devices, shift(): lax.ppermute(array, 'seq', [(at, (at + step) % seq_count) for at in range...  4.76 us
    ppermute x2, waiting for transfers between devices, shift(): lax.ppermute(array, 'seq', [(at, (at + step) % seq_count) for at in range...  4.51 us
    pallas_call x1, Pallas kernels, body(): pl.pallas_call(functools.partial(pack_kernel, rounds, seq_count), out_sha...  2.2 us
    unnamed x4, local copies, waits for them, and re-layouts  1.8 us
    pallas_call x1, Pallas kernels, body(): pl.pallas_call(functools.partial(value_kernel, rounds, seq_count, nodes,...  1.32 us
  transfers between devices with their start and end apart: 6, of which 6 were waited for; matrix products, arithmetic and copies ran while one was open for 0% of the time, Pallas kernels for 16%

commit v1 on v0

--- a/solution.py
+++ b/solution.py
@@ -120,71 +120,65 @@
 def pack_kernel(
     rounds,
     seq_count,
-    strat_ref,
     reach_ref,
     parent_ref,
     pot_ref,
     rank_ref,
     board_ref,
-    *refs,
+    count_ref,
+    weight_ref,
+    small_ref,
+    info_ref,
+    reach_tmp,
+    parent_tmp,
+    pot_tmp,
+    rank_tmp,
+    board_tmp,
+    count_tmp,
+    weight_tmp,
+    small,
+    info,
+    sems,
+    out_sems,
 ):
-    packs, info_ref = refs[:seq_count], refs[seq_count]
-    strat_tmp, reach_tmp, parent_tmp, pot_tmp, rank_tmp, board_tmp, small, info = refs[
-        seq_count + 1 : -2
-    ]
-    in_sems, out_sems = refs[-2:]
-    rivers, leaves, hands = strat_ref.shape[1:]
-    padded = info.shape[-1]
+    hands, padded = small.shape[-1], info.shape[-1]
+    nodes, leaves = reach_tmp.shape[1], parent_tmp.shape[-1]
+    rivers = rank_tmp.shape[0]
     here = lax.axis_index("seq")
-    loads = [
-        (reach_ref, reach_tmp),
-        (parent_ref, parent_tmp),
-        (pot_ref, pot_tmp),
-        (rank_ref, rank_tmp),
-        (board_ref, board_tmp),
-    ]
-    first = len(loads)
-    stores = []
-    order = [step % seq_count for step in range(1, seq_count + 1)]
-    for step in order:
-        owner = lax.rem(here + step, seq_count)
-        for at in range(rounds):
-            river = jnp.minimum(at * seq_count + owner, rivers - 1)
-            held = strat_tmp.at[step, pl.ds(at * leaves, leaves)]
-            loads.append((strat_ref.at[0, river], held))
-            stores.append((held, packs[step].at[pl.ds(at * leaves, leaves)]))
-    loads = copy_all(loads, in_sems)
-
+    loads = copy_all(
+        [
+            (reach_ref, reach_tmp),
+            (parent_ref, parent_tmp),
+            (pot_ref, pot_tmp),
+            (rank_ref, rank_tmp),
+            (board_ref, board_tmp),
+            (count_ref, count_tmp),
+            (weight_ref, weight_tmp),
+        ],
+        sems,
+    )
     low, high = hand_cards(padded)
+    info[...] = jnp.zeros_like(info)
     for copy in loads[:3]:
         copy.wait()
     pot = pot_tmp[...]
+    parent = parent_tmp[...].astype(jnp.float32)
+    reach = reach_tmp[0].astype(jnp.float32)
     top = pot.astype(jnp.bfloat16).astype(jnp.float32)
     middle = (pot - top).astype(jnp.bfloat16).astype(jnp.float32)
-    labels = jnp.concatenate(
-        [parent_tmp[...].astype(jnp.float32), top, middle, pot - top - middle], axis=0
-    )
-    extra, nodes = small.shape[0], reach_tmp.shape[1]
-    wide = jnp.concatenate([labels, jnp.zeros((4, hands - leaves), jnp.float32)], axis=1)
-    rows = [reach_tmp[0].astype(jnp.float32), wide]
+    labels = jnp.concatenate([parent, top, middle, pot - top - middle], axis=0)
+    rows = [reach, jnp.concatenate([labels, jnp.zeros((4, hands - leaves), jnp.float32)], axis=1)]
+    extra = small.shape[0]
     if extra > nodes + 4:
         rows.append(jnp.zeros((extra - nodes - 4, hands), jnp.float32))
     small[...] = jnp.concatenate(rows, axis=0).astype(jnp.bfloat16)
-    stores += [(small, pack.at[pl.ds(rounds * leaves, extra)]) for pack in packs]
-    stores += [(info, info_ref)]
-    stores = [
-        pltpu.make_async_copy(source, target, out_sems.at[at])
-        for at, (source, target) in enumerate(stores)
-    ]
-    for copy in stores[-1 - seq_count : -1]:
-        copy.start()
-    for at in range((seq_count - 1) * rounds):
-        loads[first + at].wait()
-        stores[at].start()
-
-    for copy in loads[3:first]:
+    sent = pltpu.make_async_copy(small, small_ref, out_sems.at[0])
+    sent.start()
+
+    for copy in loads[3:]:
         copy.wait()
-    info[...] = jnp.zeros_like(info)
+    live_count = count_tmp[0]
+    base = 2 * rounds
     for at in range(rounds):
         river = jnp.minimum(at * seq_count + here, rivers - 1)
         info[at : at + 1, :hands] = rank_tmp[river].astype(jnp.float32)
@@ -193,46 +187,22 @@
             card = board_tmp[slot, 0, river]
             live = jnp.where((low == card) | (high == card), 0.0, live)
         info[rounds + at : rounds + at + 1, :] = live
-    stores[-1].start()
-    for at in range((seq_count - 1) * rounds, seq_count * rounds):
-        loads[first + at].wait()
-        stores[at].start()
-    for copy in stores:
-        copy.wait()
-
-
-def build_kernel(
-    rounds,
-    seq_count,
-    count_ref,
-    weight_ref,
-    info_ref,
-    pack_ref,
-    payoff_ref,
-    own_ref,
-    live_ref,
-    holds,
-    apart,
-    sem,
-):
+    info[base : base + 1, :] = 1.0 / (hands * jnp.full((1, padded), live_count.astype(jnp.float32)))
+    live_rounds = lax.div(live_count - here + seq_count - 1, seq_count)
+    info[base + 1 : base + 2, :] = jnp.full((1, padded), live_rounds.astype(jnp.float32))
+    info[base + 2 : base + 3, :] = jnp.full((1, padded), weight_tmp[0] / lax.axis_size("board"))
+    info[base + 3 : base + 4, :leaves] = parent
+    info[base + 4 : base + 5, :leaves] = pot
+    info[base + 5 : base + 5 + nodes, :hands] = reach
+    kept = pltpu.make_async_copy(info, info_ref, out_sems.at[1])
+    kept.start()
+    sent.wait()
+    kept.wait()
+
+
+def build_kernel(rounds, info_ref, payoff_ref, kept_ref, holds, apart):
     padded = payoff_ref.shape[-1]
-    hands = pack_ref.shape[-1]
-    here = lax.axis_index("seq")
-    handed = pltpu.make_async_copy(pack_ref, own_ref, sem)
-    handed.start()
-    live_count = count_ref[0]
-    live_rounds = lax.div(live_count - here + seq_count - 1, seq_count)
-    live_ref[...] = jnp.zeros_like(live_ref)
-    live_ref[:rounds, :] = info_ref[rounds : 2 * rounds, :]
-    live_ref[rounds : rounds + 1, :] = 1.0 / (
-        hands * jnp.full((1, padded), live_count.astype(jnp.float32))
-    )
-    live_ref[rounds + 1 : rounds + 2, :] = jnp.full(
-        (1, padded), live_rounds.astype(jnp.float32)
-    )
-    live_ref[rounds + 2 : rounds + 3, :] = jnp.full(
-        (1, padded), weight_ref[0] / lax.axis_size("board")
-    )
+    kept_ref[...] = info_ref[...]
 
     low, high = hand_cards(padded)
     card = lax.broadcasted_iota(jnp.int32, (holds.shape[0], padded), 0)
@@ -260,28 +230,33 @@
             here_lanes = slice(lane, lane + LANES)
             mask = apart[rows, here_lanes]
             for at in range(rounds):
-                gap = (info_ref[at : at + 1, here_lanes] - columns[at]).astype(jnp.bfloat16)
+                gap = (columns[at] - info_ref[at : at + 1, here_lanes]).astype(jnp.bfloat16)
                 payoff_ref[at, rows, here_lanes] = jnp.maximum(jnp.minimum(gap, mask), -mask)
-    handed.wait()
 
 
 def value_kernel(rounds, seq_count, nodes, leaves, *refs):
-    payoff_ref, own_ref, live_ref = refs[:3]
-    came = refs[3 : 3 + seq_count - 1]
-    outs, (total, reach_all) = refs[3 + seq_count - 1 : -2], refs[-2:]
+    payoff_ref, info_ref, own_ref = refs[:3]
+    came = refs[3 : 2 + seq_count]
+    smalls = refs[2 + seq_count : 1 + 2 * seq_count]
+    outs, (total, reach_all) = refs[1 + 2 * seq_count : -2], refs[-2:]
     hands = own_ref.shape[-1]
     padded = payoff_ref.shape[-1]
     local_leaves, local_nodes = leaves // seq_count, nodes // seq_count
     here = lax.axis_index("seq")
-    packs = (own_ref,) + tuple(came)
-    base = rounds * local_leaves
+    base = 2 * rounds
 
     reach, places, pots = [], [], []
-    for pack in packs:
-        small = pack[base:, :].astype(jnp.float32)
-        reach.append(small[:local_nodes])
-        labels = small[local_nodes : local_nodes + 4, :LANES]
-        parent = labels[0:1]
+    for at in range(seq_count):
+        if at == 0:
+            reach.append(info_ref[base + 5 : base + 5 + local_nodes, :hands])
+            parent = info_ref[base + 3 : base + 4, :LANES]
+            pots.append(info_ref[base + 4 : base + 5, :LANES])
+        else:
+            small = smalls[at - 1][...].astype(jnp.float32)
+            reach.append(small[:local_nodes])
+            labels = small[local_nodes : local_nodes + 4, :LANES]
+            parent = labels[0:1]
+            pots.append(labels[1:2] + labels[2:3] + labels[3:4])
         place = parent
         for owner in range(seq_count):
             inside = (parent >= owner * local_nodes) & (parent < (owner + 1) * local_nodes)
@@ -289,7 +264,6 @@
             place = jnp.where(inside, parent + move.astype(jnp.float32), place)
         lane = lax.broadcasted_iota(jnp.int32, (1, LANES), 1)
         places.append(jnp.where(lane < local_leaves, place, -1.0))
-        pots.append(labels[1:2] + labels[2:3] + labels[3:4])
 
     sub = lax.broadcasted_iota(jnp.int32, (LANES, LANES), 0)
     lane = lax.broadcasted_iota(jnp.int32, (LANES, LANES), 1)
@@ -313,26 +287,31 @@
 
     reach_all[...] = jnp.zeros_like(reach_all)
     total[...] = jnp.zeros_like(total)
-    live_rounds = jnp.max(live_ref[rounds + 1 : rounds + 2, :LANES])
+    live_rounds = jnp.max(info_ref[base + 1 : base + 2, :LANES])
     for at in range(rounds):
 
         @pl.when(live_rounds > at)
         def _():
             rows = slice(at * local_leaves, (at + 1) * local_leaves)
-            live = live_ref[at : at + 1, :]
+            live = info_ref[rounds + at : rounds + at + 1, :]
             strat = jnp.dot(picks[0], own_ref[rows, :], preferred_element_type=jnp.float32)
             for pick, pack in zip(picks[1:], came):
                 strat = strat + jnp.dot(pick, pack[rows, :], preferred_element_type=jnp.float32)
             reach_all[:, :hands] = (lookup * strat * live[:, :hands]).astype(jnp.bfloat16)
-            shown = jnp.dot(reach_all[...], payoff_ref[at], preferred_element_type=jnp.float32)
-            value = shown * pot_sorted
+            shown = lax.dot_general(
+                payoff_ref[at],
+                reach_all[...],
+                (((1,), (1,)), ((), ())),
+                preferred_element_type=jnp.float32,
+            )
+            value = shown.T * pot_sorted
             best = value[:nodes]
             for row in range(nodes, leaves, nodes):
                 best = jnp.maximum(best, value[row : row + nodes])
-            gain = best * (live * live_ref[rounds : rounds + 1, :])
+            gain = best * (live * info_ref[base : base + 1, :])
             total[...] += gain
 
-    outs[-1][...] = jnp.broadcast_to(live_ref[rounds + 2 : rounds + 3, :LANES], (8, LANES))
+    outs[-1][...] = jnp.broadcast_to(info_ref[base + 2 : base + 3, :LANES], (8, LANES))
     short = round_up(local_nodes, 8) - local_nodes
     for step in range(seq_count):
         rows = total[step * local_nodes : (step + 1) * local_nodes, :]
@@ -352,8 +331,13 @@
     copy.wait()
 
 
-def root_kernel(rows, hands, mine_ref, came_ref, out_ref, tmp, sem):
-    tiles = [mine_ref[at] + came_ref[at] for at in range(tile_count(rows, hands))]
+def root_kernel(rows, hands, mine_ref, other_ref, out_ref, tmp, sem):
+    first = lax.rem(lax.axis_index("board"), 2) == 0
+    lower = jnp.where(first, mine_ref[...], other_ref[...])
+    upper = jnp.where(first, other_ref[...], mine_ref[...])
+    half = mine_ref.shape[0]
+    count = tile_count(rows, hands)
+    tiles = [lower[at] for at in range(half)] + [upper[at] for at in range(count - half)]
     for at, group in enumerate(unpack_tiles(tiles, rows, hands)):
         height = min(8, rows - 8 * at)
         tmp[8 * at : 8 * at + height, :] = group[:height]
@@ -366,6 +350,7 @@
     board_cards, hand_ranks, river_count, reach_in, strategy, parent_node, pot_size, flop_weight
 ):
     seq_count = lax.axis_size("seq")
+    seq_here = lax.axis_index("seq")
     board_count = lax.axis_size("board")
     rivers, local_leaves, hands = strategy.shape[1:]
     local_nodes = reach_in.shape[1]
@@ -381,67 +366,85 @@
             array, "seq", [(at, (at + step) % seq_count) for at in range(seq_count)]
         )
 
+    def strategy_for(step):
+        owner = (seq_here + step) % seq_count
+        if rivers % seq_count == 0:
+            split = strategy.reshape(rounds, seq_count, local_leaves, hands)
+            rows = lax.dynamic_slice_in_dim(split, owner, 1, axis=1)
+        else:
+            picked = [
+                lax.dynamic_slice_in_dim(
+                    strategy[0], jnp.minimum(at * seq_count + owner, rivers - 1), 1, axis=0
+                )
+                for at in range(rounds)
+            ]
+            rows = jnp.concatenate(picked, axis=0)
+        return rows.reshape(rounds * local_leaves, hands)
+
+    own = strategy_for(0)
+    came = [shift(strategy_for(step), step) for step in range(1, seq_count)]
+
     small_rows = round_up(local_nodes + 4, 16)
-    pack_rows = rounds * local_leaves + small_rows
-    info_rows = round_up(2 * rounds, 8)
-    own_pack, *packs, info = pl.pallas_call(
+    info_rows = round_up(2 * rounds + 5 + local_nodes, 8)
+    small, info = pl.pallas_call(
         functools.partial(pack_kernel, rounds, seq_count),
-        out_shape=[jax.ShapeDtypeStruct((pack_rows, hands), jnp.bfloat16)] * seq_count
-        + [jax.ShapeDtypeStruct((info_rows, padded), jnp.float32)],
-        in_specs=[anywhere] * 6,
-        out_specs=[anywhere] * (seq_count + 1),
+        out_shape=[
+            jax.ShapeDtypeStruct((small_rows, hands), jnp.bfloat16),
+            jax.ShapeDtypeStruct((info_rows, padded), jnp.float32),
+        ],
+        in_specs=[anywhere] * 7,
+        out_specs=[anywhere] * 2,
         scratch_shapes=[
-            pltpu.VMEM((seq_count, rounds * local_leaves, hands), jnp.bfloat16),
             pltpu.VMEM(reach_in.shape, jnp.bfloat16),
             pltpu.VMEM((1, local_leaves), jnp.int32),
             pltpu.VMEM((1, local_leaves), jnp.float32),
             pltpu.VMEM((rivers, 1, hands), jnp.int32),
             pltpu.SMEM((board_cards.shape[2], 1, rivers), jnp.int32),
+            pltpu.SMEM((1,), jnp.int32),
+            pltpu.SMEM((1,), jnp.float32),
             pltpu.VMEM((small_rows, hands), jnp.bfloat16),
             pltpu.VMEM((info_rows, padded), jnp.float32),
-            pltpu.SemaphoreType.DMA((5 + rounds * seq_count,)),
-            pltpu.SemaphoreType.DMA((1 + (1 + rounds) * seq_count,)),
+            pltpu.SemaphoreType.DMA((7,)),
+            pltpu.SemaphoreType.DMA((2,)),
         ],
         compiler_params=pltpu.CompilerParams(vmem_limit_bytes=60 * MIB),
         name="pack",
     )(
-        strategy,
         reach_in,
         parent_node[None],
         pot_size[None],
         hand_ranks.transpose(1, 0, 2),
         board_cards.transpose(2, 0, 1),
+        river_count,
+        flop_weight,
     )
-    came = [shift(pack, step) for step, pack in enumerate(packs, 1)]
-
-    smem = pl.BlockSpec(memory_space=pltpu.SMEM)
-    payoff, own, live = pl.pallas_call(
-        functools.partial(build_kernel, rounds, seq_count),
+    smalls = [shift(small, step) for step in range(1, seq_count)]
+
+    payoff, info = pl.pallas_call(
+        functools.partial(build_kernel, rounds),
         out_shape=[
             jax.ShapeDtypeStruct((rounds, padded, padded), jnp.bfloat16),
-            jax.ShapeDtypeStruct((pack_rows, hands), jnp.bfloat16),
-            jax.ShapeDtypeStruct((round_up(rounds + 3, 8), padded), jnp.float32),
-        ],
-        in_specs=[smem, smem, vmem, vmem],
-        out_specs=[vmem] * 3,
+            jax.ShapeDtypeStruct((info_rows, padded), jnp.float32),
+        ],
+        in_specs=[vmem],
+        out_specs=[vmem] * 2,
         scratch_shapes=[
             pltpu.VMEM((round_up(DECK, 16), padded), jnp.bfloat16),
             pltpu.VMEM((padded, padded), jnp.bfloat16),
-            pltpu.SemaphoreType.DMA,
         ],
         compiler_params=pltpu.CompilerParams(vmem_limit_bytes=30 * MIB),
         cost_estimate=pl.CostEstimate(
             flops=10 * rounds * padded * padded, bytes_accessed=4 * padded * padded, transcendentals=0
         ),
         name="build",
-    )(river_count, flop_weight, info, own_pack)
+    )(info)
 
     count = tile_count(local_nodes, hands)
     *shares, weight = pl.pallas_call(
         functools.partial(value_kernel, rounds, seq_count, nodes, leaves),
         out_shape=[jax.ShapeDtypeStruct((count, 8, LANES), jnp.float32)] * seq_count
         + [jax.ShapeDtypeStruct((8, LANES), jnp.float32)],
-        in_specs=[vmem] * (3 + seq_count - 1),
+        in_specs=[vmem] * (1 + 2 * seq_count),
         out_specs=[vmem] * (seq_count + 1),
         scratch_shapes=[
             pltpu.VMEM((nodes, padded), jnp.float32),
@@ -449,19 +452,27 @@
         ],
         compiler_params=params,
         name="value",
-    )(payoff, own, live, *came)
+    )(payoff, info, own, *came, *smalls)
 
     share = shares[0]
     for step in range(1, seq_count):
         share = share + shift(shares[step], -step)
+    def swap(array, step):
+        return lax.ppermute(array, "board", [(at, at ^ step) for at in range(board_count)])
+
+    half = -(-count // 2)
+    parity = lax.axis_index("board") % 2
     root = share * weight[None]
-    step = 1
-    while True:
-        came = lax.ppermute(root, "board", [(at, at ^ step) for at in range(board_count)])
+    if count % 2:
+        root = jnp.concatenate([root, jnp.zeros((1, 8, LANES), jnp.float32)], axis=0)
+    root = root.reshape(2, half, 8, LANES)
+    mine = lax.dynamic_index_in_dim(root, parity, 0, keepdims=False)
+    mine = mine + swap(lax.dynamic_index_in_dim(root, 1 - parity, 0, keepdims=False), 1)
+    step = 2
+    while step < board_count:
+        mine = mine + swap(mine, step)
         step *= 2
-        if step >= board_count:
-            break
-        root = root + came
+    other = swap(mine, 1)
 
     turn_value = pl.pallas_call(
         functools.partial(share_kernel, local_nodes, hands),
@@ -483,7 +494,7 @@
         scratch_shapes=[pltpu.VMEM((local_nodes, hands), jnp.float32), pltpu.SemaphoreType.DMA],
         compiler_params=params,
         name="root",
-    )(root, came)
+    )(mine, other)
     return (turn_value.transpose(1, 0, 2), root_value)
 
 

time: 39.9 us -> 40.1 us (level)
  waiting for transfers between devices: 12.5 us -> 14.4 us
  starting transfers between devices: 12.7 us -> 11 us
    ppermute x2 -> x3, starting transfers between devices: 4.76 us -> 3.33 us  [shift(): lax.ppermute(array, 'seq', [(at, (at + step) % seq_count) for at in range...]
    ppermute x2 -> x3, waiting for transfers between devices: 4.51 us -> 5.72 us  [shift(): lax.ppermute(array, 'seq', [(at, (at + step) % seq_count) for at in range...]
    dynamic_slice x0 -> x1, local copies, waits for them, and re-layouts: none -> 1.19 us  [strategy_for(): rows = lax.dynamic_slice_in_dim(split, owner, 1, axis=1)]
    unnamed x4 -> x2, local copies, waits for them, and re-layouts: 1.8 us -> 0.9 us
    ppermute x4 -> x5, waiting for transfers between devices: 8.01 us -> 8.65 us  [swap(): lax.ppermute(array, 'board', [(at, at ^ step) for at in range(board_count)])]
    pallas_call x1, Pallas kernels: 1.32 us -> 1.82 us  [body(): pl.pallas_call(functools.partial(value_kernel, rounds, seq_count, nodes,...]
    pallas_call x1, Pallas kernels: 2.2 us -> 1.72 us  [body(): pl.pallas_call(functools.partial(pack_kernel, rounds, seq_count), out_sha...]
    ppermute x4 -> x5, starting transfers between devices: 7.97 us -> 7.7 us  [swap(): lax.ppermute(array, 'board', [(at, at ^ step) for at in range(board_count)])]
  transfers between devices with their start and end apart: 6 -> 8, of which waited for: 6 -> 7; matrix products, arithmetic and copies ran while one was open for 0% -> 0% of each run, Pallas kernels for 16% -> 19%
where the time goes in v1:
time: 40.1 us; the launch traced here: 39.7 us
  waiting for transfers between devices  14.4 us (36%)
  starting transfers between devices  11 us (27%)
  Pallas kernels  10.1 us (25%)
  local copies, waits for them, and re-layouts  2.1 us (5%)
  between operations  2.03 us (5%)
    ppermute x5, waiting for transfers between devices, swap(): lax.ppermute(array, 'board', [(at, at ^ step) for at in range(board_count)])  8.65 us
    ppermute x5, starting transfers between devices, swap(): lax.ppermute(array, 'board', [(at, at ^ step) for at in range(board_count)])  7.7 us
    ppermute x3, waiting for transfers between devices, shift(): lax.ppermute(array, 'seq', [(at, (at + step) % seq_count) for at in range...  5.72 us
    pallas_call x1, Pallas kernels, body(): pl.pallas_call(functools.partial(build_kernel, rounds), out_shape=[jax.Sh...  5.16 us
    ppermute x3, starting transfers between devices, shift(): lax.ppermute(array, 'seq', [(at, (at + step) % seq_count) for at in range...  3.33 us
    pallas_call x1, Pallas kernels, body(): pl.pallas_call(functools.partial(value_kernel, rounds, seq_count, nodes,...  1.82 us
    pallas_call x1, Pallas kernels, body(): pl.pallas_call(functools.partial(pack_kernel, rounds, seq_count), out_sha...  1.72 us
    dynamic_slice x1, local copies, waits for them, and re-layouts, strategy_for(): rows = lax.dynamic_slice_in_dim(split, owner, 1, axis=1)  1.19 us
  transfers between devices with their start and end apart: 8, of which 7 were waited for; matrix products, arithmetic and copies ran while one was open for 0% of the time, Pallas kernels for 19%

profile of v1, /device:TPU:0, one launch (start us, length us, event | category | flops | bytes accessed | tf_op | source)
XLA Modules:
  0.0 39.7 jit_solution(14517200192929786287)
XLA Ops:
  0.7 1.2 %constant_dynamic-slice_fusion = (bf16[3,1,48,1326]{3,2,1,0:T(8,128)(2,1)S(1)}, bf16[3,1,48,1326]{3,2,1,0:T(8,128)(2,1)S(1)}) fusion(bf16[3,2,48,1326]{3,2,1,0:T(8,128)(2,1)} %bitcast.18, s32[]{:T(128)S(6)} %select_n.31, s32[]{:T(128)S(6)} %select_n.29), kind=kLoop, calls=%fused_computation.3 | loop fusion | bytes 1527560 | tf_op jit(solution)/shard_map/dynamic_slice | solution.py:373
  1.9 3.0 %collective-permute-start = (bf16[144,1326]{1,0:T(8,128)(2,1)S(1)}, bf16[144,1326]{1,0:T(8,128)(2,1)S(1)}, u32[]{:S(2)}, u32[]{:S(2)}) collective-permute-start(bf16[144,1326]{1,0:T(8,128)(2,1)S(1)} %bitcast.19), channel_id=1, source_target_pairs={{0,1},{1,0},{2,3},{3,2},{4,5},{5,4},{6,7},{7,6},{8,9},{9,8},{10,11... | collective-permute-start | bytes 1145672 | tf_op jit(solution)/shard_map/ppermute | solution.py:365
  6.2 1.7 %pack.1 = (bf16[16,1326]{1,0:T(8,128)(2,1)}, f32[24,1408]{1,0:T(8,128)}) custom-call(bf16[1,12,1326]{2,1,0:T(8,128)(2,1)} %reach_ref.1, s32[1,48]{1,0:T(1,128)} %bitcast.25, f32[1,48]{1,0:T(1,128)} %bitcast.26, s32[6,1,1326]{2,1,0:T(1,128)} %bitcast.23, s32[5,1,6]{2,1,0:T(1,128)} %bitcast.24, s32[1]{0:T(128)S(6)} %copy.14.count_ref, f32[1]{0:T(128)S(6)} %copy.15.weight_ref), custom_call_target="tpu_custom_call" | custom-call | tf_op jit(solution)/shard_map/pack/pallas_call | solution.py:389
  7.9 0.1 collective-permute-start.1
  8.0 0.0 copy-start
  8.0 0.9 %copy-done = f32[24,1408]{1,0:T(8,128)S(1)} copy-done((f32[24,1408]{1,0:T(8,128)S(1)}, f32[24,1408]{1,0:T(8,128)}, u32[]{:S(2)}) %copy-start) | copy-done | bytes 135192
  8.9 5.2 %build.1 = (bf16[3,1408,1408]{2,1,0:T(8,128)(2,1)S(1)}, f32[24,1408]{1,0:T(8,128)S(1)}) custom-call(f32[24,1408]{1,0:T(8,128)S(1)} %copy-done), custom_call_target="tpu_custom_call" | custom-call | flops 59473920 | bytes 7929856 | tf_op jit(solution)/shard_map/build/pallas_call | solution.py:423
  14.0 1.2 %collective-permute-done.1.refs_4_ = bf16[16,1326]{1,0:T(8,128)(2,1)S(1)} collective-permute-done((bf16[16,1326]{1,0:T(8,128)(2,1)}, bf16[16,1326]{1,0:T(8,128)(2,1)S(1)}, u32[]{:S(2)}, u32[]{:S(2)}) %collective-permute-start.1) | collective-permute-done | bytes 42464 | tf_op jit(solution)/shard_map/ppermute | solution.py:365
  15.2 0.0 collective-permute-done.refs_3_
  15.2 1.8 %value.1 = (f32[16,8,128]{2,1,0:T(8,128)S(1)}, f32[16,8,128]{2,1,0:T(8,128)S(1)}, f32[8,128]{1,0:T(8,128)S(1)}) custom-call(bf16[3,1408,1408]{2,1,0:T(8,128)(2,1)S(1)} %get-tuple-element.10.refs_0_, f32[24,1408]{1,0:T(8,128)S(1)} %get-tuple-element.11.refs_1_, bf16[144,1326]{1,0:T(8,128)(2,1)S(1)} %bitcast.17, ...), custom_call_target="tpu_custom_call" | custom-call | tf_op jit(solution)/shard_map/value/pallas_call | solution.py:443
  17.0 0.3 collective-permute-start.2
  17.3 4.6 %collective-permute-done.2 = f32[16,8,128]{2,1,0:T(8,128)S(1)} collective-permute-done((f32[16,8,128]{2,1,0:T(8,128)S(1)}, f32[16,8,128]{2,1,0:T(8,128)S(1)}, u32[]{:S(2)}, u32[]{:S(2)}) %collective-permute-start.2) | collective-permute-done | bytes 65568 | tf_op jit(solution)/shard_map/ppermute | solution.py:365
  21.9 0.1 collective-permute-start.3
  22.0 1.2 %collective-permute-done.3 = f32[8,8,128]{2,1,0:T(8,128)S(1)} collective-permute-done((f32[8,8,128]{2,1,0:T(8,128)S(1)}, f32[8,8,128]{2,1,0:T(8,128)S(1)}, u32[]{:S(2)}, u32[]{:S(2)}) %collective-permute-start.3) | collective-permute-done | bytes 32800 | tf_op jit(solution)/shard_map/ppermute | solution.py:461
  23.1 1.2 %collective-permute-start.4 = (f32[8,8,128]{2,1,0:T(8,128)S(1)}, f32[8,8,128]{2,1,0:T(8,128)S(1)}, u32[]{:S(2)}, u32[]{:S(2)}) collective-permute-start(f32[8,8,128]{2,1,0:T(8,128)S(1)} %bitcast_add_fusion), channel_id=1, source_target_pairs={{0,4},{2,6},{4,0},{6,2},{8,12},{10,14},{12,8},{14,10},{16,20},{18,... | collective-permute-start | bytes 98312 | tf_op jit(solution)/shard_map/ppermute | solution.py:461
  24.4 2.7 %collective-permute-done.4 = f32[8,8,128]{2,1,0:T(8,128)S(1)} collective-permute-done((f32[8,8,128]{2,1,0:T(8,128)S(1)}, f32[8,8,128]{2,1,0:T(8,128)S(1)}, u32[]{:S(2)}, u32[]{:S(2)}) %collective-permute-start.4) | collective-permute-done | bytes 32800 | tf_op jit(solution)/shard_map/ppermute | solution.py:461
  27.1 1.5 %collective-permute-start.5 = (f32[8,8,128]{2,1,0:T(8,128)S(1)}, f32[8,8,128]{2,1,0:T(8,128)S(1)}, u32[]{:S(2)}, u32[]{:S(2)}) collective-permute-start(f32[8,8,128]{2,1,0:T(8,128)S(1)} %add.52), channel_id=1, source_target_pairs={{0,8},{2,10},{4,12},{6,14},{8,0},{10,2},{12,4},{14,6},{16,24},{18,... | collective-permute-start | bytes 98312 | tf_op jit(solution)/shard_map/ppermute | solution.py:461
  28.6 2.4 %collective-permute-done.5 = f32[8,8,128]{2,1,0:T(8,128)S(1)} collective-permute-done((f32[8,8,128]{2,1,0:T(8,128)S(1)}, f32[8,8,128]{2,1,0:T(8,128)S(1)}, u32[]{:S(2)}, u32[]{:S(2)}) %collective-permute-start.5) | collective-permute-done | bytes 32800 | tf_op jit(solution)/shard_map/ppermute | solution.py:461
  31.0 4.9 %collective-permute-start.6 = (f32[8,8,128]{2,1,0:T(8,128)S(1)}, f32[8,8,128]{2,1,0:T(8,128)S(1)}, u32[]{:S(2)}, u32[]{:S(2)}) collective-permute-start(f32[8,8,128]{2,1,0:T(8,128)S(1)} %add.53), channel_id=1, source_target_pairs={{0,16},{2,18},{4,20},{6,22},{8,24},{10,26},{12,28},{14,30},{16,0},... | collective-permute-start | bytes 98312 | tf_op jit(solution)/shard_map/ppermute | solution.py:461
  35.9 1.9 %collective-permute-done.6 = f32[8,8,128]{2,1,0:T(8,128)S(1)} collective-permute-done((f32[8,8,128]{2,1,0:T(8,128)S(1)}, f32[8,8,128]{2,1,0:T(8,128)S(1)}, u32[]{:S(2)}, u32[]{:S(2)}) %collective-permute-start.6) | collective-permute-done | bytes 32800 | tf_op jit(solution)/shard_map/ppermute | solution.py:461
  37.8 0.0 collective-permute-start.7
  37.8 0.7 %share.1 = f32[12,1,1326]{2,1,0:T(1,128)} custom-call(f32[16,8,128]{2,1,0:T(8,128)S(1)} %get-tuple-element.17.tiles_ref), custom_call_target="tpu_custom_call" | custom-call | tf_op jit(solution)/shard_map/share/pallas_call | solution.py:477
  38.5 0.5 %collective-permute-done.7.other_ref = f32[8,8,128]{2,1,0:T(8,128)S(1)} collective-permute-done((f32[8,8,128]{2,1,0:T(8,128)S(1)}, f32[8,8,128]{2,1,0:T(8,128)S(1)}, u32[]{:S(2)}, u32[]{:S(2)}) %collective-permute-start.7) | collective-permute-done | bytes 32800 | tf_op jit(solution)/shard_map/ppermute | solution.py:461
  39.0 0.7 %root.1 = f32[12,1326]{1,0:T(8,128)} custom-call(f32[8,8,128]{2,1,0:T(8,128)S(1)} %add.54.mine_ref, f32[8,8,128]{2,1,0:T(8,128)S(1)} %collective-permute-done.7.other_ref), custom_call_target="tpu_custom_call" | custom-call | tf_op jit(solution)/shard_map/root/pallas_call | solution.py:489
  (6 shorter events, 0.0 us)
Async XLA Ops:
  1.9 13.4 %collective-permute-start = (bf16[144,1326]{1,0:T(8,128)(2,1)S(1)}, bf16[144,1326]{1,0:T(8,128)(2,1)S(1)}, u32[]{:S(2)}, u32[]{:S(2)}) collective-permute-start(bf16[144,1326]{1,0:T(8,128)(2,1)S(1)} %bitcast.19), channel_id=1, source_target_pairs={{0,1},{1,0},{2,3},{3,2},{4,5},{5,4},{6,7},{7,6},{8,9},{9,8},{10,11... | collective-permute-start | bytes 1145672 | tf_op jit(solution)/shard_map/ppermute | solution.py:365
  7.9 7.3 %collective-permute-start.1 = (bf16[16,1326]{1,0:T(8,128)(2,1)}, bf16[16,1326]{1,0:T(8,128)(2,1)S(1)}, u32[]{:S(2)}, u32[]{:S(2)}) collective-permute-start(bf16[16,1326]{1,0:T(8,128)(2,1)} %get-tuple-element.12), channel_id=1, source_target_pairs={{0,1},{1,0},{2,3},{3,2},{4,5},{5,4},{6,7},{7,6},{8,9},{9,8},{10,11... | collective-permute-start | bytes 127304 | tf_op jit(solution)/shard_map/ppermute | solution.py:365
  8.0 0.9 %copy-start = (f32[24,1408]{1,0:T(8,128)S(1)}, f32[24,1408]{1,0:T(8,128)}, u32[]{:S(2)}) copy-start(f32[24,1408]{1,0:T(8,128)} %get-tuple-element.9.info_ref) | copy-start | bytes 405508
  17.0 4.8 %collective-permute-start.2 = (f32[16,8,128]{2,1,0:T(8,128)S(1)}, f32[16,8,128]{2,1,0:T(8,128)S(1)}, u32[]{:S(2)}, u32[]{:S(2)}) collective-permute-start(f32[16,8,128]{2,1,0:T(8,128)S(1)} %get-tuple-element.14), channel_id=1, source_target_pairs={{0,1},{1,0},{2,3},{3,2},{4,5},{5,4},{6,7},{7,6},{8,9},{9,8},{10,11... | collective-permute-start | bytes 196616 | tf_op jit(solution)/shard_map/ppermute | solution.py:365
  21.9 1.3 %collective-permute-start.3 = (f32[8,8,128]{2,1,0:T(8,128)S(1)}, f32[8,8,128]{2,1,0:T(8,128)S(1)}, u32[]{:S(2)}, u32[]{:S(2)}) collective-permute-start(f32[8,8,128]{2,1,0:T(8,128)S(1)} %dynamic-slice_bitcast_fusion), channel_id=1, source_target_pairs={{0,2},{2,0},{4,6},{6,4},{8,10},{10,8},{12,14},{14,12},{16,18},{18,... | collective-permute-start | bytes 98312 | tf_op jit(solution)/shard_map/ppermute | solution.py:461
  23.1 3.9 %collective-permute-start.4 = (f32[8,8,128]{2,1,0:T(8,128)S(1)}, f32[8,8,128]{2,1,0:T(8,128)S(1)}, u32[]{:S(2)}, u32[]{:S(2)}) collective-permute-start(f32[8,8,128]{2,1,0:T(8,128)S(1)} %bitcast_add_fusion), channel_id=1, source_target_pairs={{0,4},{2,6},{4,0},{6,2},{8,12},{10,14},{12,8},{14,10},{16,20},{18,... | collective-permute-start | bytes 98312 | tf_op jit(solution)/shard_map/ppermute | solution.py:461
  27.1 3.9 %collective-permute-start.5 = (f32[8,8,128]{2,1,0:T(8,128)S(1)}, f32[8,8,128]{2,1,0:T(8,128)S(1)}, u32[]{:S(2)}, u32[]{:S(2)}) collective-permute-start(f32[8,8,128]{2,1,0:T(8,128)S(1)} %add.52), channel_id=1, source_target_pairs={{0,8},{2,10},{4,12},{6,14},{8,0},{10,2},{12,4},{14,6},{16,24},{18,... | collective-permute-start | bytes 98312 | tf_op jit(solution)/shard_map/ppermute | solution.py:461
  31.0 6.8 %collective-permute-start.6 = (f32[8,8,128]{2,1,0:T(8,128)S(1)}, f32[8,8,128]{2,1,0:T(8,128)S(1)}, u32[]{:S(2)}, u32[]{:S(2)}) collective-permute-start(f32[8,8,128]{2,1,0:T(8,128)S(1)} %add.53), channel_id=1, source_target_pairs={{0,16},{2,18},{4,20},{6,22},{8,24},{10,26},{12,28},{14,30},{16,0},... | collective-permute-start | bytes 98312 | tf_op jit(solution)/shard_map/ppermute | solution.py:461
  37.8 1.2 %collective-permute-start.7 = (f32[8,8,128]{2,1,0:T(8,128)S(1)}, f32[8,8,128]{2,1,0:T(8,128)S(1)}, u32[]{:S(2)}, u32[]{:S(2)}) collective-permute-start(f32[8,8,128]{2,1,0:T(8,128)S(1)} %add.54.mine_ref), channel_id=1, source_target_pairs={{0,2},{2,0},{4,6},{6,4},{8,10},{10,8},{12,14},{14,12},{16,18},{18,... | collective-permute-start | bytes 98312 | tf_op jit(solution)/shard_map/ppermute | solution.py:461

commit v2 on v1

--- a/solution.py
+++ b/solution.py
@@ -126,7 +126,6 @@
     rank_ref,
     board_ref,
     count_ref,
-    weight_ref,
     small_ref,
     info_ref,
     reach_tmp,
@@ -135,7 +134,6 @@
     rank_tmp,
     board_tmp,
     count_tmp,
-    weight_tmp,
     small,
     info,
     sems,
@@ -153,7 +151,6 @@
             (rank_ref, rank_tmp),
             (board_ref, board_tmp),
             (count_ref, count_tmp),
-            (weight_ref, weight_tmp),
         ],
         sems,
     )
@@ -190,48 +187,49 @@
     info[base : base + 1, :] = 1.0 / (hands * jnp.full((1, padded), live_count.astype(jnp.float32)))
     live_rounds = lax.div(live_count - here + seq_count - 1, seq_count)
     info[base + 1 : base + 2, :] = jnp.full((1, padded), live_rounds.astype(jnp.float32))
-    info[base + 2 : base + 3, :] = jnp.full((1, padded), weight_tmp[0] / lax.axis_size("board"))
-    info[base + 3 : base + 4, :leaves] = parent
-    info[base + 4 : base + 5, :leaves] = pot
-    info[base + 5 : base + 5 + nodes, :hands] = reach
+    info[base + 2 : base + 3, :leaves] = parent
+    info[base + 3 : base + 4, :leaves] = pot
+    info[base + 4 : base + 4 + nodes, :hands] = reach
     kept = pltpu.make_async_copy(info, info_ref, out_sems.at[1])
     kept.start()
     sent.wait()
     kept.wait()
 
 
-def build_kernel(rounds, info_ref, payoff_ref, kept_ref, holds, apart):
+def build_kernel(rounds, info_ref, payoff_ref, kept_ref, ranks, gaps, holds, lacks):
     padded = payoff_ref.shape[-1]
     kept_ref[...] = info_ref[...]
 
     low, high = hand_cards(padded)
     card = lax.broadcasted_iota(jnp.int32, (holds.shape[0], padded), 0)
-    holds[...] = jnp.where((card == low) | (card == high), 1.0, 0.0).astype(jnp.bfloat16)
-
-    def mask_rows(start):
-        shared = lax.dot_general(
-            holds[:, start : start + LANES],
-            holds[...],
-            (((0,), (0,)), ((), ())),
-            preferred_element_type=jnp.float32,
-        )
-        apart[start : start + LANES, :] = jnp.maximum(1.0 - shared, 0.0).astype(jnp.bfloat16)
-
-    mask_rows(0)
+    held = jnp.where((card == low) | (card == high), 1.0, 0.0)
+    holds[...] = jnp.where(card == DECK, 1.0, held).astype(jnp.bfloat16)
+    lacks[...] = jnp.where(card == DECK, 1.0, -held).astype(jnp.bfloat16)
+    row = lax.broadcasted_iota(jnp.int32, (ranks.shape[1], padded), 0)
+    for at in range(rounds):
+        rank = info_ref[at : at + 1, :]
+        top = jnp.floor(rank * (1.0 / LANES)) * LANES
+        rest = rank - top
+        sides = jnp.where(row % 2 == 0, top, rest)
+        ones = jnp.where(row < 4, 1.0, 0.0)
+        ranks[at] = jnp.where(row < 2, -sides, ones).astype(jnp.bfloat16)
+        gaps[at] = jnp.where(row < 2, ones, jnp.where(row < 4, sides, 0.0)).astype(jnp.bfloat16)
+
+    def product(left, right):
+        return lax.dot_general(
+            left, right, (((0,), (0,)), ((), ())), preferred_element_type=jnp.float32
+        ).astype(jnp.bfloat16)
+
     for start in range(0, padded, LANES):
-        if start + LANES < padded:
-            mask_rows(start + LANES)
         rows = slice(start, start + LANES)
-        columns = [
-            jnp.broadcast_to(info_ref[at : at + 1, rows], (LANES, LANES)).T
-            for at in range(rounds)
-        ]
-        for lane in range(0, padded, LANES):
-            here_lanes = slice(lane, lane + LANES)
-            mask = apart[rows, here_lanes]
+        for lane in range(0, padded, 2 * LANES):
+            here = slice(lane, min(lane + 2 * LANES, padded))
+            mask = product(holds[:, rows], lacks[:, here])
+            if here.start <= start < here.stop:
+                mask = jnp.maximum(mask, 0.0)
             for at in range(rounds):
-                gap = (columns[at] - info_ref[at : at + 1, here_lanes]).astype(jnp.bfloat16)
-                payoff_ref[at, rows, here_lanes] = jnp.maximum(jnp.minimum(gap, mask), -mask)
+                gap = product(ranks[at, :, rows], gaps[at, :, here])
+                payoff_ref[at, rows, here] = jnp.maximum(jnp.minimum(gap, mask), -mask)
 
 
 def value_kernel(rounds, seq_count, nodes, leaves, *refs):
@@ -248,9 +246,9 @@
     reach, places, pots = [], [], []
     for at in range(seq_count):
         if at == 0:
-            reach.append(info_ref[base + 5 : base + 5 + local_nodes, :hands])
-            parent = info_ref[base + 3 : base + 4, :LANES]
-            pots.append(info_ref[base + 4 : base + 5, :LANES])
+            reach.append(info_ref[base + 4 : base + 4 + local_nodes, :hands])
+            parent = info_ref[base + 2 : base + 3, :LANES]
+            pots.append(info_ref[base + 3 : base + 4, :LANES])
         else:
             small = smalls[at - 1][...].astype(jnp.float32)
             reach.append(small[:local_nodes])
@@ -298,20 +296,14 @@
             for pick, pack in zip(picks[1:], came):
                 strat = strat + jnp.dot(pick, pack[rows, :], preferred_element_type=jnp.float32)
             reach_all[:, :hands] = (lookup * strat * live[:, :hands]).astype(jnp.bfloat16)
-            shown = lax.dot_general(
-                payoff_ref[at],
-                reach_all[...],
-                (((1,), (1,)), ((), ())),
-                preferred_element_type=jnp.float32,
-            )
-            value = shown.T * pot_sorted
+            shown = jnp.dot(reach_all[...], payoff_ref[at], preferred_element_type=jnp.float32)
+            value = shown * pot_sorted
             best = value[:nodes]
             for row in range(nodes, leaves, nodes):
                 best = jnp.maximum(best, value[row : row + nodes])
             gain = best * (live * info_ref[base : base + 1, :])
             total[...] += gain
 
-    outs[-1][...] = jnp.broadcast_to(info_ref[base + 2 : base + 3, :LANES], (8, LANES))
     short = round_up(local_nodes, 8) - local_nodes
     for step in range(seq_count):
         rows = total[step * local_nodes : (step + 1) * local_nodes, :]
@@ -385,14 +377,14 @@
     came = [shift(strategy_for(step), step) for step in range(1, seq_count)]
 
     small_rows = round_up(local_nodes + 4, 16)
-    info_rows = round_up(2 * rounds + 5 + local_nodes, 8)
+    info_rows = round_up(2 * rounds + 4 + local_nodes, 8)
     small, info = pl.pallas_call(
         functools.partial(pack_kernel, rounds, seq_count),
         out_shape=[
             jax.ShapeDtypeStruct((small_rows, hands), jnp.bfloat16),
             jax.ShapeDtypeStruct((info_rows, padded), jnp.float32),
         ],
-        in_specs=[anywhere] * 7,
+        in_specs=[anywhere] * 6,
         out_specs=[anywhere] * 2,
         scratch_shapes=[
             pltpu.VMEM(reach_in.shape, jnp.bfloat16),
@@ -401,10 +393,9 @@
             pltpu.VMEM((rivers, 1, hands), jnp.int32),
             pltpu.SMEM((board_cards.shape[2], 1, rivers), jnp.int32),
             pltpu.SMEM((1,), jnp.int32),
-            pltpu.SMEM((1,), jnp.float32),
             pltpu.VMEM((small_rows, hands), jnp.bfloat16),
             pltpu.VMEM((info_rows, padded), jnp.float32),
-            pltpu.SemaphoreType.DMA((7,)),
+            pltpu.SemaphoreType.DMA((6,)),
             pltpu.SemaphoreType.DMA((2,)),
         ],
         compiler_params=pltpu.CompilerParams(vmem_limit_bytes=60 * MIB),
@@ -416,7 +407,6 @@
         hand_ranks.transpose(1, 0, 2),
         board_cards.transpose(2, 0, 1),
         river_count,
-        flop_weight,
     )
     smalls = [shift(small, step) for step in range(1, seq_count)]
 
@@ -429,8 +419,10 @@
         in_specs=[vmem],
         out_specs=[vmem] * 2,
         scratch_shapes=[
-            pltpu.VMEM((round_up(DECK, 16), padded), jnp.bfloat16),
-            pltpu.VMEM((padded, padded), jnp.bfloat16),
+            pltpu.VMEM((rounds, 16, padded), jnp.bfloat16),
+            pltpu.VMEM((rounds, 16, padded), jnp.bfloat16),
+            pltpu.VMEM((round_up(DECK + 1, 16), padded), jnp.bfloat16),
+            pltpu.VMEM((round_up(DECK + 1, 16), padded), jnp.bfloat16),
         ],
         compiler_params=pltpu.CompilerParams(vmem_limit_bytes=30 * MIB),
         cost_estimate=pl.CostEstimate(
@@ -440,12 +432,11 @@
     )(info)
 
     count = tile_count(local_nodes, hands)
-    *shares, weight = pl.pallas_call(
+    shares = pl.pallas_call(
         functools.partial(value_kernel, rounds, seq_count, nodes, leaves),
-        out_shape=[jax.ShapeDtypeStruct((count, 8, LANES), jnp.float32)] * seq_count
-        + [jax.ShapeDtypeStruct((8, LANES), jnp.float32)],
+        out_shape=[jax.ShapeDtypeStruct((count, 8, LANES), jnp.float32)] * seq_count,
         in_specs=[vmem] * (1 + 2 * seq_count),
-        out_specs=[vmem] * (seq_count + 1),
+        out_specs=[vmem] * seq_count,
         scratch_shapes=[
             pltpu.VMEM((nodes, padded), jnp.float32),
             pltpu.VMEM((leaves, padded), jnp.bfloat16),
@@ -462,7 +453,7 @@
 
     half = -(-count // 2)
     parity = lax.axis_index("board") % 2
-    root = share * weight[None]
+    root = share * (flop_weight[0] / board_count)
     if count % 2:
         root = jnp.concatenate([root, jnp.zeros((1, 8, LANES), jnp.float32)], axis=0)
     root = root.reshape(2, half, 8, LANES)

time: 40.1 us -> 38.8 us (0.968)
  Pallas kernels: 10.1 us -> 8.83 us
  starting transfers between devices: 11 us -> 10.4 us
  waiting for transfers between devices: 14.4 us -> 15 us
    ppermute x5, starting transfers between devices: 7.7 us -> 6.56 us  [swap(): lax.ppermute(array, 'board', [(at, at ^ step) for at in range(board_count)])]
    ppermute x5, waiting for transfers between devices: 8.65 us -> 9.57 us  [swap(): lax.ppermute(array, 'board', [(at, at ^ step) for at in range(board_count)])]
    pallas_call x1, Pallas kernels: 5.16 us -> 4.38 us  [body(): pl.pallas_call(functools.partial(build_kernel, rounds), out_shape=[jax.Sh...]
    pallas_call x1, Pallas kernels: 1.82 us -> 1.3 us  [body(): pl.pallas_call(functools.partial(value_kernel, rounds, seq_count, nodes,...]
    ppermute x3, starting transfers between devices: 3.33 us -> 3.84 us  [shift(): lax.ppermute(array, 'seq', [(at, (at + step) % seq_count) for at in range...]
  transfers between devices with their start and end apart: 8 -> 8, of which waited for: 7 -> 7; matrix products, arithmetic and copies ran while one was open for 0% -> 0% of each run, Pallas kernels for 19% -> 18%
where the time goes in v2:
time: 38.8 us; the launch traced here: 38.5 us
  waiting for transfers between devices  15 us (39%)
  starting transfers between devices  10.4 us (27%)
  Pallas kernels  8.83 us (23%)
  local copies, waits for them, and re-layouts  2.1 us (5%)
  between operations  2.05 us (5%)
    ppermute x5, waiting for transfers between devices, swap(): lax.ppermute(array, 'board', [(at, at ^ step) for at in range(board_count)])  9.57 us
    ppermute x5, starting transfers between devices, swap(): lax.ppermute(array, 'board', [(at, at ^ step) for at in range(board_count)])  6.56 us
    ppermute x3, waiting for transfers between devices, shift(): lax.ppermute(array, 'seq', [(at, (at + step) % seq_count) for at in range...  5.46 us
    pallas_call x1, Pallas kernels, body(): pl.pallas_call(functools.partial(build_kernel, rounds), out_shape=[jax.Sh...  4.38 us
    ppermute x3, starting transfers between devices, shift(): lax.ppermute(array, 'seq', [(at, (at + step) % seq_count) for at in range...  3.84 us
    pallas_call x1, Pallas kernels, body(): pl.pallas_call(functools.partial(pack_kernel, rounds, seq_count), out_sha...  1.71 us
    pallas_call x1, Pallas kernels, body(): pl.pallas_call(functools.partial(value_kernel, rounds, seq_count, nodes,...  1.3 us
    dynamic_slice x1, local copies, waits for them, and re-layouts, strategy_for(): rows = lax.dynamic_slice_in_dim(split, owner, 1, axis=1)  1.19 us
  transfers between devices with their start and end apart: 8, of which 7 were waited for; matrix products, arithmetic and copies ran while one was open for 0% of the time, Pallas kernels for 18%

profile of v2, /device:TPU:0, one launch (start us, length us, event | category | flops | bytes accessed | tf_op | source)
XLA Modules:
  0.0 38.5 jit_solution(13361223048350979424)
XLA Ops:
  0.7 1.2 %constant_dynamic-slice_fusion = (bf16[3,1,48,1326]{3,2,1,0:T(8,128)(2,1)S(1)}, bf16[3,1,48,1326]{3,2,1,0:T(8,128)(2,1)S(1)}) fusion(bf16[3,2,48,1326]{3,2,1,0:T(8,128)(2,1)} %bitcast.19, s32[]{:T(128)S(6)} %select_n.31, s32[]{:T(128)S(6)} %select_n.29), kind=kLoop, calls=%fused_computation.3 | loop fusion | bytes 1527560 | tf_op jit(solution)/shard_map/dynamic_slice | solution.py:365
  1.9 3.0 %collective-permute-start = (bf16[144,1326]{1,0:T(8,128)(2,1)S(1)}, bf16[144,1326]{1,0:T(8,128)(2,1)S(1)}, u32[]{:S(2)}, u32[]{:S(2)}) collective-permute-start(bf16[144,1326]{1,0:T(8,128)(2,1)S(1)} %bitcast.20), channel_id=1, source_target_pairs={{0,1},{1,0},{2,3},{3,2},{4,5},{5,4},{6,7},{7,6},{8,9},{9,8},{10,11... | collective-permute-start | bytes 1145672 | tf_op jit(solution)/shard_map/ppermute | solution.py:357
  5.5 1.7 %pack.1 = (bf16[16,1326]{1,0:T(8,128)(2,1)}, f32[24,1408]{1,0:T(8,128)}) custom-call(bf16[1,12,1326]{2,1,0:T(8,128)(2,1)} %reach_ref.1, s32[1,48]{1,0:T(1,128)} %bitcast.26, f32[1,48]{1,0:T(1,128)} %bitcast.27, s32[6,1,1326]{2,1,0:T(1,128)} %bitcast.24, s32[5,1,6]{2,1,0:T(1,128)} %bitcast.25, s32[1]{0:T(128)S(6)} %copy.14.count_ref), custom_call_target="tpu_custom_call" | custom-call | tf_op jit(solution)/shard_map/pack/pallas_call | solution.py:381
  7.2 0.1 collective-permute-start.1
  7.3 0.0 copy-start
  7.3 0.9 %copy-done = f32[24,1408]{1,0:T(8,128)S(1)} copy-done((f32[24,1408]{1,0:T(8,128)S(1)}, f32[24,1408]{1,0:T(8,128)}, u32[]{:S(2)}) %copy-start) | copy-done | bytes 135192
  8.2 4.4 %build.1 = (bf16[3,1408,1408]{2,1,0:T(8,128)(2,1)S(1)}, f32[24,1408]{1,0:T(8,128)S(1)}) custom-call(f32[24,1408]{1,0:T(8,128)S(1)} %copy-done), custom_call_target="tpu_custom_call" | custom-call | flops 59473920 | bytes 7929856 | tf_op jit(solution)/shard_map/build/pallas_call | solution.py:413
  12.6 2.6 %collective-permute-done.1.refs_4_ = bf16[16,1326]{1,0:T(8,128)(2,1)S(1)} collective-permute-done((bf16[16,1326]{1,0:T(8,128)(2,1)}, bf16[16,1326]{1,0:T(8,128)(2,1)S(1)}, u32[]{:S(2)}, u32[]{:S(2)}) %collective-permute-start.1) | collective-permute-done | bytes 42464 | tf_op jit(solution)/shard_map/ppermute | solution.py:357
  15.2 0.0 collective-permute-done.refs_3_
  15.2 1.3 %value.1 = (f32[16,8,128]{2,1,0:T(8,128)S(1)}, f32[16,8,128]{2,1,0:T(8,128)S(1)}) custom-call(bf16[3,1408,1408]{2,1,0:T(8,128)(2,1)S(1)} %get-tuple-element.9.refs_0_, f32[24,1408]{1,0:T(8,128)S(1)} %get-tuple-element.10.refs_1_, bf16[144,1326]{1,0:T(8,128)(2,1)S(1)} %bitcast.18, bf16[144,1326]{1,0:T(8,128)(2,1)S(1)} %collective-permute-done.refs_3_, ...), custom_call_target="tpu_custom_call" | custom-call | tf_op jit(solution)/shard_map/value/pallas_call | solution.py:435
  16.5 0.8 %collective-permute-start.2 = (f32[16,8,128]{2,1,0:T(8,128)S(1)}, f32[16,8,128]{2,1,0:T(8,128)S(1)}, u32[]{:S(2)}, u32[]{:S(2)}) collective-permute-start(f32[16,8,128]{2,1,0:T(8,128)S(1)} %get-tuple-element.13), channel_id=1, source_target_pairs={{0,1},{1,0},{2,3},{3,2},{4,5},{5,4},{6,7},{7,6},{8,9},{9,8},{10,11... | collective-permute-start | bytes 196616 | tf_op jit(solution)/shard_map/ppermute | solution.py:357
  17.9 2.9 %collective-permute-done.2 = f32[16,8,128]{2,1,0:T(8,128)S(1)} collective-permute-done((f32[16,8,128]{2,1,0:T(8,128)S(1)}, f32[16,8,128]{2,1,0:T(8,128)S(1)}, u32[]{:S(2)}, u32[]{:S(2)}) %collective-permute-start.2) | collective-permute-done | bytes 65568 | tf_op jit(solution)/shard_map/ppermute | solution.py:357
  20.8 0.1 collective-permute-start.3
  20.9 1.2 %collective-permute-done.3 = f32[8,8,128]{2,1,0:T(8,128)S(1)} collective-permute-done((f32[8,8,128]{2,1,0:T(8,128)S(1)}, f32[8,8,128]{2,1,0:T(8,128)S(1)}, u32[]{:S(2)}, u32[]{:S(2)}) %collective-permute-start.3) | collective-permute-done | bytes 32800 | tf_op jit(solution)/shard_map/ppermute | solution.py:452
  22.1 3.8 %collective-permute-start.4 = (f32[8,8,128]{2,1,0:T(8,128)S(1)}, f32[8,8,128]{2,1,0:T(8,128)S(1)}, u32[]{:S(2)}, u32[]{:S(2)}) collective-permute-start(f32[8,8,128]{2,1,0:T(8,128)S(1)} %bitcast_add_fusion), channel_id=1, source_target_pairs={{0,4},{2,6},{4,0},{6,2},{8,12},{10,14},{12,8},{14,10},{16,20},{18,... | collective-permute-start | bytes 98312 | tf_op jit(solution)/shard_map/ppermute | solution.py:452
  25.9 1.9 %collective-permute-done.4 = f32[8,8,128]{2,1,0:T(8,128)S(1)} collective-permute-done((f32[8,8,128]{2,1,0:T(8,128)S(1)}, f32[8,8,128]{2,1,0:T(8,128)S(1)}, u32[]{:S(2)}, u32[]{:S(2)}) %collective-permute-start.4) | collective-permute-done | bytes 32800 | tf_op jit(solution)/shard_map/ppermute | solution.py:452
  27.8 0.1 collective-permute-start.5
  27.9 3.8 %collective-permute-done.5 = f32[8,8,128]{2,1,0:T(8,128)S(1)} collective-permute-done((f32[8,8,128]{2,1,0:T(8,128)S(1)}, f32[8,8,128]{2,1,0:T(8,128)S(1)}, u32[]{:S(2)}, u32[]{:S(2)}) %collective-permute-start.5) | collective-permute-done | bytes 32800 | tf_op jit(solution)/shard_map/ppermute | solution.py:452
  31.7 2.6 %collective-permute-start.6 = (f32[8,8,128]{2,1,0:T(8,128)S(1)}, f32[8,8,128]{2,1,0:T(8,128)S(1)}, u32[]{:S(2)}, u32[]{:S(2)}) collective-permute-start(f32[8,8,128]{2,1,0:T(8,128)S(1)} %add.53), channel_id=1, source_target_pairs={{0,16},{2,18},{4,20},{6,22},{8,24},{10,26},{12,28},{14,30},{16,0},... | collective-permute-start | bytes 98312 | tf_op jit(solution)/shard_map/ppermute | solution.py:452
  34.3 2.2 %collective-permute-done.6 = f32[8,8,128]{2,1,0:T(8,128)S(1)} collective-permute-done((f32[8,8,128]{2,1,0:T(8,128)S(1)}, f32[8,8,128]{2,1,0:T(8,128)S(1)}, u32[]{:S(2)}, u32[]{:S(2)}) %collective-permute-start.6) | collective-permute-done | bytes 32800 | tf_op jit(solution)/shard_map/ppermute | solution.py:452
  36.5 0.0 collective-permute-start.7
  36.5 0.7 %share.1 = f32[12,1,1326]{2,1,0:T(1,128)} custom-call(f32[16,8,128]{2,1,0:T(8,128)S(1)} %get-tuple-element.15.tiles_ref), custom_call_target="tpu_custom_call" | custom-call | tf_op jit(solution)/shard_map/share/pallas_call | solution.py:468
  37.3 0.5 %collective-permute-done.7.other_ref = f32[8,8,128]{2,1,0:T(8,128)S(1)} collective-permute-done((f32[8,8,128]{2,1,0:T(8,128)S(1)}, f32[8,8,128]{2,1,0:T(8,128)S(1)}, u32[]{:S(2)}, u32[]{:S(2)}) %collective-permute-start.7) | collective-permute-done | bytes 32800 | tf_op jit(solution)/shard_map/ppermute | solution.py:452
  37.7 0.7 %root.1 = f32[12,1326]{1,0:T(8,128)} custom-call(f32[8,8,128]{2,1,0:T(8,128)S(1)} %add.54.mine_ref, f32[8,8,128]{2,1,0:T(8,128)S(1)} %collective-permute-done.7.other_ref), custom_call_target="tpu_custom_call" | custom-call | tf_op jit(solution)/shard_map/root/pallas_call | solution.py:480
  (6 shorter events, 0.0 us)
Async XLA Ops:
  1.9 13.4 %collective-permute-start = (bf16[144,1326]{1,0:T(8,128)(2,1)S(1)}, bf16[144,1326]{1,0:T(8,128)(2,1)S(1)}, u32[]{:S(2)}, u32[]{:S(2)}) collective-permute-start(bf16[144,1326]{1,0:T(8,128)(2,1)S(1)} %bitcast.20), channel_id=1, source_target_pairs={{0,1},{1,0},{2,3},{3,2},{4,5},{5,4},{6,7},{7,6},{8,9},{9,8},{10,11... | collective-permute-start | bytes 1145672 | tf_op jit(solution)/shard_map/ppermute | solution.py:357
  7.2 8.0 %collective-permute-start.1 = (bf16[16,1326]{1,0:T(8,128)(2,1)}, bf16[16,1326]{1,0:T(8,128)(2,1)S(1)}, u32[]{:S(2)}, u32[]{:S(2)}) collective-permute-start(bf16[16,1326]{1,0:T(8,128)(2,1)} %get-tuple-element.11), channel_id=1, source_target_pairs={{0,1},{1,0},{2,3},{3,2},{4,5},{5,4},{6,7},{7,6},{8,9},{9,8},{10,11... | collective-permute-start | bytes 127304 | tf_op jit(solution)/shard_map/ppermute | solution.py:357
  7.3 0.9 %copy-start = (f32[24,1408]{1,0:T(8,128)S(1)}, f32[24,1408]{1,0:T(8,128)}, u32[]{:S(2)}) copy-start(f32[24,1408]{1,0:T(8,128)} %get-tuple-element.8.info_ref) | copy-start | bytes 405508
  16.5 4.3 %collective-permute-start.2 = (f32[16,8,128]{2,1,0:T(8,128)S(1)}, f32[16,8,128]{2,1,0:T(8,128)S(1)}, u32[]{:S(2)}, u32[]{:S(2)}) collective-permute-start(f32[16,8,128]{2,1,0:T(8,128)S(1)} %get-tuple-element.13), channel_id=1, source_target_pairs={{0,1},{1,0},{2,3},{3,2},{4,5},{5,4},{6,7},{7,6},{8,9},{9,8},{10,11... | collective-permute-start | bytes 196616 | tf_op jit(solution)/shard_map/ppermute | solution.py:357
  20.8 1.3 %collective-permute-start.3 = (f32[8,8,128]{2,1,0:T(8,128)S(1)}, f32[8,8,128]{2,1,0:T(8,128)S(1)}, u32[]{:S(2)}, u32[]{:S(2)}) collective-permute-start(f32[8,8,128]{2,1,0:T(8,128)S(1)} %dynamic-slice_bitcast_fusion), channel_id=1, source_target_pairs={{0,2},{2,0},{4,6},{6,4},{8,10},{10,8},{12,14},{14,12},{16,18},{18,... | collective-permute-start | bytes 98312 | tf_op jit(solution)/shard_map/ppermute | solution.py:452
  22.1 5.7 %collective-permute-start.4 = (f32[8,8,128]{2,1,0:T(8,128)S(1)}, f32[8,8,128]{2,1,0:T(8,128)S(1)}, u32[]{:S(2)}, u32[]{:S(2)}) collective-permute-start(f32[8,8,128]{2,1,0:T(8,128)S(1)} %bitcast_add_fusion), channel_id=1, source_target_pairs={{0,4},{2,6},{4,0},{6,2},{8,12},{10,14},{12,8},{14,10},{16,20},{18,... | collective-permute-start | bytes 98312 | tf_op jit(solution)/shard_map/ppermute | solution.py:452
  27.8 3.9 %collective-permute-start.5 = (f32[8,8,128]{2,1,0:T(8,128)S(1)}, f32[8,8,128]{2,1,0:T(8,128)S(1)}, u32[]{:S(2)}, u32[]{:S(2)}) collective-permute-start(f32[8,8,128]{2,1,0:T(8,128)S(1)} %add.52), channel_id=1, source_target_pairs={{0,8},{2,10},{4,12},{6,14},{8,0},{10,2},{12,4},{14,6},{16,24},{18,... | collective-permute-start | bytes 98312 | tf_op jit(solution)/shard_map/ppermute | solution.py:452
  31.7 4.8 %collective-permute-start.6 = (f32[8,8,128]{2,1,0:T(8,128)S(1)}, f32[8,8,128]{2,1,0:T(8,128)S(1)}, u32[]{:S(2)}, u32[]{:S(2)}) collective-permute-start(f32[8,8,128]{2,1,0:T(8,128)S(1)} %add.53), channel_id=1, source_target_pairs={{0,16},{2,18},{4,20},{6,22},{8,24},{10,26},{12,28},{14,30},{16,0},... | collective-permute-start | bytes 98312 | tf_op jit(solution)/shard_map/ppermute | solution.py:452
  36.5 1.2 %collective-permute-start.7 = (f32[8,8,128]{2,1,0:T(8,128)S(1)}, f32[8,8,128]{2,1,0:T(8,128)S(1)}, u32[]{:S(2)}, u32[]{:S(2)}) collective-permute-start(f32[8,8,128]{2,1,0:T(8,128)S(1)} %add.54.mine_ref), channel_id=1, source_target_pairs={{0,2},{2,0},{4,6},{6,4},{8,10},{10,8},{12,14},{14,12},{16,18},{18,... | collective-permute-start | bytes 98312 | tf_op jit(solution)/shard_map/ppermute | solution.py:452

commit v3 on v2

--- a/solution.py
+++ b/solution.py
@@ -461,8 +461,13 @@
     mine = mine + swap(lax.dynamic_index_in_dim(root, 1 - parity, 0, keepdims=False), 1)
     step = 2
     while step < board_count:
-        mine = mine + swap(mine, step)
-        step *= 2
+        if step == 2 and board_count >= 8:
+            near, far, across = [swap(mine, at) for at in (2, 4, 6)]
+            mine = (mine + near) + (far + across)
+            step *= 4
+        else:
+            mine = mine + swap(mine, step)
+            step *= 2
     other = swap(mine, 1)
 
     turn_value = pl.pallas_call(

time: 38.8 us -> 38.7 us (level)
  waiting for transfers between devices: 15 us -> 12.8 us
  starting transfers between devices: 10.4 us -> 12.3 us
    ppermute x5 -> x6, waiting for transfers between devices: 9.57 us -> 7.33 us  [swap(): lax.ppermute(array, 'board', [(at, at ^ step) for at in range(board_count)])]
    ppermute x5 -> x6, starting transfers between devices: 6.56 us -> 8.48 us  [swap(): lax.ppermute(array, 'board', [(at, at ^ step) for at in range(board_count)])]
  transfers between devices with their start and end apart: 8 -> 9, of which waited for: 7 -> 7; matrix products, arithmetic and copies ran while one was open for 0% -> 0% of each run, Pallas kernels for 18% -> 18%
where the time goes in v3:
time: 38.7 us; the launch traced here: 38.1 us
  waiting for transfers between devices  12.8 us (33%)
  starting transfers between devices  12.3 us (32%)
  Pallas kernels  8.84 us (23%)
  local copies, waits for them, and re-layouts  2.1 us (5%)
  between operations  2.05 us (5%)
    ppermute x6, starting transfers between devices, swap(): lax.ppermute(array, 'board', [(at, at ^ step) for at in range(board_count)])  8.48 us
    ppermute x6, waiting for transfers between devices, swap(): lax.ppermute(array, 'board', [(at, at ^ step) for at in range(board_count)])  7.33 us
    ppermute x3, waiting for transfers between devices, shift(): lax.ppermute(array, 'seq', [(at, (at + step) % seq_count) for at in range...  5.45 us
    pallas_call x1, Pallas kernels, body(): pl.pallas_call(functools.partial(build_kernel, rounds), out_shape=[jax.Sh...  4.38 us
    ppermute x3, starting transfers between devices, shift(): lax.ppermute(array, 'seq', [(at, (at + step) % seq_count) for at in range...  3.84 us
    pallas_call x1, Pallas kernels, body(): pl.pallas_call(functools.partial(pack_kernel, rounds, seq_count), out_sha...  1.72 us
    pallas_call x1, Pallas kernels, body(): pl.pallas_call(functools.partial(value_kernel, rounds, seq_count, nodes,...  1.3 us
    dynamic_slice x1, local copies, waits for them, and re-layouts, strategy_for(): rows = lax.dynamic_slice_in_dim(split, owner, 1, axis=1)  1.19 us
  transfers between devices with their start and end apart: 9, of which 7 were waited for; matrix products, arithmetic and copies ran while one was open for 0% of the time, Pallas kernels for 18%

profile of v3, /device:TPU:0, one launch (start us, length us, event | category | flops | bytes accessed | tf_op | source)
XLA Modules:
  0.0 38.1 jit_solution(3765207536245558745)
XLA Ops:
  0.7 1.2 %constant_dynamic-slice_fusion = (bf16[3,1,48,1326]{3,2,1,0:T(8,128)(2,1)S(1)}, bf16[3,1,48,1326]{3,2,1,0:T(8,128)(2,1)S(1)}) fusion(bf16[3,2,48,1326]{3,2,1,0:T(8,128)(2,1)} %bitcast.19, s32[]{:T(128)S(6)} %select_n.31, s32[]{:T(128)S(6)} %select_n.29), kind=kLoop, calls=%fused_computation.4 | loop fusion | bytes 1527560 | tf_op jit(solution)/shard_map/dynamic_slice | solution.py:365
  1.9 3.0 %collective-permute-start = (bf16[144,1326]{1,0:T(8,128)(2,1)S(1)}, bf16[144,1326]{1,0:T(8,128)(2,1)S(1)}, u32[]{:S(2)}, u32[]{:S(2)}) collective-permute-start(bf16[144,1326]{1,0:T(8,128)(2,1)S(1)} %bitcast.20), channel_id=1, source_target_pairs={{0,1},{1,0},{2,3},{3,2},{4,5},{5,4},{6,7},{7,6},{8,9},{9,8},{10,11... | collective-permute-start | bytes 1145672 | tf_op jit(solution)/shard_map/ppermute | solution.py:357
  5.5 1.7 %pack.1 = (bf16[16,1326]{1,0:T(8,128)(2,1)}, f32[24,1408]{1,0:T(8,128)}) custom-call(bf16[1,12,1326]{2,1,0:T(8,128)(2,1)} %reach_ref.1, s32[1,48]{1,0:T(1,128)} %bitcast.26, f32[1,48]{1,0:T(1,128)} %bitcast.27, s32[6,1,1326]{2,1,0:T(1,128)} %bitcast.24, s32[5,1,6]{2,1,0:T(1,128)} %bitcast.25, s32[1]{0:T(128)S(6)} %copy.14.count_ref), custom_call_target="tpu_custom_call" | custom-call | tf_op jit(solution)/shard_map/pack/pallas_call | solution.py:381
  7.2 0.1 collective-permute-start.1
  7.3 0.9 %copy-done = f32[24,1408]{1,0:T(8,128)S(1)} copy-done((f32[24,1408]{1,0:T(8,128)S(1)}, f32[24,1408]{1,0:T(8,128)}, u32[]{:S(2)}) %copy-start) | copy-done | bytes 135192
  8.2 4.4 %build.1 = (bf16[3,1408,1408]{2,1,0:T(8,128)(2,1)S(1)}, f32[24,1408]{1,0:T(8,128)S(1)}) custom-call(f32[24,1408]{1,0:T(8,128)S(1)} %copy-done), custom_call_target="tpu_custom_call" | custom-call | flops 59473920 | bytes 7929856 | tf_op jit(solution)/shard_map/build/pallas_call | solution.py:413
  12.6 2.6 %collective-permute-done.1.refs_4_ = bf16[16,1326]{1,0:T(8,128)(2,1)S(1)} collective-permute-done((bf16[16,1326]{1,0:T(8,128)(2,1)}, bf16[16,1326]{1,0:T(8,128)(2,1)S(1)}, u32[]{:S(2)}, u32[]{:S(2)}) %collective-permute-start.1) | collective-permute-done | bytes 42464 | tf_op jit(solution)/shard_map/ppermute | solution.py:357
  15.2 0.0 collective-permute-done.refs_3_
  15.2 1.3 %value.1 = (f32[16,8,128]{2,1,0:T(8,128)S(1)}, f32[16,8,128]{2,1,0:T(8,128)S(1)}) custom-call(bf16[3,1408,1408]{2,1,0:T(8,128)(2,1)S(1)} %get-tuple-element.9.refs_0_, f32[24,1408]{1,0:T(8,128)S(1)} %get-tuple-element.10.refs_1_, bf16[144,1326]{1,0:T(8,128)(2,1)S(1)} %bitcast.18, bf16[144,1326]{1,0:T(8,128)(2,1)S(1)} %collective-permute-done.refs_3_, ...), custom_call_target="tpu_custom_call" | custom-call | tf_op jit(solution)/shard_map/value/pallas_call | solution.py:435
  16.5 0.8 %collective-permute-start.2 = (f32[16,8,128]{2,1,0:T(8,128)S(1)}, f32[16,8,128]{2,1,0:T(8,128)S(1)}, u32[]{:S(2)}, u32[]{:S(2)}) collective-permute-start(f32[16,8,128]{2,1,0:T(8,128)S(1)} %get-tuple-element.13), channel_id=1, source_target_pairs={{0,1},{1,0},{2,3},{3,2},{4,5},{5,4},{6,7},{7,6},{8,9},{9,8},{10,11... | collective-permute-start | bytes 196616 | tf_op jit(solution)/shard_map/ppermute | solution.py:357
  17.9 2.9 %collective-permute-done.2 = f32[16,8,128]{2,1,0:T(8,128)S(1)} collective-permute-done((f32[16,8,128]{2,1,0:T(8,128)S(1)}, f32[16,8,128]{2,1,0:T(8,128)S(1)}, u32[]{:S(2)}, u32[]{:S(2)}) %collective-permute-start.2) | collective-permute-done | bytes 65568 | tf_op jit(solution)/shard_map/ppermute | solution.py:357
  20.8 0.1 collective-permute-start.3
  20.9 1.2 %collective-permute-done.3 = f32[8,8,128]{2,1,0:T(8,128)S(1)} collective-permute-done((f32[8,8,128]{2,1,0:T(8,128)S(1)}, f32[8,8,128]{2,1,0:T(8,128)S(1)}, u32[]{:S(2)}, u32[]{:S(2)}) %collective-permute-start.3) | collective-permute-done | bytes 32800 | tf_op jit(solution)/shard_map/ppermute | solution.py:452
  22.1 1.8 %collective-permute-start.4 = (f32[8,8,128]{2,1,0:T(8,128)S(1)}, f32[8,8,128]{2,1,0:T(8,128)S(1)}, u32[]{:S(2)}, u32[]{:S(2)}) collective-permute-start(f32[8,8,128]{2,1,0:T(8,128)S(1)} %bitcast_add_fusion), channel_id=1, source_target_pairs={{0,4},{2,6},{4,0},{6,2},{8,12},{10,14},{12,8},{14,10},{16,20},{18,... | collective-permute-start | bytes 98312 | tf_op jit(solution)/shard_map/ppermute | solution.py:452
  23.9 2.2 %collective-permute-start.5 = (f32[8,8,128]{2,1,0:T(8,128)S(1)}, f32[8,8,128]{2,1,0:T(8,128)S(1)}, u32[]{:S(2)}, u32[]{:S(2)}) collective-permute-start(f32[8,8,128]{2,1,0:T(8,128)S(1)} %bitcast_add_fusion), channel_id=1, source_target_pairs={{0,8},{2,10},{4,12},{6,14},{8,0},{10,2},{12,4},{14,6},{16,24},{18,... | collective-permute-start | bytes 98312 | tf_op jit(solution)/shard_map/ppermute | solution.py:452
  26.0 1.4 %collective-permute-start.6 = (f32[8,8,128]{2,1,0:T(8,128)S(1)}, f32[8,8,128]{2,1,0:T(8,128)S(1)}, u32[]{:S(2)}, u32[]{:S(2)}) collective-permute-start(f32[8,8,128]{2,1,0:T(8,128)S(1)} %bitcast_add_fusion), channel_id=1, source_target_pairs={{0,12},{2,14},{4,8},{6,10},{8,4},{10,6},{12,0},{14,2},{16,28},{18,... | collective-permute-start | bytes 98312 | tf_op jit(solution)/shard_map/ppermute | solution.py:452
  27.4 0.0 collective-permute-done.4
  27.4 0.5 %collective-permute-done.5 = f32[8,8,128]{2,1,0:T(8,128)S(1)} collective-permute-done((f32[8,8,128]{2,1,0:T(8,128)S(1)}, f32[8,8,128]{2,1,0:T(8,128)S(1)}, u32[]{:S(2)}, u32[]{:S(2)}) %collective-permute-start.5) | collective-permute-done | bytes 32800 | tf_op jit(solution)/shard_map/ppermute | solution.py:452
  27.9 2.9 %collective-permute-done.6 = f32[8,8,128]{2,1,0:T(8,128)S(1)} collective-permute-done((f32[8,8,128]{2,1,0:T(8,128)S(1)}, f32[8,8,128]{2,1,0:T(8,128)S(1)}, u32[]{:S(2)}, u32[]{:S(2)}) %collective-permute-start.6) | collective-permute-done | bytes 32800 | tf_op jit(solution)/shard_map/ppermute | solution.py:452
  30.9 3.1 %collective-permute-start.7 = (f32[8,8,128]{2,1,0:T(8,128)S(1)}, f32[8,8,128]{2,1,0:T(8,128)S(1)}, u32[]{:S(2)}, u32[]{:S(2)}) collective-permute-start(f32[8,8,128]{2,1,0:T(8,128)S(1)} %add_add_fusion), channel_id=1, source_target_pairs={{0,16},{2,18},{4,20},{6,22},{8,24},{10,26},{12,28},{14,30},{16,0},... | collective-permute-start | bytes 98312 | tf_op jit(solution)/shard_map/ppermute | solution.py:452
  34.0 2.2 %collective-permute-done.7 = f32[8,8,128]{2,1,0:T(8,128)S(1)} collective-permute-done((f32[8,8,128]{2,1,0:T(8,128)S(1)}, f32[8,8,128]{2,1,0:T(8,128)S(1)}, u32[]{:S(2)}, u32[]{:S(2)}) %collective-permute-start.7) | collective-permute-done | bytes 32800 | tf_op jit(solution)/shard_map/ppermute | solution.py:452
  36.2 0.7 %share.1 = f32[12,1,1326]{2,1,0:T(1,128)} custom-call(f32[16,8,128]{2,1,0:T(8,128)S(1)} %get-tuple-element.15.tiles_ref), custom_call_target="tpu_custom_call" | custom-call | tf_op jit(solution)/shard_map/share/pallas_call | solution.py:473
  36.9 0.5 %collective-permute-done.8.other_ref = f32[8,8,128]{2,1,0:T(8,128)S(1)} collective-permute-done((f32[8,8,128]{2,1,0:T(8,128)S(1)}, f32[8,8,128]{2,1,0:T(8,128)S(1)}, u32[]{:S(2)}, u32[]{:S(2)}) %collective-permute-start.8) | collective-permute-done | bytes 32800 | tf_op jit(solution)/shard_map/ppermute | solution.py:452
  37.4 0.7 %root.1 = f32[12,1326]{1,0:T(8,128)} custom-call(f32[8,8,128]{2,1,0:T(8,128)S(1)} %add.58.mine_ref, f32[8,8,128]{2,1,0:T(8,128)S(1)} %collective-permute-done.8.other_ref), custom_call_target="tpu_custom_call" | custom-call | tf_op jit(solution)/shard_map/root/pallas_call | solution.py:485
  (7 shorter events, 0.0 us)
Async XLA Ops:
  1.9 13.4 %collective-permute-start = (bf16[144,1326]{1,0:T(8,128)(2,1)S(1)}, bf16[144,1326]{1,0:T(8,128)(2,1)S(1)}, u32[]{:S(2)}, u32[]{:S(2)}) collective-permute-start(bf16[144,1326]{1,0:T(8,128)(2,1)S(1)} %bitcast.20), channel_id=1, source_target_pairs={{0,1},{1,0},{2,3},{3,2},{4,5},{5,4},{6,7},{7,6},{8,9},{9,8},{10,11... | collective-permute-start | bytes 1145672 | tf_op jit(solution)/shard_map/ppermute | solution.py:357
  7.2 8.0 %collective-permute-start.1 = (bf16[16,1326]{1,0:T(8,128)(2,1)}, bf16[16,1326]{1,0:T(8,128)(2,1)S(1)}, u32[]{:S(2)}, u32[]{:S(2)}) collective-permute-start(bf16[16,1326]{1,0:T(8,128)(2,1)} %get-tuple-element.11), channel_id=1, source_target_pairs={{0,1},{1,0},{2,3},{3,2},{4,5},{5,4},{6,7},{7,6},{8,9},{9,8},{10,11... | collective-permute-start | bytes 127304 | tf_op jit(solution)/shard_map/ppermute | solution.py:357
  7.3 0.9 %copy-start = (f32[24,1408]{1,0:T(8,128)S(1)}, f32[24,1408]{1,0:T(8,128)}, u32[]{:S(2)}) copy-start(f32[24,1408]{1,0:T(8,128)} %get-tuple-element.8.info_ref) | copy-start | bytes 405508
  16.5 4.3 %collective-permute-start.2 = (f32[16,8,128]{2,1,0:T(8,128)S(1)}, f32[16,8,128]{2,1,0:T(8,128)S(1)}, u32[]{:S(2)}, u32[]{:S(2)}) collective-permute-start(f32[16,8,128]{2,1,0:T(8,128)S(1)} %get-tuple-element.13), channel_id=1, source_target_pairs={{0,1},{1,0},{2,3},{3,2},{4,5},{5,4},{6,7},{7,6},{8,9},{9,8},{10,11... | collective-permute-start | bytes 196616 | tf_op jit(solution)/shard_map/ppermute | solution.py:357
  20.8 1.3 %collective-permute-start.3 = (f32[8,8,128]{2,1,0:T(8,128)S(1)}, f32[8,8,128]{2,1,0:T(8,128)S(1)}, u32[]{:S(2)}, u32[]{:S(2)}) collective-permute-start(f32[8,8,128]{2,1,0:T(8,128)S(1)} %dynamic-slice_bitcast_fusion), channel_id=1, source_target_pairs={{0,2},{2,0},{4,6},{6,4},{8,10},{10,8},{12,14},{14,12},{16,18},{18,... | collective-permute-start | bytes 98312 | tf_op jit(solution)/shard_map/ppermute | solution.py:452
  22.1 5.3 %collective-permute-start.4 = (f32[8,8,128]{2,1,0:T(8,128)S(1)}, f32[8,8,128]{2,1,0:T(8,128)S(1)}, u32[]{:S(2)}, u32[]{:S(2)}) collective-permute-start(f32[8,8,128]{2,1,0:T(8,128)S(1)} %bitcast_add_fusion), channel_id=1, source_target_pairs={{0,4},{2,6},{4,0},{6,2},{8,12},{10,14},{12,8},{14,10},{16,20},{18,... | collective-permute-start | bytes 98312 | tf_op jit(solution)/shard_map/ppermute | solution.py:452
  23.9 4.0 %collective-permute-start.5 = (f32[8,8,128]{2,1,0:T(8,128)S(1)}, f32[8,8,128]{2,1,0:T(8,128)S(1)}, u32[]{:S(2)}, u32[]{:S(2)}) collective-permute-start(f32[8,8,128]{2,1,0:T(8,128)S(1)} %bitcast_add_fusion), channel_id=1, source_target_pairs={{0,8},{2,10},{4,12},{6,14},{8,0},{10,2},{12,4},{14,6},{16,24},{18,... | collective-permute-start | bytes 98312 | tf_op jit(solution)/shard_map/ppermute | solution.py:452
  26.0 4.8 %collective-permute-start.6 = (f32[8,8,128]{2,1,0:T(8,128)S(1)}, f32[8,8,128]{2,1,0:T(8,128)S(1)}, u32[]{:S(2)}, u32[]{:S(2)}) collective-permute-start(f32[8,8,128]{2,1,0:T(8,128)S(1)} %bitcast_add_fusion), channel_id=1, source_target_pairs={{0,12},{2,14},{4,8},{6,10},{8,4},{10,6},{12,0},{14,2},{16,28},{18,... | collective-permute-start | bytes 98312 | tf_op jit(solution)/shard_map/ppermute | solution.py:452
  30.9 5.3 %collective-permute-start.7 = (f32[8,8,128]{2,1,0:T(8,128)S(1)}, f32[8,8,128]{2,1,0:T(8,128)S(1)}, u32[]{:S(2)}, u32[]{:S(2)}) collective-permute-start(f32[8,8,128]{2,1,0:T(8,128)S(1)} %add_add_fusion), channel_id=1, source_target_pairs={{0,16},{2,18},{4,20},{6,22},{8,24},{10,26},{12,28},{14,30},{16,0},... | collective-permute-start | bytes 98312 | tf_op jit(solution)/shard_map/ppermute | solution.py:452
  36.2 1.2 %collective-permute-start.8 = (f32[8,8,128]{2,1,0:T(8,128)S(1)}, f32[8,8,128]{2,1,0:T(8,128)S(1)}, u32[]{:S(2)}, u32[]{:S(2)}) collective-permute-start(f32[8,8,128]{2,1,0:T(8,128)S(1)} %add.58.mine_ref), channel_id=1, source_target_pairs={{0,2},{2,0},{4,6},{6,4},{8,10},{10,8},{12,14},{14,12},{16,18},{18,... | collective-permute-start | bytes 98312 | tf_op jit(solution)/shard_map/ppermute | solution.py:452

commit v4 on v3

--- a/solution.py
+++ b/solution.py
@@ -179,17 +179,16 @@
     for at in range(rounds):
         river = jnp.minimum(at * seq_count + here, rivers - 1)
         info[at : at + 1, :hands] = rank_tmp[river].astype(jnp.float32)
-        live = jnp.where(low >= 0, 1.0, 0.0)
+        alive = jnp.where(at * seq_count + here < live_count, 1.0, 0.0)
+        live = jnp.where(low >= 0, alive, 0.0)
         for slot in range(board_tmp.shape[0]):
             card = board_tmp[slot, 0, river]
             live = jnp.where((low == card) | (high == card), 0.0, live)
         info[rounds + at : rounds + at + 1, :] = live
     info[base : base + 1, :] = 1.0 / (hands * jnp.full((1, padded), live_count.astype(jnp.float32)))
-    live_rounds = lax.div(live_count - here + seq_count - 1, seq_count)
-    info[base + 1 : base + 2, :] = jnp.full((1, padded), live_rounds.astype(jnp.float32))
-    info[base + 2 : base + 3, :leaves] = parent
-    info[base + 3 : base + 4, :leaves] = pot
-    info[base + 4 : base + 4 + nodes, :hands] = reach
+    info[base + 1 : base + 2, :leaves] = parent
+    info[base + 2 : base + 3, :leaves] = pot
+    info[base + 3 : base + 3 + nodes, :hands] = reach
     kept = pltpu.make_async_copy(info, info_ref, out_sems.at[1])
     kept.start()
     sent.wait()
@@ -246,9 +245,9 @@
     reach, places, pots = [], [], []
     for at in range(seq_count):
         if at == 0:
-            reach.append(info_ref[base + 4 : base + 4 + local_nodes, :hands])
-            parent = info_ref[base + 2 : base + 3, :LANES]
-            pots.append(info_ref[base + 3 : base + 4, :LANES])
+            reach.append(info_ref[base + 3 : base + 3 + local_nodes, :hands])
+            parent = info_ref[base + 1 : base + 2, :LANES]
+            pots.append(info_ref[base + 2 : base + 3, :LANES])
         else:
             small = smalls[at - 1][...].astype(jnp.float32)
             reach.append(small[:local_nodes])
@@ -284,25 +283,23 @@
     lookup = jnp.concatenate(reach * (leaves // nodes), axis=0)
 
     reach_all[...] = jnp.zeros_like(reach_all)
-    total[...] = jnp.zeros_like(total)
-    live_rounds = jnp.max(info_ref[base + 1 : base + 2, :LANES])
+    gains = []
     for at in range(rounds):
-
-        @pl.when(live_rounds > at)
-        def _():
-            rows = slice(at * local_leaves, (at + 1) * local_leaves)
-            live = info_ref[rounds + at : rounds + at + 1, :]
-            strat = jnp.dot(picks[0], own_ref[rows, :], preferred_element_type=jnp.float32)
-            for pick, pack in zip(picks[1:], came):
-                strat = strat + jnp.dot(pick, pack[rows, :], preferred_element_type=jnp.float32)
-            reach_all[:, :hands] = (lookup * strat * live[:, :hands]).astype(jnp.bfloat16)
-            shown = jnp.dot(reach_all[...], payoff_ref[at], preferred_element_type=jnp.float32)
-            value = shown * pot_sorted
-            best = value[:nodes]
-            for row in range(nodes, leaves, nodes):
-                best = jnp.maximum(best, value[row : row + nodes])
-            gain = best * (live * info_ref[base : base + 1, :])
-            total[...] += gain
+        rows = slice(at * local_leaves, (at + 1) * local_leaves)
+        live = info_ref[rounds + at : rounds + at + 1, :]
+        strat = jnp.dot(picks[0], own_ref[rows, :], preferred_element_type=jnp.float32)
+        for pick, pack in zip(picks[1:], came):
+            strat = strat + jnp.dot(pick, pack[rows, :], preferred_element_type=jnp.float32)
+        reach_all[at, :, :hands] = (lookup * strat * live[:, :hands]).astype(jnp.bfloat16)
+    for at in range(rounds):
+        live = info_ref[rounds + at : rounds + at + 1, :]
+        shown = jnp.dot(reach_all[at], payoff_ref[at], preferred_element_type=jnp.float32)
+        value = shown * pot_sorted
+        best = value[:nodes]
+        for row in range(nodes, leaves, nodes):
+            best = jnp.maximum(best, value[row : row + nodes])
+        gains.append(best * (live * info_ref[base : base + 1, :]))
+    total[...] = sum(gains[1:], gains[0])
 
     short = round_up(local_nodes, 8) - local_nodes
     for step in range(seq_count):
@@ -377,7 +374,7 @@
     came = [shift(strategy_for(step), step) for step in range(1, seq_count)]
 
     small_rows = round_up(local_nodes + 4, 16)
-    info_rows = round_up(2 * rounds + 4 + local_nodes, 8)
+    info_rows = round_up(2 * rounds + 3 + local_nodes, 8)
     small, info = pl.pallas_call(
         functools.partial(pack_kernel, rounds, seq_count),
         out_shape=[
@@ -439,7 +436,7 @@
         out_specs=[vmem] * seq_count,
         scratch_shapes=[
             pltpu.VMEM((nodes, padded), jnp.float32),
-            pltpu.VMEM((leaves, padded), jnp.bfloat16),
+            pltpu.VMEM((rounds, leaves, padded), jnp.bfloat16),
         ],
         compiler_params=params,
         name="value",

time: 38.7 us -> 38.9 us (level)
  Pallas kernels: 8.84 us -> 10.2 us
  starting transfers between devices: 12.3 us -> 11 us
  waiting for transfers between devices: 12.8 us -> 13.2 us
    ppermute x6, starting transfers between devices: 8.48 us -> 6.22 us  [swap(): lax.ppermute(array, 'board', [(at, at ^ step) for at in range(board_count)])]
    ppermute x6, waiting for transfers between devices: 7.33 us -> 8.79 us  [swap(): lax.ppermute(array, 'board', [(at, at ^ step) for at in range(board_count)])]
    pallas_call x1, Pallas kernels: 1.3 us -> 2.64 us  [body(): pl.pallas_call(functools.partial(value_kernel, rounds, seq_count, nodes,...]
    ppermute x3, waiting for transfers between devices: 5.45 us -> 4.45 us  [shift(): lax.ppermute(array, 'seq', [(at, (at + step) % seq_count) for at in range...]
    ppermute x3, starting transfers between devices: 3.84 us -> 4.83 us  [shift(): lax.ppermute(array, 'seq', [(at, (at + step) % seq_count) for at in range...]
  transfers between devices with their start and end apart: 9 -> 9, of which waited for: 7 -> 8; matrix products, arithmetic and copies ran while one was open for 0% -> 0% of each run, Pallas kernels for 18% -> 18%
where the time goes in v4:
time: 38.9 us; the launch traced here: 38.7 us
  waiting for transfers between devices  13.2 us (34%)
  starting transfers between devices  11 us (28%)
  Pallas kernels  10.2 us (26%)
  local copies, waits for them, and re-layouts  2.1 us (5%)
  between operations  2.05 us (5%)
    ppermute x6, waiting for transfers between devices, swap(): lax.ppermute(array, 'board', [(at, at ^ step) for at in range(board_count)])  8.79 us
    ppermute x6, starting transfers between devices, swap(): lax.ppermute(array, 'board', [(at, at ^ step) for at in range(board_count)])  6.22 us
    ppermute x3, starting transfers between devices, shift(): lax.ppermute(array, 'seq', [(at, (at + step) % seq_count) for at in range...  4.83 us
    ppermute x3, waiting for transfers between devices, shift(): lax.ppermute(array, 'seq', [(at, (at + step) % seq_count) for at in range...  4.45 us
    pallas_call x1, Pallas kernels, body(): pl.pallas_call(functools.partial(build_kernel, rounds), out_shape=[jax.Sh...  4.38 us
    pallas_call x1, Pallas kernels, body(): pl.pallas_call(functools.partial(value_kernel, rounds, seq_count, nodes,...  2.64 us
    pallas_call x1, Pallas kernels, body(): pl.pallas_call(functools.partial(pack_kernel, rounds, seq_count), out_sha...  1.72 us
    dynamic_slice x1, local copies, waits for them, and re-layouts, strategy_for(): rows = lax.dynamic_slice_in_dim(split, owner, 1, axis=1)  1.19 us
  transfers between devices with their start and end apart: 9, of which 8 were waited for; matrix products, arithmetic and copies ran while one was open for 0% of the time, Pallas kernels for 18%

profile of v4, /device:TPU:0, one launch (start us, length us, event | category | flops | bytes accessed | tf_op | source)
XLA Modules:
  0.0 38.7 jit_solution(14218615334950288836)
XLA Ops:
  0.7 1.2 %constant_dynamic-slice_fusion = (bf16[3,1,48,1326]{3,2,1,0:T(8,128)(2,1)S(1)}, bf16[3,1,48,1326]{3,2,1,0:T(8,128)(2,1)S(1)}) fusion(bf16[3,2,48,1326]{3,2,1,0:T(8,128)(2,1)} %bitcast.19, s32[]{:T(128)S(6)} %select_n.31, s32[]{:T(128)S(6)} %select_n.29), kind=kLoop, calls=%fused_computation.4 | loop fusion | bytes 1527560 | tf_op jit(solution)/shard_map/dynamic_slice | solution.py:362
  1.9 3.0 %collective-permute-start = (bf16[144,1326]{1,0:T(8,128)(2,1)S(1)}, bf16[144,1326]{1,0:T(8,128)(2,1)S(1)}, u32[]{:S(2)}, u32[]{:S(2)}) collective-permute-start(bf16[144,1326]{1,0:T(8,128)(2,1)S(1)} %bitcast.20), channel_id=1, source_target_pairs={{0,1},{1,0},{2,3},{3,2},{4,5},{5,4},{6,7},{7,6},{8,9},{9,8},{10,11... | collective-permute-start | bytes 1145672 | tf_op jit(solution)/shard_map/ppermute | solution.py:354
  5.5 1.7 %pack.1 = (bf16[16,1326]{1,0:T(8,128)(2,1)}, f32[24,1408]{1,0:T(8,128)}) custom-call(bf16[1,12,1326]{2,1,0:T(8,128)(2,1)} %reach_ref.1, s32[1,48]{1,0:T(1,128)} %bitcast.26, f32[1,48]{1,0:T(1,128)} %bitcast.27, s32[6,1,1326]{2,1,0:T(1,128)} %bitcast.24, s32[5,1,6]{2,1,0:T(1,128)} %bitcast.25, s32[1]{0:T(128)S(6)} %copy.14.count_ref), custom_call_target="tpu_custom_call" | custom-call | tf_op jit(solution)/shard_map/pack/pallas_call | solution.py:378
  7.2 0.1 collective-permute-start.1
  7.3 0.9 %copy-done = f32[24,1408]{1,0:T(8,128)S(1)} copy-done((f32[24,1408]{1,0:T(8,128)S(1)}, f32[24,1408]{1,0:T(8,128)}, u32[]{:S(2)}) %copy-start) | copy-done | bytes 135192
  8.2 4.4 %build.1 = (bf16[3,1408,1408]{2,1,0:T(8,128)(2,1)S(1)}, f32[24,1408]{1,0:T(8,128)S(1)}) custom-call(f32[24,1408]{1,0:T(8,128)S(1)} %copy-done), custom_call_target="tpu_custom_call" | custom-call | flops 59473920 | bytes 7929856 | tf_op jit(solution)/shard_map/build/pallas_call | solution.py:410
  12.6 2.6 %collective-permute-done.1.refs_4_ = bf16[16,1326]{1,0:T(8,128)(2,1)S(1)} collective-permute-done((bf16[16,1326]{1,0:T(8,128)(2,1)}, bf16[16,1326]{1,0:T(8,128)(2,1)S(1)}, u32[]{:S(2)}, u32[]{:S(2)}) %collective-permute-start.1) | collective-permute-done | bytes 42464 | tf_op jit(solution)/shard_map/ppermute | solution.py:354
  15.2 0.0 collective-permute-done.refs_3_
  15.2 2.6 %value.1 = (f32[16,8,128]{2,1,0:T(8,128)S(1)}, f32[16,8,128]{2,1,0:T(8,128)S(1)}) custom-call(bf16[3,1408,1408]{2,1,0:T(8,128)(2,1)S(1)} %get-tuple-element.9.refs_0_, f32[24,1408]{1,0:T(8,128)S(1)} %get-tuple-element.10.refs_1_, bf16[144,1326]{1,0:T(8,128)(2,1)S(1)} %bitcast.18, bf16[144,1326]{1,0:T(8,128)(2,1)S(1)} %collective-permute-done.refs_3_, ...), custom_call_target="tpu_custom_call" | custom-call | tf_op jit(solution)/shard_map/value/pallas_call | solution.py:432
  17.8 1.8 %collective-permute-start.2 = (f32[16,8,128]{2,1,0:T(8,128)S(1)}, f32[16,8,128]{2,1,0:T(8,128)S(1)}, u32[]{:S(2)}, u32[]{:S(2)}) collective-permute-start(f32[16,8,128]{2,1,0:T(8,128)S(1)} %get-tuple-element.13), channel_id=1, source_target_pairs={{0,1},{1,0},{2,3},{3,2},{4,5},{5,4},{6,7},{7,6},{8,9},{9,8},{10,11... | collective-permute-start | bytes 196616 | tf_op jit(solution)/shard_map/ppermute | solution.py:354
  20.3 1.9 %collective-permute-done.2 = f32[16,8,128]{2,1,0:T(8,128)S(1)} collective-permute-done((f32[16,8,128]{2,1,0:T(8,128)S(1)}, f32[16,8,128]{2,1,0:T(8,128)S(1)}, u32[]{:S(2)}, u32[]{:S(2)}) %collective-permute-start.2) | collective-permute-done | bytes 65568 | tf_op jit(solution)/shard_map/ppermute | solution.py:354
  22.2 0.1 collective-permute-start.3
  22.2 1.2 %collective-permute-done.3 = f32[8,8,128]{2,1,0:T(8,128)S(1)} collective-permute-done((f32[8,8,128]{2,1,0:T(8,128)S(1)}, f32[8,8,128]{2,1,0:T(8,128)S(1)}, u32[]{:S(2)}, u32[]{:S(2)}) %collective-permute-start.3) | collective-permute-done | bytes 32800 | tf_op jit(solution)/shard_map/ppermute | solution.py:449
  23.4 1.8 %collective-permute-start.4 = (f32[8,8,128]{2,1,0:T(8,128)S(1)}, f32[8,8,128]{2,1,0:T(8,128)S(1)}, u32[]{:S(2)}, u32[]{:S(2)}) collective-permute-start(f32[8,8,128]{2,1,0:T(8,128)S(1)} %bitcast_add_fusion), channel_id=1, source_target_pairs={{0,4},{2,6},{4,0},{6,2},{8,12},{10,14},{12,8},{14,10},{16,20},{18,... | collective-permute-start | bytes 98312 | tf_op jit(solution)/shard_map/ppermute | solution.py:449
  25.2 1.6 %collective-permute-start.5 = (f32[8,8,128]{2,1,0:T(8,128)S(1)}, f32[8,8,128]{2,1,0:T(8,128)S(1)}, u32[]{:S(2)}, u32[]{:S(2)}) collective-permute-start(f32[8,8,128]{2,1,0:T(8,128)S(1)} %bitcast_add_fusion), channel_id=1, source_target_pairs={{0,8},{2,10},{4,12},{6,14},{8,0},{10,2},{12,4},{14,6},{16,24},{18,... | collective-permute-start | bytes 98312 | tf_op jit(solution)/shard_map/ppermute | solution.py:449
  26.8 0.1 collective-permute-start.6
  26.9 0.4 %collective-permute-done.4 = f32[8,8,128]{2,1,0:T(8,128)S(1)} collective-permute-done((f32[8,8,128]{2,1,0:T(8,128)S(1)}, f32[8,8,128]{2,1,0:T(8,128)S(1)}, u32[]{:S(2)}, u32[]{:S(2)}) %collective-permute-start.4) | collective-permute-done | bytes 32800 | tf_op jit(solution)/shard_map/ppermute | solution.py:449
  27.3 1.9 %collective-permute-done.5 = f32[8,8,128]{2,1,0:T(8,128)S(1)} collective-permute-done((f32[8,8,128]{2,1,0:T(8,128)S(1)}, f32[8,8,128]{2,1,0:T(8,128)S(1)}, u32[]{:S(2)}, u32[]{:S(2)}) %collective-permute-start.5) | collective-permute-done | bytes 32800 | tf_op jit(solution)/shard_map/ppermute | solution.py:449
  29.3 2.3 %collective-permute-done.6 = f32[8,8,128]{2,1,0:T(8,128)S(1)} collective-permute-done((f32[8,8,128]{2,1,0:T(8,128)S(1)}, f32[8,8,128]{2,1,0:T(8,128)S(1)}, u32[]{:S(2)}, u32[]{:S(2)}) %collective-permute-start.6) | collective-permute-done | bytes 32800 | tf_op jit(solution)/shard_map/ppermute | solution.py:449
  31.6 2.7 %collective-permute-start.7 = (f32[8,8,128]{2,1,0:T(8,128)S(1)}, f32[8,8,128]{2,1,0:T(8,128)S(1)}, u32[]{:S(2)}, u32[]{:S(2)}) collective-permute-start(f32[8,8,128]{2,1,0:T(8,128)S(1)} %add_add_fusion), channel_id=1, source_target_pairs={{0,16},{2,18},{4,20},{6,22},{8,24},{10,26},{12,28},{14,30},{16,0},... | collective-permute-start | bytes 98312 | tf_op jit(solution)/shard_map/ppermute | solution.py:449
  34.3 2.4 %collective-permute-done.7 = f32[8,8,128]{2,1,0:T(8,128)S(1)} collective-permute-done((f32[8,8,128]{2,1,0:T(8,128)S(1)}, f32[8,8,128]{2,1,0:T(8,128)S(1)}, u32[]{:S(2)}, u32[]{:S(2)}) %collective-permute-start.7) | collective-permute-done | bytes 32800 | tf_op jit(solution)/shard_map/ppermute | solution.py:449
  36.7 0.7 %share.1 = f32[12,1,1326]{2,1,0:T(1,128)} custom-call(f32[16,8,128]{2,1,0:T(8,128)S(1)} %get-tuple-element.15.tiles_ref), custom_call_target="tpu_custom_call" | custom-call | tf_op jit(solution)/shard_map/share/pallas_call | solution.py:470
  37.5 0.5 %collective-permute-done.8.other_ref = f32[8,8,128]{2,1,0:T(8,128)S(1)} collective-permute-done((f32[8,8,128]{2,1,0:T(8,128)S(1)}, f32[8,8,128]{2,1,0:T(8,128)S(1)}, u32[]{:S(2)}, u32[]{:S(2)}) %collective-permute-start.8) | collective-permute-done | bytes 32800 | tf_op jit(solution)/shard_map/ppermute | solution.py:449
  37.9 0.7 %root.1 = f32[12,1326]{1,0:T(8,128)} custom-call(f32[8,8,128]{2,1,0:T(8,128)S(1)} %add.58.mine_ref, f32[8,8,128]{2,1,0:T(8,128)S(1)} %collective-permute-done.8.other_ref), custom_call_target="tpu_custom_call" | custom-call | tf_op jit(solution)/shard_map/root/pallas_call | solution.py:482
  (7 shorter events, 0.0 us)
Async XLA Ops:
  1.9 13.4 %collective-permute-start = (bf16[144,1326]{1,0:T(8,128)(2,1)S(1)}, bf16[144,1326]{1,0:T(8,128)(2,1)S(1)}, u32[]{:S(2)}, u32[]{:S(2)}) collective-permute-start(bf16[144,1326]{1,0:T(8,128)(2,1)S(1)} %bitcast.20), channel_id=1, source_target_pairs={{0,1},{1,0},{2,3},{3,2},{4,5},{5,4},{6,7},{7,6},{8,9},{9,8},{10,11... | collective-permute-start | bytes 1145672 | tf_op jit(solution)/shard_map/ppermute | solution.py:354
  7.2 8.0 %collective-permute-start.1 = (bf16[16,1326]{1,0:T(8,128)(2,1)}, bf16[16,1326]{1,0:T(8,128)(2,1)S(1)}, u32[]{:S(2)}, u32[]{:S(2)}) collective-permute-start(bf16[16,1326]{1,0:T(8,128)(2,1)} %get-tuple-element.11), channel_id=1, source_target_pairs={{0,1},{1,0},{2,3},{3,2},{4,5},{5,4},{6,7},{7,6},{8,9},{9,8},{10,11... | collective-permute-start | bytes 127304 | tf_op jit(solution)/shard_map/ppermute | solution.py:354
  7.3 0.9 %copy-start = (f32[24,1408]{1,0:T(8,128)S(1)}, f32[24,1408]{1,0:T(8,128)}, u32[]{:S(2)}) copy-start(f32[24,1408]{1,0:T(8,128)} %get-tuple-element.8.info_ref) | copy-start | bytes 405508
  17.8 4.3 %collective-permute-start.2 = (f32[16,8,128]{2,1,0:T(8,128)S(1)}, f32[16,8,128]{2,1,0:T(8,128)S(1)}, u32[]{:S(2)}, u32[]{:S(2)}) collective-permute-start(f32[16,8,128]{2,1,0:T(8,128)S(1)} %get-tuple-element.13), channel_id=1, source_target_pairs={{0,1},{1,0},{2,3},{3,2},{4,5},{5,4},{6,7},{7,6},{8,9},{9,8},{10,11... | collective-permute-start | bytes 196616 | tf_op jit(solution)/shard_map/ppermute | solution.py:354
  22.2 1.3 %collective-permute-start.3 = (f32[8,8,128]{2,1,0:T(8,128)S(1)}, f32[8,8,128]{2,1,0:T(8,128)S(1)}, u32[]{:S(2)}, u32[]{:S(2)}) collective-permute-start(f32[8,8,128]{2,1,0:T(8,128)S(1)} %dynamic-slice_bitcast_fusion), channel_id=1, source_target_pairs={{0,2},{2,0},{4,6},{6,4},{8,10},{10,8},{12,14},{14,12},{16,18},{18,... | collective-permute-start | bytes 98312 | tf_op jit(solution)/shard_map/ppermute | solution.py:449
  23.4 3.9 %collective-permute-start.4 = (f32[8,8,128]{2,1,0:T(8,128)S(1)}, f32[8,8,128]{2,1,0:T(8,128)S(1)}, u32[]{:S(2)}, u32[]{:S(2)}) collective-permute-start(f32[8,8,128]{2,1,0:T(8,128)S(1)} %bitcast_add_fusion), channel_id=1, source_target_pairs={{0,4},{2,6},{4,0},{6,2},{8,12},{10,14},{12,8},{14,10},{16,20},{18,... | collective-permute-start | bytes 98312 | tf_op jit(solution)/shard_map/ppermute | solution.py:449
  25.2 4.1 %collective-permute-start.5 = (f32[8,8,128]{2,1,0:T(8,128)S(1)}, f32[8,8,128]{2,1,0:T(8,128)S(1)}, u32[]{:S(2)}, u32[]{:S(2)}) collective-permute-start(f32[8,8,128]{2,1,0:T(8,128)S(1)} %bitcast_add_fusion), channel_id=1, source_target_pairs={{0,8},{2,10},{4,12},{6,14},{8,0},{10,2},{12,4},{14,6},{16,24},{18,... | collective-permute-start | bytes 98312 | tf_op jit(solution)/shard_map/ppermute | solution.py:449
  26.8 4.8 %collective-permute-start.6 = (f32[8,8,128]{2,1,0:T(8,128)S(1)}, f32[8,8,128]{2,1,0:T(8,128)S(1)}, u32[]{:S(2)}, u32[]{:S(2)}) collective-permute-start(f32[8,8,128]{2,1,0:T(8,128)S(1)} %bitcast_add_fusion), channel_id=1, source_target_pairs={{0,12},{2,14},{4,8},{6,10},{8,4},{10,6},{12,0},{14,2},{16,28},{18,... | collective-permute-start | bytes 98312 | tf_op jit(solution)/shard_map/ppermute | solution.py:449
  31.6 5.1 %collective-permute-start.7 = (f32[8,8,128]{2,1,0:T(8,128)S(1)}, f32[8,8,128]{2,1,0:T(8,128)S(1)}, u32[]{:S(2)}, u32[]{:S(2)}) collective-permute-start(f32[8,8,128]{2,1,0:T(8,128)S(1)} %add_add_fusion), channel_id=1, source_target_pairs={{0,16},{2,18},{4,20},{6,22},{8,24},{10,26},{12,28},{14,30},{16,0},... | collective-permute-start | bytes 98312 | tf_op jit(solution)/shard_map/ppermute | solution.py:449
  36.7 1.2 %collective-permute-start.8 = (f32[8,8,128]{2,1,0:T(8,128)S(1)}, f32[8,8,128]{2,1,0:T(8,128)S(1)}, u32[]{:S(2)}, u32[]{:S(2)}) collective-permute-start(f32[8,8,128]{2,1,0:T(8,128)S(1)} %add.58.mine_ref), channel_id=1, source_target_pairs={{0,2},{2,0},{4,6},{6,4},{8,10},{10,8},{12,14},{14,12},{16,18},{18,... | collective-permute-start | bytes 98312 | tf_op jit(solution)/shard_map/ppermute | solution.py:449

commit v5 on v3

--- a/solution.py
+++ b/solution.py
@@ -179,17 +179,20 @@
     for at in range(rounds):
         river = jnp.minimum(at * seq_count + here, rivers - 1)
         info[at : at + 1, :hands] = rank_tmp[river].astype(jnp.float32)
-        live = jnp.where(low >= 0, 1.0, 0.0)
+        alive = jnp.where(at * seq_count + here < live_count, 1.0, 0.0)
+        live = jnp.where(low >= 0, alive, 0.0)
         for slot in range(board_tmp.shape[0]):
             card = board_tmp[slot, 0, river]
             live = jnp.where((low == card) | (high == card), 0.0, live)
         info[rounds + at : rounds + at + 1, :] = live
     info[base : base + 1, :] = 1.0 / (hands * jnp.full((1, padded), live_count.astype(jnp.float32)))
     live_rounds = lax.div(live_count - here + seq_count - 1, seq_count)
-    info[base + 1 : base + 2, :] = jnp.full((1, padded), live_rounds.astype(jnp.float32))
-    info[base + 2 : base + 3, :leaves] = parent
-    info[base + 3 : base + 4, :leaves] = pot
-    info[base + 4 : base + 4 + nodes, :hands] = reach
+    info[base + 3 + nodes : base + 4 + nodes, :] = jnp.full(
+        (1, padded), live_rounds.astype(jnp.float32)
+    )
+    info[base + 1 : base + 2, :leaves] = parent
+    info[base + 2 : base + 3, :leaves] = pot
+    info[base + 3 : base + 3 + nodes, :hands] = reach
     kept = pltpu.make_async_copy(info, info_ref, out_sems.at[1])
     kept.start()
     sent.wait()
@@ -246,9 +249,9 @@
     reach, places, pots = [], [], []
     for at in range(seq_count):
         if at == 0:
-            reach.append(info_ref[base + 4 : base + 4 + local_nodes, :hands])
-            parent = info_ref[base + 2 : base + 3, :LANES]
-            pots.append(info_ref[base + 3 : base + 4, :LANES])
+            reach.append(info_ref[base + 3 : base + 3 + local_nodes, :hands])
+            parent = info_ref[base + 1 : base + 2, :LANES]
+            pots.append(info_ref[base + 2 : base + 3, :LANES])
         else:
             small = smalls[at - 1][...].astype(jnp.float32)
             reach.append(small[:local_nodes])
@@ -284,25 +287,30 @@
     lookup = jnp.concatenate(reach * (leaves // nodes), axis=0)
 
     reach_all[...] = jnp.zeros_like(reach_all)
-    total[...] = jnp.zeros_like(total)
-    live_rounds = jnp.max(info_ref[base + 1 : base + 2, :LANES])
-    for at in range(rounds):
-
-        @pl.when(live_rounds > at)
-        def _():
+    live_rounds = jnp.max(info_ref[base + 3 + local_nodes : base + 4 + local_nodes, :LANES])
+
+    def sum_rounds(number):
+        gains = []
+        for at in range(number):
             rows = slice(at * local_leaves, (at + 1) * local_leaves)
             live = info_ref[rounds + at : rounds + at + 1, :]
             strat = jnp.dot(picks[0], own_ref[rows, :], preferred_element_type=jnp.float32)
             for pick, pack in zip(picks[1:], came):
                 strat = strat + jnp.dot(pick, pack[rows, :], preferred_element_type=jnp.float32)
-            reach_all[:, :hands] = (lookup * strat * live[:, :hands]).astype(jnp.bfloat16)
-            shown = jnp.dot(reach_all[...], payoff_ref[at], preferred_element_type=jnp.float32)
+            reach_all[at, :, :hands] = (lookup * strat * live[:, :hands]).astype(jnp.bfloat16)
+        for at in range(number):
+            live = info_ref[rounds + at : rounds + at + 1, :]
+            shown = jnp.dot(reach_all[at], payoff_ref[at], preferred_element_type=jnp.float32)
             value = shown * pot_sorted
             best = value[:nodes]
             for row in range(nodes, leaves, nodes):
                 best = jnp.maximum(best, value[row : row + nodes])
-            gain = best * (live * info_ref[base : base + 1, :])
-            total[...] += gain
+            gains.append(best * (live * info_ref[base : base + 1, :]))
+        total[...] = sum(gains[1:], gains[0])
+
+    total[...] = jnp.zeros_like(total)
+    for number in range(1, rounds + 1):
+        pl.when(live_rounds == number)(functools.partial(sum_rounds, number))
 
     short = round_up(local_nodes, 8) - local_nodes
     for step in range(seq_count):
@@ -439,7 +447,7 @@
         out_specs=[vmem] * seq_count,
         scratch_shapes=[
             pltpu.VMEM((nodes, padded), jnp.float32),
-            pltpu.VMEM((leaves, padded), jnp.bfloat16),
+            pltpu.VMEM((rounds, leaves, padded), jnp.bfloat16),
         ],
         compiler_params=params,
         name="value",

time: 38.7 us -> 37.7 us (0.974); the launches traced: 38.1 us -> 37.8 us
  starting transfers between devices: 12.3 us -> 9.9 us
  waiting for transfers between devices: 12.8 us -> 14.8 us
    ppermute x6, starting transfers between devices: 8.48 us -> 6.07 us  [swap(): lax.ppermute(array, 'board', [(at, at ^ step) for at in range(board_count)])]
    ppermute x6, waiting for transfers between devices: 7.33 us -> 9.36 us  [swap(): lax.ppermute(array, 'board', [(at, at ^ step) for at in range(board_count)])]
where the time goes in v5:
time: 37.7 us; the launch traced here: 37.8 us
  waiting for transfers between devices  14.8 us (39%)
  starting transfers between devices  9.9 us (26%)
  Pallas kernels  8.86 us (24%)
  local copies, waits for them, and re-layouts  2.1 us (6%)
  between operations  2.05 us (5%)
    ppermute x6, waiting for transfers between devices, swap(): lax.ppermute(array, 'board', [(at, at ^ step) for at in range(board_count)])  9.36 us
    ppermute x6, starting transfers between devices, swap(): lax.ppermute(array, 'board', [(at, at ^ step) for at in range(board_count)])  6.07 us
    ppermute x3, waiting for transfers between devices, shift(): lax.ppermute(array, 'seq', [(at, (at + step) % seq_count) for at in range...  5.47 us
    pallas_call x1, Pallas kernels, body(): pl.pallas_call(functools.partial(build_kernel, rounds), out_shape=[jax.Sh...  4.38 us
    ppermute x3, starting transfers between devices, shift(): lax.ppermute(array, 'seq', [(at, (at + step) % seq_count) for at in range...  3.83 us
    pallas_call x1, Pallas kernels, body(): pl.pallas_call(functools.partial(pack_kernel, rounds, seq_count), out_sha...  1.72 us
    pallas_call x1, Pallas kernels, body(): pl.pallas_call(functools.partial(value_kernel, rounds, seq_count, nodes,...  1.32 us
    dynamic_slice x1, local copies, waits for them, and re-layouts, strategy_for(): rows = lax.dynamic_slice_in_dim(split, owner, 1, axis=1)  1.19 us
  transfers between devices with their start and end apart: 9, of which 7 were waited for; matrix products, arithmetic and copies ran while one was open for 0% of the time, Pallas kernels for 18%

profile of v5, /device:TPU:0, one launch (start us, length us, event | category | flops | bytes accessed | tf_op | source)
XLA Modules:
  0.0 37.8 jit_solution(137926783181286176)
XLA Ops:
  0.7 1.2 %constant_dynamic-slice_fusion = (bf16[3,1,48,1326]{3,2,1,0:T(8,128)(2,1)S(1)}, bf16[3,1,48,1326]{3,2,1,0:T(8,128)(2,1)S(1)}) fusion(bf16[3,2,48,1326]{3,2,1,0:T(8,128)(2,1)} %bitcast.19, s32[]{:T(128)S(6)} %select_n.31, s32[]{:T(128)S(6)} %select_n.29), kind=kLoop, calls=%fused_computation.4 | loop fusion | bytes 1527560 | tf_op jit(solution)/shard_map/dynamic_slice | solution.py:373
  1.9 3.0 %collective-permute-start = (bf16[144,1326]{1,0:T(8,128)(2,1)S(1)}, bf16[144,1326]{1,0:T(8,128)(2,1)S(1)}, u32[]{:S(2)}, u32[]{:S(2)}) collective-permute-start(bf16[144,1326]{1,0:T(8,128)(2,1)S(1)} %bitcast.20), channel_id=1, source_target_pairs={{0,1},{1,0},{2,3},{3,2},{4,5},{5,4},{6,7},{7,6},{8,9},{9,8},{10,11... | collective-permute-start | bytes 1145672 | tf_op jit(solution)/shard_map/ppermute | solution.py:365
  5.5 1.7 %pack.1 = (bf16[16,1326]{1,0:T(8,128)(2,1)}, f32[24,1408]{1,0:T(8,128)}) custom-call(bf16[1,12,1326]{2,1,0:T(8,128)(2,1)} %reach_ref.1, s32[1,48]{1,0:T(1,128)} %bitcast.26, f32[1,48]{1,0:T(1,128)} %bitcast.27, s32[6,1,1326]{2,1,0:T(1,128)} %bitcast.24, s32[5,1,6]{2,1,0:T(1,128)} %bitcast.25, s32[1]{0:T(128)S(6)} %copy.14.count_ref), custom_call_target="tpu_custom_call" | custom-call | tf_op jit(solution)/shard_map/pack/pallas_call | solution.py:389
  7.2 0.1 collective-permute-start.1
  7.3 0.9 %copy-done = f32[24,1408]{1,0:T(8,128)S(1)} copy-done((f32[24,1408]{1,0:T(8,128)S(1)}, f32[24,1408]{1,0:T(8,128)}, u32[]{:S(2)}) %copy-start) | copy-done | bytes 135192
  8.2 4.4 %build.1 = (bf16[3,1408,1408]{2,1,0:T(8,128)(2,1)S(1)}, f32[24,1408]{1,0:T(8,128)S(1)}) custom-call(f32[24,1408]{1,0:T(8,128)S(1)} %copy-done), custom_call_target="tpu_custom_call" | custom-call | flops 59473920 | bytes 7929856 | tf_op jit(solution)/shard_map/build/pallas_call | solution.py:421
  12.6 2.6 %collective-permute-done.1.refs_4_ = bf16[16,1326]{1,0:T(8,128)(2,1)S(1)} collective-permute-done((bf16[16,1326]{1,0:T(8,128)(2,1)}, bf16[16,1326]{1,0:T(8,128)(2,1)S(1)}, u32[]{:S(2)}, u32[]{:S(2)}) %collective-permute-start.1) | collective-permute-done | bytes 42464 | tf_op jit(solution)/shard_map/ppermute | solution.py:365
  15.2 0.0 collective-permute-done.refs_3_
  15.2 1.3 %value.1 = (f32[16,8,128]{2,1,0:T(8,128)S(1)}, f32[16,8,128]{2,1,0:T(8,128)S(1)}) custom-call(bf16[3,1408,1408]{2,1,0:T(8,128)(2,1)S(1)} %get-tuple-element.9.refs_0_, f32[24,1408]{1,0:T(8,128)S(1)} %get-tuple-element.10.refs_1_, bf16[144,1326]{1,0:T(8,128)(2,1)S(1)} %bitcast.18, bf16[144,1326]{1,0:T(8,128)(2,1)S(1)} %collective-permute-done.refs_3_, ...), custom_call_target="tpu_custom_call" | custom-call | tf_op jit(solution)/shard_map/value/pallas_call | solution.py:443
  16.5 0.7 %collective-permute-start.2 = (f32[16,8,128]{2,1,0:T(8,128)S(1)}, f32[16,8,128]{2,1,0:T(8,128)S(1)}, u32[]{:S(2)}, u32[]{:S(2)}) collective-permute-start(f32[16,8,128]{2,1,0:T(8,128)S(1)} %get-tuple-element.13), channel_id=1, source_target_pairs={{0,1},{1,0},{2,3},{3,2},{4,5},{5,4},{6,7},{7,6},{8,9},{9,8},{10,11... | collective-permute-start | bytes 196616 | tf_op jit(solution)/shard_map/ppermute | solution.py:365
  17.9 2.9 %collective-permute-done.2 = f32[16,8,128]{2,1,0:T(8,128)S(1)} collective-permute-done((f32[16,8,128]{2,1,0:T(8,128)S(1)}, f32[16,8,128]{2,1,0:T(8,128)S(1)}, u32[]{:S(2)}, u32[]{:S(2)}) %collective-permute-start.2) | collective-permute-done | bytes 65568 | tf_op jit(solution)/shard_map/ppermute | solution.py:365
  20.8 0.1 collective-permute-start.3
  20.9 1.2 %collective-permute-done.3 = f32[8,8,128]{2,1,0:T(8,128)S(1)} collective-permute-done((f32[8,8,128]{2,1,0:T(8,128)S(1)}, f32[8,8,128]{2,1,0:T(8,128)S(1)}, u32[]{:S(2)}, u32[]{:S(2)}) %collective-permute-start.3) | collective-permute-done | bytes 32800 | tf_op jit(solution)/shard_map/ppermute | solution.py:460
  22.1 1.9 %collective-permute-start.4 = (f32[8,8,128]{2,1,0:T(8,128)S(1)}, f32[8,8,128]{2,1,0:T(8,128)S(1)}, u32[]{:S(2)}, u32[]{:S(2)}) collective-permute-start(f32[8,8,128]{2,1,0:T(8,128)S(1)} %bitcast_add_fusion), channel_id=1, source_target_pairs={{0,4},{2,6},{4,0},{6,2},{8,12},{10,14},{12,8},{14,10},{16,20},{18,... | collective-permute-start | bytes 98312 | tf_op jit(solution)/shard_map/ppermute | solution.py:460
  24.0 2.1 %collective-permute-start.5 = (f32[8,8,128]{2,1,0:T(8,128)S(1)}, f32[8,8,128]{2,1,0:T(8,128)S(1)}, u32[]{:S(2)}, u32[]{:S(2)}) collective-permute-start(f32[8,8,128]{2,1,0:T(8,128)S(1)} %bitcast_add_fusion), channel_id=1, source_target_pairs={{0,8},{2,10},{4,12},{6,14},{8,0},{10,2},{12,4},{14,6},{16,24},{18,... | collective-permute-start | bytes 98312 | tf_op jit(solution)/shard_map/ppermute | solution.py:460
  26.1 0.0 collective-permute-start.6
  26.1 0.0 collective-permute-done.4
  26.1 1.9 %collective-permute-done.5 = f32[8,8,128]{2,1,0:T(8,128)S(1)} collective-permute-done((f32[8,8,128]{2,1,0:T(8,128)S(1)}, f32[8,8,128]{2,1,0:T(8,128)S(1)}, u32[]{:S(2)}, u32[]{:S(2)}) %collective-permute-start.5) | collective-permute-done | bytes 32800 | tf_op jit(solution)/shard_map/ppermute | solution.py:460
  28.0 2.9 %collective-permute-done.6 = f32[8,8,128]{2,1,0:T(8,128)S(1)} collective-permute-done((f32[8,8,128]{2,1,0:T(8,128)S(1)}, f32[8,8,128]{2,1,0:T(8,128)S(1)}, u32[]{:S(2)}, u32[]{:S(2)}) %collective-permute-start.6) | collective-permute-done | bytes 32800 | tf_op jit(solution)/shard_map/ppermute | solution.py:460
  31.0 2.0 %collective-permute-start.7 = (f32[8,8,128]{2,1,0:T(8,128)S(1)}, f32[8,8,128]{2,1,0:T(8,128)S(1)}, u32[]{:S(2)}, u32[]{:S(2)}) collective-permute-start(f32[8,8,128]{2,1,0:T(8,128)S(1)} %add_add_fusion), channel_id=1, source_target_pairs={{0,16},{2,18},{4,20},{6,22},{8,24},{10,26},{12,28},{14,30},{16,0},... | collective-permute-start | bytes 98312 | tf_op jit(solution)/shard_map/ppermute | solution.py:460
  33.0 2.9 %collective-permute-done.7 = f32[8,8,128]{2,1,0:T(8,128)S(1)} collective-permute-done((f32[8,8,128]{2,1,0:T(8,128)S(1)}, f32[8,8,128]{2,1,0:T(8,128)S(1)}, u32[]{:S(2)}, u32[]{:S(2)}) %collective-permute-start.7) | collective-permute-done | bytes 32800 | tf_op jit(solution)/shard_map/ppermute | solution.py:460
  35.9 0.7 %share.1 = f32[12,1,1326]{2,1,0:T(1,128)} custom-call(f32[16,8,128]{2,1,0:T(8,128)S(1)} %get-tuple-element.15.tiles_ref), custom_call_target="tpu_custom_call" | custom-call | tf_op jit(solution)/shard_map/share/pallas_call | solution.py:481
  36.6 0.5 %collective-permute-done.8.other_ref = f32[8,8,128]{2,1,0:T(8,128)S(1)} collective-permute-done((f32[8,8,128]{2,1,0:T(8,128)S(1)}, f32[8,8,128]{2,1,0:T(8,128)S(1)}, u32[]{:S(2)}, u32[]{:S(2)}) %collective-permute-start.8) | collective-permute-done | bytes 32800 | tf_op jit(solution)/shard_map/ppermute | solution.py:460
  37.1 0.7 %root.1 = f32[12,1326]{1,0:T(8,128)} custom-call(f32[8,8,128]{2,1,0:T(8,128)S(1)} %add.58.mine_ref, f32[8,8,128]{2,1,0:T(8,128)S(1)} %collective-permute-done.8.other_ref), custom_call_target="tpu_custom_call" | custom-call | tf_op jit(solution)/shard_map/root/pallas_call | solution.py:493
  (7 shorter events, 0.0 us)
Async XLA Ops:
  1.9 13.4 %collective-permute-start = (bf16[144,1326]{1,0:T(8,128)(2,1)S(1)}, bf16[144,1326]{1,0:T(8,128)(2,1)S(1)}, u32[]{:S(2)}, u32[]{:S(2)}) collective-permute-start(bf16[144,1326]{1,0:T(8,128)(2,1)S(1)} %bitcast.20), channel_id=1, source_target_pairs={{0,1},{1,0},{2,3},{3,2},{4,5},{5,4},{6,7},{7,6},{8,9},{9,8},{10,11... | collective-permute-start | bytes 1145672 | tf_op jit(solution)/shard_map/ppermute | solution.py:365
  7.2 8.0 %collective-permute-start.1 = (bf16[16,1326]{1,0:T(8,128)(2,1)}, bf16[16,1326]{1,0:T(8,128)(2,1)S(1)}, u32[]{:S(2)}, u32[]{:S(2)}) collective-permute-start(bf16[16,1326]{1,0:T(8,128)(2,1)} %get-tuple-element.11), channel_id=1, source_target_pairs={{0,1},{1,0},{2,3},{3,2},{4,5},{5,4},{6,7},{7,6},{8,9},{9,8},{10,11... | collective-permute-start | bytes 127304 | tf_op jit(solution)/shard_map/ppermute | solution.py:365
  7.3 0.9 %copy-start = (f32[24,1408]{1,0:T(8,128)S(1)}, f32[24,1408]{1,0:T(8,128)}, u32[]{:S(2)}) copy-start(f32[24,1408]{1,0:T(8,128)} %get-tuple-element.8.info_ref) | copy-start | bytes 405508
  16.5 4.3 %collective-permute-start.2 = (f32[16,8,128]{2,1,0:T(8,128)S(1)}, f32[16,8,128]{2,1,0:T(8,128)S(1)}, u32[]{:S(2)}, u32[]{:S(2)}) collective-permute-start(f32[16,8,128]{2,1,0:T(8,128)S(1)} %get-tuple-element.13), channel_id=1, source_target_pairs={{0,1},{1,0},{2,3},{3,2},{4,5},{5,4},{6,7},{7,6},{8,9},{9,8},{10,11... | collective-permute-start | bytes 196616 | tf_op jit(solution)/shard_map/ppermute | solution.py:365
  20.8 1.3 %collective-permute-start.3 = (f32[8,8,128]{2,1,0:T(8,128)S(1)}, f32[8,8,128]{2,1,0:T(8,128)S(1)}, u32[]{:S(2)}, u32[]{:S(2)}) collective-permute-start(f32[8,8,128]{2,1,0:T(8,128)S(1)} %dynamic-slice_bitcast_fusion), channel_id=1, source_target_pairs={{0,2},{2,0},{4,6},{6,4},{8,10},{10,8},{12,14},{14,12},{16,18},{18,... | collective-permute-start | bytes 98312 | tf_op jit(solution)/shard_map/ppermute | solution.py:460
  22.1 4.0 %collective-permute-start.4 = (f32[8,8,128]{2,1,0:T(8,128)S(1)}, f32[8,8,128]{2,1,0:T(8,128)S(1)}, u32[]{:S(2)}, u32[]{:S(2)}) collective-permute-start(f32[8,8,128]{2,1,0:T(8,128)S(1)} %bitcast_add_fusion), channel_id=1, source_target_pairs={{0,4},{2,6},{4,0},{6,2},{8,12},{10,14},{12,8},{14,10},{16,20},{18,... | collective-permute-start | bytes 98312 | tf_op jit(solution)/shard_map/ppermute | solution.py:460
  24.0 4.0 %collective-permute-start.5 = (f32[8,8,128]{2,1,0:T(8,128)S(1)}, f32[8,8,128]{2,1,0:T(8,128)S(1)}, u32[]{:S(2)}, u32[]{:S(2)}) collective-permute-start(f32[8,8,128]{2,1,0:T(8,128)S(1)} %bitcast_add_fusion), channel_id=1, source_target_pairs={{0,8},{2,10},{4,12},{6,14},{8,0},{10,2},{12,4},{14,6},{16,24},{18,... | collective-permute-start | bytes 98312 | tf_op jit(solution)/shard_map/ppermute | solution.py:460
  26.1 4.8 %collective-permute-start.6 = (f32[8,8,128]{2,1,0:T(8,128)S(1)}, f32[8,8,128]{2,1,0:T(8,128)S(1)}, u32[]{:S(2)}, u32[]{:S(2)}) collective-permute-start(f32[8,8,128]{2,1,0:T(8,128)S(1)} %bitcast_add_fusion), channel_id=1, source_target_pairs={{0,12},{2,14},{4,8},{6,10},{8,4},{10,6},{12,0},{14,2},{16,28},{18,... | collective-permute-start | bytes 98312 | tf_op jit(solution)/shard_map/ppermute | solution.py:460
  31.0 4.9 %collective-permute-start.7 = (f32[8,8,128]{2,1,0:T(8,128)S(1)}, f32[8,8,128]{2,1,0:T(8,128)S(1)}, u32[]{:S(2)}, u32[]{:S(2)}) collective-permute-start(f32[8,8,128]{2,1,0:T(8,128)S(1)} %add_add_fusion), channel_id=1, source_target_pairs={{0,16},{2,18},{4,20},{6,22},{8,24},{10,26},{12,28},{14,30},{16,0},... | collective-permute-start | bytes 98312 | tf_op jit(solution)/shard_map/ppermute | solution.py:460
  35.8 1.2 %collective-permute-start.8 = (f32[8,8,128]{2,1,0:T(8,128)S(1)}, f32[8,8,128]{2,1,0:T(8,128)S(1)}, u32[]{:S(2)}, u32[]{:S(2)}) collective-permute-start(f32[8,8,128]{2,1,0:T(8,128)S(1)} %add.58.mine_ref), channel_id=1, source_target_pairs={{0,2},{2,0},{4,6},{6,4},{8,10},{10,8},{12,14},{14,12},{16,18},{18,... | collective-permute-start | bytes 98312 | tf_op jit(solution)/shard_map/ppermute | solution.py:460

commit v6 on v5

--- a/solution.py
+++ b/solution.py
@@ -235,11 +235,11 @@
                 payoff_ref[at, rows, here] = jnp.maximum(jnp.minimum(gap, mask), -mask)
 
 
-def value_kernel(rounds, seq_count, nodes, leaves, *refs):
+def head_kernel(rounds, seq_count, nodes, leaves, *refs):
     payoff_ref, info_ref, own_ref = refs[:3]
     came = refs[3 : 2 + seq_count]
     smalls = refs[2 + seq_count : 1 + 2 * seq_count]
-    outs, (total, reach_all) = refs[1 + 2 * seq_count : -2], refs[-2:]
+    total, picks_ref, pot_ref, lookup_ref, reach_all = refs[1 + 2 * seq_count :]
     hands = own_ref.shape[-1]
     padded = payoff_ref.shape[-1]
     local_leaves, local_nodes = leaves // seq_count, nodes // seq_count
@@ -283,8 +283,11 @@
         slot = jnp.where(places[at] >= 0.0, nth * nodes + places[at], -1.0)
         pick = jnp.where(target == slot, 1.0, 0.0)
         pot_sorted = pot_sorted + jnp.sum(pick * pots[at], axis=1, keepdims=True)
-        picks.append(pick.astype(jnp.bfloat16)[:, :local_leaves])
+        picks_ref[at] = pick.astype(jnp.bfloat16)
+        picks.append(picks_ref[at, :, :local_leaves])
     lookup = jnp.concatenate(reach * (leaves // nodes), axis=0)
+    lookup_ref[...] = lookup
+    pot_ref[...] = jnp.broadcast_to(pot_sorted, pot_ref.shape)
 
     reach_all[...] = jnp.zeros_like(reach_all)
     live_rounds = jnp.max(info_ref[base + 3 + local_nodes : base + 4 + local_nodes, :LANES])
@@ -309,8 +312,42 @@
         total[...] = sum(gains[1:], gains[0])
 
     total[...] = jnp.zeros_like(total)
-    for number in range(1, rounds + 1):
+    for number in range(1, rounds - 1):
         pl.when(live_rounds == number)(functools.partial(sum_rounds, number))
+    if rounds > 1:
+        pl.when(live_rounds >= rounds - 1)(functools.partial(sum_rounds, rounds - 1))
+
+
+def tail_kernel(rounds, seq_count, nodes, *refs):
+    payoff_ref, info_ref, own_ref = refs[:3]
+    came = refs[3 : 2 + seq_count]
+    before_ref, picks_ref, pot_ref, lookup_ref = refs[2 + seq_count : 6 + seq_count]
+    outs, (total, reach_all) = refs[6 + seq_count : -2], refs[-2:]
+    hands = own_ref.shape[-1]
+    padded = payoff_ref.shape[-1]
+    leaves = lookup_ref.shape[0]
+    local_leaves, local_nodes = leaves // seq_count, nodes // seq_count
+    base = 2 * rounds
+    last = rounds - 1
+    live_rounds = jnp.max(info_ref[base + 3 + local_nodes : base + 4 + local_nodes, :LANES])
+    total[...] = before_ref[...]
+
+    @pl.when(live_rounds > last)
+    def _():
+        reach_all[...] = jnp.zeros_like(reach_all)
+        live = info_ref[rounds + last : rounds + last + 1, :]
+        own = own_ref[last * local_leaves : rounds * local_leaves, :]
+        strat = jnp.dot(picks_ref[0, :, :local_leaves], own, preferred_element_type=jnp.float32)
+        for at, block in enumerate(came, 1):
+            pick = picks_ref[at, :, :local_leaves]
+            strat = strat + jnp.dot(pick, block[...], preferred_element_type=jnp.float32)
+        reach_all[:, :hands] = (lookup_ref[...] * strat * live[:, :hands]).astype(jnp.bfloat16)
+        shown = jnp.dot(reach_all[...], payoff_ref[last], preferred_element_type=jnp.float32)
+        value = shown * pot_ref[:, :1]
+        best = value[:nodes]
+        for row in range(nodes, leaves, nodes):
+            best = jnp.maximum(best, value[row : row + nodes])
+        total[...] += best * (live * info_ref[base : base + 1, :])
 
     short = round_up(local_nodes, 8) - local_nodes
     for step in range(seq_count):
@@ -382,7 +419,10 @@
         return rows.reshape(rounds * local_leaves, hands)
 
     own = strategy_for(0)
-    came = [shift(strategy_for(step), step) for step in range(1, seq_count)]
+    last = rounds - 1
+    sent = [strategy_for(step) for step in range(1, seq_count)]
+    own, *sent = lax.optimization_barrier((own, *sent))
+    came_head = [shift(rows[: last * local_leaves], step) for step, rows in enumerate(sent, 1)]
 
     small_rows = round_up(local_nodes + 4, 16)
     info_rows = round_up(2 * rounds + 4 + local_nodes, 8)
@@ -417,6 +457,8 @@
         river_count,
     )
     smalls = [shift(small, step) for step in range(1, seq_count)]
+    *sent, info = lax.optimization_barrier((*sent, info))
+    came_tail = [shift(rows[last * local_leaves :], step) for step, rows in enumerate(sent, 1)]
 
     payoff, info = pl.pallas_call(
         functools.partial(build_kernel, rounds),
@@ -440,18 +482,35 @@
     )(info)
 
     count = tile_count(local_nodes, hands)
+    total, *labels = pl.pallas_call(
+        functools.partial(head_kernel, rounds, seq_count, nodes, leaves),
+        out_shape=[
+            jax.ShapeDtypeStruct((nodes, padded), jnp.float32),
+            jax.ShapeDtypeStruct((seq_count, leaves, LANES), jnp.bfloat16),
+            jax.ShapeDtypeStruct((leaves, LANES), jnp.float32),
+            jax.ShapeDtypeStruct((leaves, hands), jnp.float32),
+        ],
+        in_specs=[vmem] * (1 + 2 * seq_count),
+        out_specs=[vmem] * 4,
+        scratch_shapes=[pltpu.VMEM((max(last, 1), leaves, padded), jnp.bfloat16)],
+        compiler_params=params,
+        cost_estimate=pl.CostEstimate(
+            flops=2 * rounds * leaves * padded * padded, bytes_accessed=2 * rounds * padded * padded, transcendentals=0
+        ),
+        name="head",
+    )(payoff, info, own, *came_head, *smalls)
     shares = pl.pallas_call(
-        functools.partial(value_kernel, rounds, seq_count, nodes, leaves),
+        functools.partial(tail_kernel, rounds, seq_count, nodes),
         out_shape=[jax.ShapeDtypeStruct((count, 8, LANES), jnp.float32)] * seq_count,
-        in_specs=[vmem] * (1 + 2 * seq_count),
+        in_specs=[vmem] * (6 + seq_count),
         out_specs=[vmem] * seq_count,
         scratch_shapes=[
             pltpu.VMEM((nodes, padded), jnp.float32),
-            pltpu.VMEM((rounds, leaves, padded), jnp.bfloat16),
+            pltpu.VMEM((leaves, padded), jnp.bfloat16),
         ],
         compiler_params=params,
-        name="value",
-    )(payoff, info, own, *came, *smalls)
+        name="tail",
+    )(payoff, info, own, *came_tail, total, *labels)
 
     share = shares[0]
     for step in range(1, seq_count):

time: 37.7 us -> 37.5 us (level)
  waiting for transfers between devices: 14.8 us -> 12.2 us
  starting transfers between devices: 9.9 us -> 11.8 us
    ppermute x3 -> x4, waiting for transfers between devices: 5.47 us -> 2.68 us  [shift(): lax.ppermute(array, 'seq', [(at, (at + step) % seq_count) for at in range...]
    ppermute x3 -> x4, starting transfers between devices: 3.83 us -> 6.09 us  [shift(): lax.ppermute(array, 'seq', [(at, (at + step) % seq_count) for at in range...]
    pallas_call x1 -> x2, Pallas kernels: 1.32 us -> 1.47 us  [the longest x1 1.27 us: body(): pl.pallas_call(functools.partial(head_kernel, rounds, seq_count, nodes, l...]
  transfers between devices with their start and end apart: 9 -> 10, of which waited for: 7 -> 6; matrix products, arithmetic and copies ran while one was open for 0% -> 0% of each run, Pallas kernels for 18% -> 22%
where the time goes in v6:
time: 37.5 us; the launch traced here: 37.3 us
  waiting for transfers between devices  12.2 us (33%)
  starting transfers between devices  11.8 us (31%)
  Pallas kernels  9 us (24%)
  local copies, waits for them, and re-layouts  2.15 us (6%)
  between operations  2.09 us (6%)
    ppermute x6, waiting for transfers between devices, swap(): lax.ppermute(array, 'board', [(at, at ^ step) for at in range(board_count)])  9.53 us
    ppermute x4, starting transfers between devices, shift(): lax.ppermute(array, 'seq', [(at, (at + step) % seq_count) for at in range...  6.09 us
    ppermute x6, starting transfers between devices, swap(): lax.ppermute(array, 'board', [(at, at ^ step) for at in range(board_count)])  5.7 us
    pallas_call x1, Pallas kernels, body(): pl.pallas_call(functools.partial(build_kernel, rounds), out_shape=[jax.Sh...  4.38 us
    ppermute x4, waiting for transfers between devices, shift(): lax.ppermute(array, 'seq', [(at, (at + step) % seq_count) for at in range...  2.68 us
    pallas_call x1, Pallas kernels, body(): pl.pallas_call(functools.partial(pack_kernel, rounds, seq_count), out_sha...  1.71 us
    pallas_call x1, Pallas kernels, body(): pl.pallas_call(functools.partial(head_kernel, rounds, seq_count, nodes, l...  1.27 us
    dynamic_slice x1, local copies, waits for them, and re-layouts, strategy_for(): rows = lax.dynamic_slice_in_dim(split, owner, 1, axis=1)  1.19 us
  transfers between devices with their start and end apart: 10, of which 6 were waited for; matrix products, arithmetic and copies ran while one was open for 0% of the time, Pallas kernels for 22%

profile of v6, /device:TPU:0, one launch (start us, length us, event | category | flops | bytes accessed | tf_op | source)
XLA Modules:
  0.0 37.3 jit_solution(9117200043105272846)
XLA Ops:
  0.7 1.2 %constant_dynamic-slice_fusion = (bf16[3,1,48,1326]{3,2,1,0:T(8,128)(2,1)S(1)}, bf16[3,1,48,1326]{3,2,1,0:T(8,128)(2,1)S(1)}) fusion(bf16[3,2,48,1326]{3,2,1,0:T(8,128)(2,1)} %bitcast.22, s32[]{:T(128)S(6)} %select_n.31, s32[]{:T(128)S(6)} %select_n.29), kind=kLoop, calls=%fused_computation.4 | loop fusion | bytes 1527560 | tf_op jit(solution)/shard_map/dynamic_slice | solution.py:410
  1.9 3.0 %collective-permute-start.1 = (bf16[96,1326]{1,0:T(8,128)(2,1)S(1)}, bf16[96,1326]{1,0:T(8,128)(2,1)S(1)}, u32[]{:S(2)}, u32[]{:S(2)}) collective-permute-start(bf16[96,1326]{1,0:T(8,128)(2,1)S(1)} %slice.7), channel_id=1, source_target_pairs={{0,1},{1,0},{2,3},{3,2},{4,5},{5,4},{6,7},{7,6},{8,9},{9,8},{10,11... | collective-permute-start | bytes 763784 | tf_op jit(solution)/shard_map/ppermute | solution.py:402
  5.5 1.7 %pack.1 = (bf16[16,1326]{1,0:T(8,128)(2,1)}, f32[24,1408]{1,0:T(8,128)}) custom-call(bf16[1,12,1326]{2,1,0:T(8,128)(2,1)} %reach_ref.1, s32[1,48]{1,0:T(1,128)} %bitcast.28, f32[1,48]{1,0:T(1,128)} %bitcast.29, s32[6,1,1326]{2,1,0:T(1,128)} %bitcast.26, s32[5,1,6]{2,1,0:T(1,128)} %bitcast.27, s32[1]{0:T(128)S(6)} %copy.14.count_ref), custom_call_target="tpu_custom_call" | custom-call | tf_op jit(solution)/shard_map/pack/pallas_call | solution.py:429
  7.3 0.1 collective-permute-start.2
  7.4 2.1 %collective-permute-start = (bf16[48,1326]{1,0:T(8,128)(2,1)S(1)}, bf16[48,1326]{1,0:T(8,128)(2,1)S(1)}, u32[]{:S(2)}, u32[]{:S(2)}) collective-permute-start(bf16[48,1326]{1,0:T(8,128)(2,1)S(1)} %slice.6), channel_id=1, source_target_pairs={{0,1},{1,0},{2,3},{3,2},{4,5},{5,4},{6,7},{7,6},{8,9},{9,8},{10,11... | collective-permute-start | bytes 381896 | tf_op jit(solution)/shard_map/ppermute | solution.py:402
  9.4 0.9 %copy-done = f32[24,1408]{1,0:T(8,128)S(1)} copy-done((f32[24,1408]{1,0:T(8,128)S(1)}, f32[24,1408]{1,0:T(8,128)}, u32[]{:S(2)}) %copy-start) | copy-done | bytes 135192
  10.3 4.4 %build.1 = (bf16[3,1408,1408]{2,1,0:T(8,128)(2,1)S(1)}, f32[24,1408]{1,0:T(8,128)S(1)}) custom-call(f32[24,1408]{1,0:T(8,128)S(1)} %copy-done), custom_call_target="tpu_custom_call" | custom-call | flops 59473920 | bytes 7929856 | tf_op jit(solution)/shard_map/build/pallas_call | solution.py:463
  14.7 0.0 collective-permute-done.2.refs_4_
  14.7 0.0 collective-permute-done.1.refs_3_
  14.7 1.3 %head.1 = (f32[24,1408]{1,0:T(8,128)S(1)}, bf16[2,96,128]{2,1,0:T(8,128)(2,1)S(1)}, f32[96,128]{1,0:T(8,128)S(1)}, f32[96,1326]{1,0:T(8,128)S(1)}) custom-call(bf16[3,1408,1408]{2,1,0:T(8,128)(2,1)S(1)} %get-tuple-element.19.refs_0_, f32[24,1408]{1,0:T(8,128)S(1)} %get-tuple-element.20.refs_1_, bf16[144,1326]{1,0:T(8,128)(2,1)S(1)} %bitcast.18, ...), custom_call_target="tpu_custom_call" | custom-call | flops 1141899264 | bytes 11894784 | tf_op jit(solution)/shard_map/head/pallas_call | solution.py:485
  16.0 0.2 tail.1
  16.2 0.9 %collective-permute-start.3 = (f32[16,8,128]{2,1,0:T(8,128)S(1)}, f32[16,8,128]{2,1,0:T(8,128)S(1)}, u32[]{:S(2)}, u32[]{:S(2)}) collective-permute-start(f32[16,8,128]{2,1,0:T(8,128)S(1)} %get-tuple-element.29), channel_id=1, source_target_pairs={{0,1},{1,0},{2,3},{3,2},{4,5},{5,4},{6,7},{7,6},{8,9},{9,8},{10,11... | collective-permute-start | bytes 196616 | tf_op jit(solution)/shard_map/ppermute | solution.py:402
  17.8 2.7 %collective-permute-done.3 = f32[16,8,128]{2,1,0:T(8,128)S(1)} collective-permute-done((f32[16,8,128]{2,1,0:T(8,128)S(1)}, f32[16,8,128]{2,1,0:T(8,128)S(1)}, u32[]{:S(2)}, u32[]{:S(2)}) %collective-permute-start.3) | collective-permute-done | bytes 65568 | tf_op jit(solution)/shard_map/ppermute | solution.py:402
  20.5 0.1 collective-permute-start.4
  20.6 1.2 %collective-permute-done.4 = f32[8,8,128]{2,1,0:T(8,128)S(1)} collective-permute-done((f32[8,8,128]{2,1,0:T(8,128)S(1)}, f32[8,8,128]{2,1,0:T(8,128)S(1)}, u32[]{:S(2)}, u32[]{:S(2)}) %collective-permute-start.4) | collective-permute-done | bytes 32800 | tf_op jit(solution)/shard_map/ppermute | solution.py:519
  21.8 1.6 %collective-permute-start.6 = (f32[8,8,128]{2,1,0:T(8,128)S(1)}, f32[8,8,128]{2,1,0:T(8,128)S(1)}, u32[]{:S(2)}, u32[]{:S(2)}) collective-permute-start(f32[8,8,128]{2,1,0:T(8,128)S(1)} %bitcast_add_fusion), channel_id=1, source_target_pairs={{0,8},{2,10},{4,12},{6,14},{8,0},{10,2},{12,4},{14,6},{16,24},{18,... | collective-permute-start | bytes 98312 | tf_op jit(solution)/shard_map/ppermute | solution.py:519
  23.4 3.0 %collective-permute-start.7 = (f32[8,8,128]{2,1,0:T(8,128)S(1)}, f32[8,8,128]{2,1,0:T(8,128)S(1)}, u32[]{:S(2)}, u32[]{:S(2)}) collective-permute-start(f32[8,8,128]{2,1,0:T(8,128)S(1)} %bitcast_add_fusion), channel_id=1, source_target_pairs={{0,12},{2,14},{4,8},{6,10},{8,4},{10,6},{12,0},{14,2},{16,28},{18,... | collective-permute-start | bytes 98312 | tf_op jit(solution)/shard_map/ppermute | solution.py:519
  26.4 2.2 %collective-permute-done.7 = f32[8,8,128]{2,1,0:T(8,128)S(1)} collective-permute-done((f32[8,8,128]{2,1,0:T(8,128)S(1)}, f32[8,8,128]{2,1,0:T(8,128)S(1)}, u32[]{:S(2)}, u32[]{:S(2)}) %collective-permute-start.7) | collective-permute-done | bytes 32800 | tf_op jit(solution)/shard_map/ppermute | solution.py:519
  28.7 1.7 %collective-permute-done.5 = f32[8,8,128]{2,1,0:T(8,128)S(1)} collective-permute-done((f32[8,8,128]{2,1,0:T(8,128)S(1)}, f32[8,8,128]{2,1,0:T(8,128)S(1)}, u32[]{:S(2)}, u32[]{:S(2)}) %collective-permute-start.5) | collective-permute-done | bytes 32800 | tf_op jit(solution)/shard_map/ppermute | solution.py:519
  30.4 1.0 %collective-permute-start.8 = (f32[8,8,128]{2,1,0:T(8,128)S(1)}, f32[8,8,128]{2,1,0:T(8,128)S(1)}, u32[]{:S(2)}, u32[]{:S(2)}) collective-permute-start(f32[8,8,128]{2,1,0:T(8,128)S(1)} %add_add_fusion), channel_id=1, source_target_pairs={{0,16},{2,18},{4,20},{6,22},{8,24},{10,26},{12,28},{14,30},{16,0},... | collective-permute-start | bytes 98312 | tf_op jit(solution)/shard_map/ppermute | solution.py:519
  31.4 4.0 %collective-permute-done.8 = f32[8,8,128]{2,1,0:T(8,128)S(1)} collective-permute-done((f32[8,8,128]{2,1,0:T(8,128)S(1)}, f32[8,8,128]{2,1,0:T(8,128)S(1)}, u32[]{:S(2)}, u32[]{:S(2)}) %collective-permute-start.8) | collective-permute-done | bytes 32800 | tf_op jit(solution)/shard_map/ppermute | solution.py:519
  35.4 0.7 %share.1 = f32[12,1,1326]{2,1,0:T(1,128)} custom-call(f32[16,8,128]{2,1,0:T(8,128)S(1)} %get-tuple-element.31.tiles_ref), custom_call_target="tpu_custom_call" | custom-call | tf_op jit(solution)/shard_map/share/pallas_call | solution.py:540
  36.1 0.5 %collective-permute-done.9.other_ref = f32[8,8,128]{2,1,0:T(8,128)S(1)} collective-permute-done((f32[8,8,128]{2,1,0:T(8,128)S(1)}, f32[8,8,128]{2,1,0:T(8,128)S(1)}, u32[]{:S(2)}, u32[]{:S(2)}) %collective-permute-start.9) | collective-permute-done | bytes 32800 | tf_op jit(solution)/shard_map/ppermute | solution.py:519
  36.5 0.7 %root.1 = f32[12,1326]{1,0:T(8,128)} custom-call(f32[8,8,128]{2,1,0:T(8,128)S(1)} %add.58.mine_ref, f32[8,8,128]{2,1,0:T(8,128)S(1)} %collective-permute-done.9.other_ref), custom_call_target="tpu_custom_call" | custom-call | tf_op jit(solution)/shard_map/root/pallas_call | solution.py:552
  (12 shorter events, 0.1 us)
Async XLA Ops:
  1.9 12.9 %collective-permute-start.1 = (bf16[96,1326]{1,0:T(8,128)(2,1)S(1)}, bf16[96,1326]{1,0:T(8,128)(2,1)S(1)}, u32[]{:S(2)}, u32[]{:S(2)}) collective-permute-start(bf16[96,1326]{1,0:T(8,128)(2,1)S(1)} %slice.7), channel_id=1, source_target_pairs={{0,1},{1,0},{2,3},{3,2},{4,5},{5,4},{6,7},{7,6},{8,9},{9,8},{10,11... | collective-permute-start | bytes 763784 | tf_op jit(solution)/shard_map/ppermute | solution.py:402
  7.3 7.5 %collective-permute-start.2 = (bf16[16,1326]{1,0:T(8,128)(2,1)}, bf16[16,1326]{1,0:T(8,128)(2,1)S(1)}, u32[]{:S(2)}, u32[]{:S(2)}) collective-permute-start(bf16[16,1326]{1,0:T(8,128)(2,1)} %get-tuple-element.23), channel_id=1, source_target_pairs={{0,1},{1,0},{2,3},{3,2},{4,5},{5,4},{6,7},{7,6},{8,9},{9,8},{10,11... | collective-permute-start | bytes 127304 | tf_op jit(solution)/shard_map/ppermute | solution.py:402
  7.4 8.7 %collective-permute-start = (bf16[48,1326]{1,0:T(8,128)(2,1)S(1)}, bf16[48,1326]{1,0:T(8,128)(2,1)S(1)}, u32[]{:S(2)}, u32[]{:S(2)}) collective-permute-start(bf16[48,1326]{1,0:T(8,128)(2,1)S(1)} %slice.6), channel_id=1, source_target_pairs={{0,1},{1,0},{2,3},{3,2},{4,5},{5,4},{6,7},{7,6},{8,9},{9,8},{10,11... | collective-permute-start | bytes 381896 | tf_op jit(solution)/shard_map/ppermute | solution.py:402
  9.4 0.9 %copy-start = (f32[24,1408]{1,0:T(8,128)S(1)}, f32[24,1408]{1,0:T(8,128)}, u32[]{:S(2)}) copy-start(f32[24,1408]{1,0:T(8,128)} %get-tuple-element.18.info_ref) | copy-start | bytes 405508
  16.2 4.3 %collective-permute-start.3 = (f32[16,8,128]{2,1,0:T(8,128)S(1)}, f32[16,8,128]{2,1,0:T(8,128)S(1)}, u32[]{:S(2)}, u32[]{:S(2)}) collective-permute-start(f32[16,8,128]{2,1,0:T(8,128)S(1)} %get-tuple-element.29), channel_id=1, source_target_pairs={{0,1},{1,0},{2,3},{3,2},{4,5},{5,4},{6,7},{7,6},{8,9},{9,8},{10,11... | collective-permute-start | bytes 196616 | tf_op jit(solution)/shard_map/ppermute | solution.py:402
  20.5 1.3 %collective-permute-start.4 = (f32[8,8,128]{2,1,0:T(8,128)S(1)}, f32[8,8,128]{2,1,0:T(8,128)S(1)}, u32[]{:S(2)}, u32[]{:S(2)}) collective-permute-start(f32[8,8,128]{2,1,0:T(8,128)S(1)} %dynamic-slice_bitcast_fusion), channel_id=1, source_target_pairs={{0,2},{2,0},{4,6},{6,4},{8,10},{10,8},{12,14},{14,12},{16,18},{18,... | collective-permute-start | bytes 98312 | tf_op jit(solution)/shard_map/ppermute | solution.py:519
  21.8 4.6 %collective-permute-start.6 = (f32[8,8,128]{2,1,0:T(8,128)S(1)}, f32[8,8,128]{2,1,0:T(8,128)S(1)}, u32[]{:S(2)}, u32[]{:S(2)}) collective-permute-start(f32[8,8,128]{2,1,0:T(8,128)S(1)} %bitcast_add_fusion), channel_id=1, source_target_pairs={{0,8},{2,10},{4,12},{6,14},{8,0},{10,2},{12,4},{14,6},{16,24},{18,... | collective-permute-start | bytes 98312 | tf_op jit(solution)/shard_map/ppermute | solution.py:519
  23.4 5.3 %collective-permute-start.7 = (f32[8,8,128]{2,1,0:T(8,128)S(1)}, f32[8,8,128]{2,1,0:T(8,128)S(1)}, u32[]{:S(2)}, u32[]{:S(2)}) collective-permute-start(f32[8,8,128]{2,1,0:T(8,128)S(1)} %bitcast_add_fusion), channel_id=1, source_target_pairs={{0,12},{2,14},{4,8},{6,10},{8,4},{10,6},{12,0},{14,2},{16,28},{18,... | collective-permute-start | bytes 98312 | tf_op jit(solution)/shard_map/ppermute | solution.py:519
  26.4 3.9 %collective-permute-start.5 = (f32[8,8,128]{2,1,0:T(8,128)S(1)}, f32[8,8,128]{2,1,0:T(8,128)S(1)}, u32[]{:S(2)}, u32[]{:S(2)}) collective-permute-start(f32[8,8,128]{2,1,0:T(8,128)S(1)} %bitcast_add_fusion), channel_id=1, source_target_pairs={{0,4},{2,6},{4,0},{6,2},{8,12},{10,14},{12,8},{14,10},{16,20},{18,... | collective-permute-start | bytes 98312 | tf_op jit(solution)/shard_map/ppermute | solution.py:519
  30.4 5.0 %collective-permute-start.8 = (f32[8,8,128]{2,1,0:T(8,128)S(1)}, f32[8,8,128]{2,1,0:T(8,128)S(1)}, u32[]{:S(2)}, u32[]{:S(2)}) collective-permute-start(f32[8,8,128]{2,1,0:T(8,128)S(1)} %add_add_fusion), channel_id=1, source_target_pairs={{0,16},{2,18},{4,20},{6,22},{8,24},{10,26},{12,28},{14,30},{16,0},... | collective-permute-start | bytes 98312 | tf_op jit(solution)/shard_map/ppermute | solution.py:519
  35.3 1.2 %collective-permute-start.9 = (f32[8,8,128]{2,1,0:T(8,128)S(1)}, f32[8,8,128]{2,1,0:T(8,128)S(1)}, u32[]{:S(2)}, u32[]{:S(2)}) collective-permute-start(f32[8,8,128]{2,1,0:T(8,128)S(1)} %add.58.mine_ref), channel_id=1, source_target_pairs={{0,2},{2,0},{4,6},{6,4},{8,10},{10,8},{12,14},{14,12},{16,18},{18,... | collective-permute-start | bytes 98312 | tf_op jit(solution)/shard_map/ppermute | solution.py:519

commit v7 on v6

--- a/solution.py
+++ b/solution.py
@@ -223,12 +223,12 @@
             left, right, (((0,), (0,)), ((), ())), preferred_element_type=jnp.float32
         ).astype(jnp.bfloat16)
 
-    for start in range(0, padded, LANES):
-        rows = slice(start, start + LANES)
+    for start in range(0, padded, 2 * LANES):
+        rows = slice(start, min(start + 2 * LANES, padded))
         for lane in range(0, padded, 2 * LANES):
             here = slice(lane, min(lane + 2 * LANES, padded))
             mask = product(holds[:, rows], lacks[:, here])
-            if here.start <= start < here.stop:
+            if lane == start:
                 mask = jnp.maximum(mask, 0.0)
             for at in range(rounds):
                 gap = product(ranks[at, :, rows], gaps[at, :, here])

time: 37.5 us -> 36 us (0.960)
  waiting for transfers between devices: 12.2 us -> 9.68 us
  Pallas kernels: 9 us -> 10.6 us
  starting transfers between devices: 11.8 us -> 11.3 us
    ppermute x6, waiting for transfers between devices: 9.53 us -> 6.09 us  [swap(): lax.ppermute(array, 'board', [(at, at ^ step) for at in range(board_count)])]
    pallas_call x1, Pallas kernels: 0.2 us -> 1.21 us  [body(): pl.pallas_call(functools.partial(tail_kernel, rounds, seq_count, nodes),...]
    ppermute x4, starting transfers between devices: 6.09 us -> 5.17 us  [shift(): lax.ppermute(array, 'seq', [(at, (at + step) % seq_count) for at in range...]
    ppermute x4, waiting for transfers between devices: 2.68 us -> 3.6 us  [shift(): lax.ppermute(array, 'seq', [(at, (at + step) % seq_count) for at in range...]
    pallas_call x1, Pallas kernels: 1.27 us -> 1.88 us  [body(): pl.pallas_call(functools.partial(head_kernel, rounds, seq_count, nodes, l...]
    ppermute x6, starting transfers between devices: 5.7 us -> 6.14 us  [swap(): lax.ppermute(array, 'board', [(at, at ^ step) for at in range(board_count)])]
  transfers between devices with their start and end apart: 10 -> 10, of which waited for: 6 -> 7; matrix products, arithmetic and copies ran while one was open for 0% -> 0% of each run, Pallas kernels for 22% -> 24%
where the time goes in v7:
time: 36 us; the launch traced here: 35.9 us
  starting transfers between devices  11.3 us (31%)
  Pallas kernels  10.6 us (29%)
  waiting for transfers between devices  9.68 us (27%)
  local copies, waits for them, and re-layouts  2.15 us (6%)
  between operations  2.11 us (6%)
    ppermute x6, starting transfers between devices, swap(): lax.ppermute(array, 'board', [(at, at ^ step) for at in range(board_count)])  6.14 us
    ppermute x6, waiting for transfers between devices, swap(): lax.ppermute(array, 'board', [(at, at ^ step) for at in range(board_count)])  6.09 us
    ppermute x4, starting transfers between devices, shift(): lax.ppermute(array, 'seq', [(at, (at + step) % seq_count) for at in range...  5.17 us
    pallas_call x1, Pallas kernels, body(): pl.pallas_call(functools.partial(build_kernel, rounds), out_shape=[jax.Sh...  4.37 us
    ppermute x4, waiting for transfers between devices, shift(): lax.ppermute(array, 'seq', [(at, (at + step) % seq_count) for at in range...  3.6 us
    pallas_call x1, Pallas kernels, body(): pl.pallas_call(functools.partial(head_kernel, rounds, seq_count, nodes, l...  1.88 us
    pallas_call x1, Pallas kernels, body(): pl.pallas_call(functools.partial(pack_kernel, rounds, seq_count), out_sha...  1.71 us
    pallas_call x1, Pallas kernels, body(): pl.pallas_call(functools.partial(tail_kernel, rounds, seq_count, nodes),...  1.21 us
  transfers between devices with their start and end apart: 10, of which 7 were waited for; matrix products, arithmetic and copies ran while one was open for 0% of the time, Pallas kernels for 24%

profile of v7, /device:TPU:0, one launch (start us, length us, event | category | flops | bytes accessed | tf_op | source)
XLA Modules:
  0.0 35.9 jit_solution(15101684028881054012)
XLA Ops:
  0.7 1.2 %constant_dynamic-slice_fusion = (bf16[3,1,48,1326]{3,2,1,0:T(8,128)(2,1)S(1)}, bf16[3,1,48,1326]{3,2,1,0:T(8,128)(2,1)S(1)}) fusion(bf16[3,2,48,1326]{3,2,1,0:T(8,128)(2,1)} %bitcast.22, s32[]{:T(128)S(6)} %select_n.31, s32[]{:T(128)S(6)} %select_n.29), kind=kLoop, calls=%fused_computation.4 | loop fusion | bytes 1527560 | tf_op jit(solution)/shard_map/dynamic_slice | solution.py:410
  1.9 3.0 %collective-permute-start.1 = (bf16[96,1326]{1,0:T(8,128)(2,1)S(1)}, bf16[96,1326]{1,0:T(8,128)(2,1)S(1)}, u32[]{:S(2)}, u32[]{:S(2)}) collective-permute-start(bf16[96,1326]{1,0:T(8,128)(2,1)S(1)} %slice.7), channel_id=1, source_target_pairs={{0,1},{1,0},{2,3},{3,2},{4,5},{5,4},{6,7},{7,6},{8,9},{9,8},{10,11... | collective-permute-start | bytes 763784 | tf_op jit(solution)/shard_map/ppermute | solution.py:402
  5.5 1.7 %pack.1 = (bf16[16,1326]{1,0:T(8,128)(2,1)}, f32[24,1408]{1,0:T(8,128)}) custom-call(bf16[1,12,1326]{2,1,0:T(8,128)(2,1)} %reach_ref.1, s32[1,48]{1,0:T(1,128)} %bitcast.28, f32[1,48]{1,0:T(1,128)} %bitcast.29, s32[6,1,1326]{2,1,0:T(1,128)} %bitcast.26, s32[5,1,6]{2,1,0:T(1,128)} %bitcast.27, s32[1]{0:T(128)S(6)} %copy.14.count_ref), custom_call_target="tpu_custom_call" | custom-call | tf_op jit(solution)/shard_map/pack/pallas_call | solution.py:429
  7.3 0.1 collective-permute-start.2
  7.4 2.1 %collective-permute-start = (bf16[48,1326]{1,0:T(8,128)(2,1)S(1)}, bf16[48,1326]{1,0:T(8,128)(2,1)S(1)}, u32[]{:S(2)}, u32[]{:S(2)}) collective-permute-start(bf16[48,1326]{1,0:T(8,128)(2,1)S(1)} %slice.6), channel_id=1, source_target_pairs={{0,1},{1,0},{2,3},{3,2},{4,5},{5,4},{6,7},{7,6},{8,9},{9,8},{10,11... | collective-permute-start | bytes 381896 | tf_op jit(solution)/shard_map/ppermute | solution.py:402
  9.4 0.9 %copy-done = f32[24,1408]{1,0:T(8,128)S(1)} copy-done((f32[24,1408]{1,0:T(8,128)S(1)}, f32[24,1408]{1,0:T(8,128)}, u32[]{:S(2)}) %copy-start) | copy-done | bytes 135192
  10.3 4.4 %build.1 = (bf16[3,1408,1408]{2,1,0:T(8,128)(2,1)S(1)}, f32[24,1408]{1,0:T(8,128)S(1)}) custom-call(f32[24,1408]{1,0:T(8,128)S(1)} %copy-done), custom_call_target="tpu_custom_call" | custom-call | flops 59473920 | bytes 7929856 | tf_op jit(solution)/shard_map/build/pallas_call | solution.py:463
  14.7 0.0 collective-permute-done.2.refs_4_
  14.7 1.9 %head.1 = (f32[24,1408]{1,0:T(8,128)S(1)}, bf16[2,96,128]{2,1,0:T(8,128)(2,1)S(1)}, f32[96,128]{1,0:T(8,128)S(1)}, f32[96,1326]{1,0:T(8,128)S(1)}) custom-call(bf16[3,1408,1408]{2,1,0:T(8,128)(2,1)S(1)} %get-tuple-element.19.refs_0_, f32[24,1408]{1,0:T(8,128)S(1)} %get-tuple-element.20.refs_1_, bf16[144,1326]{1,0:T(8,128)(2,1)S(1)} %bitcast.18, ...), custom_call_target="tpu_custom_call" | custom-call | flops 1141899264 | bytes 11894784 | tf_op jit(solution)/shard_map/head/pallas_call | solution.py:485
  16.6 1.2 %tail.1 = (f32[16,8,128]{2,1,0:T(8,128)S(1)}, f32[16,8,128]{2,1,0:T(8,128)S(1)}) custom-call(bf16[3,1408,1408]{2,1,0:T(8,128)(2,1)S(1)} %get-tuple-element.19.refs_0_, f32[24,1408]{1,0:T(8,128)S(1)} %get-tuple-element.20.refs_1_, bf16[144,1326]{1,0:T(8,128)(2,1)S(1)} %bitcast.19, bf16[48,1326]{1,0:T(8,128)(2,1)S(1)} %collective-permute-done.refs_3_, ...), custom_call_target="tpu_custom_call" | custom-call | tf_op jit(solution)/shard_map/tail/pallas_call | solution.py:502
  17.8 0.0 collective-permute-start.3
  18.5 3.6 %collective-permute-done.3 = f32[16,8,128]{2,1,0:T(8,128)S(1)} collective-permute-done((f32[16,8,128]{2,1,0:T(8,128)S(1)}, f32[16,8,128]{2,1,0:T(8,128)S(1)}, u32[]{:S(2)}, u32[]{:S(2)}) %collective-permute-start.3) | collective-permute-done | bytes 65568 | tf_op jit(solution)/shard_map/ppermute | solution.py:402
  22.1 0.1 collective-permute-start.4
  22.2 1.2 %collective-permute-done.4 = f32[8,8,128]{2,1,0:T(8,128)S(1)} collective-permute-done((f32[8,8,128]{2,1,0:T(8,128)S(1)}, f32[8,8,128]{2,1,0:T(8,128)S(1)}, u32[]{:S(2)}, u32[]{:S(2)}) %collective-permute-start.4) | collective-permute-done | bytes 32800 | tf_op jit(solution)/shard_map/ppermute | solution.py:519
  23.4 1.7 %collective-permute-start.7 = (f32[8,8,128]{2,1,0:T(8,128)S(1)}, f32[8,8,128]{2,1,0:T(8,128)S(1)}, u32[]{:S(2)}, u32[]{:S(2)}) collective-permute-start(f32[8,8,128]{2,1,0:T(8,128)S(1)} %bitcast_add_fusion), channel_id=1, source_target_pairs={{0,12},{2,14},{4,8},{6,10},{8,4},{10,6},{12,0},{14,2},{16,28},{18,... | collective-permute-start | bytes 98312 | tf_op jit(solution)/shard_map/ppermute | solution.py:519
  25.1 1.8 %collective-permute-start.5 = (f32[8,8,128]{2,1,0:T(8,128)S(1)}, f32[8,8,128]{2,1,0:T(8,128)S(1)}, u32[]{:S(2)}, u32[]{:S(2)}) collective-permute-start(f32[8,8,128]{2,1,0:T(8,128)S(1)} %bitcast_add_fusion), channel_id=1, source_target_pairs={{0,4},{2,6},{4,0},{6,2},{8,12},{10,14},{12,8},{14,10},{16,20},{18,... | collective-permute-start | bytes 98312 | tf_op jit(solution)/shard_map/ppermute | solution.py:519
  26.9 0.6 %collective-permute-done.6 = f32[8,8,128]{2,1,0:T(8,128)S(1)} collective-permute-done((f32[8,8,128]{2,1,0:T(8,128)S(1)}, f32[8,8,128]{2,1,0:T(8,128)S(1)}, u32[]{:S(2)}, u32[]{:S(2)}) %collective-permute-start.6) | collective-permute-done | bytes 32800 | tf_op jit(solution)/shard_map/ppermute | solution.py:519
  27.5 0.8 %collective-permute-done.7 = f32[8,8,128]{2,1,0:T(8,128)S(1)} collective-permute-done((f32[8,8,128]{2,1,0:T(8,128)S(1)}, f32[8,8,128]{2,1,0:T(8,128)S(1)}, u32[]{:S(2)}, u32[]{:S(2)}) %collective-permute-start.7) | collective-permute-done | bytes 32800 | tf_op jit(solution)/shard_map/ppermute | solution.py:519
  28.3 0.7 %collective-permute-done.5 = f32[8,8,128]{2,1,0:T(8,128)S(1)} collective-permute-done((f32[8,8,128]{2,1,0:T(8,128)S(1)}, f32[8,8,128]{2,1,0:T(8,128)S(1)}, u32[]{:S(2)}, u32[]{:S(2)}) %collective-permute-start.5) | collective-permute-done | bytes 32800 | tf_op jit(solution)/shard_map/ppermute | solution.py:519
  29.1 2.6 %collective-permute-start.8 = (f32[8,8,128]{2,1,0:T(8,128)S(1)}, f32[8,8,128]{2,1,0:T(8,128)S(1)}, u32[]{:S(2)}, u32[]{:S(2)}) collective-permute-start(f32[8,8,128]{2,1,0:T(8,128)S(1)} %add_add_fusion), channel_id=1, source_target_pairs={{0,16},{2,18},{4,20},{6,22},{8,24},{10,26},{12,28},{14,30},{16,0},... | collective-permute-start | bytes 98312 | tf_op jit(solution)/shard_map/ppermute | solution.py:519
  31.7 2.3 %collective-permute-done.8 = f32[8,8,128]{2,1,0:T(8,128)S(1)} collective-permute-done((f32[8,8,128]{2,1,0:T(8,128)S(1)}, f32[8,8,128]{2,1,0:T(8,128)S(1)}, u32[]{:S(2)}, u32[]{:S(2)}) %collective-permute-start.8) | collective-permute-done | bytes 32800 | tf_op jit(solution)/shard_map/ppermute | solution.py:519
  34.0 0.7 %share.1 = f32[12,1,1326]{2,1,0:T(1,128)} custom-call(f32[16,8,128]{2,1,0:T(8,128)S(1)} %get-tuple-element.31.tiles_ref), custom_call_target="tpu_custom_call" | custom-call | tf_op jit(solution)/shard_map/share/pallas_call | solution.py:540
  34.7 0.5 %collective-permute-done.9.other_ref = f32[8,8,128]{2,1,0:T(8,128)S(1)} collective-permute-done((f32[8,8,128]{2,1,0:T(8,128)S(1)}, f32[8,8,128]{2,1,0:T(8,128)S(1)}, u32[]{:S(2)}, u32[]{:S(2)}) %collective-permute-start.9) | collective-permute-done | bytes 32800 | tf_op jit(solution)/shard_map/ppermute | solution.py:519
  35.2 0.7 %root.1 = f32[12,1326]{1,0:T(8,128)} custom-call(f32[8,8,128]{2,1,0:T(8,128)S(1)} %add.58.mine_ref, f32[8,8,128]{2,1,0:T(8,128)S(1)} %collective-permute-done.9.other_ref), custom_call_target="tpu_custom_call" | custom-call | tf_op jit(solution)/shard_map/root/pallas_call | solution.py:552
  (12 shorter events, 0.1 us)
Async XLA Ops:
  1.9 12.8 %collective-permute-start.1 = (bf16[96,1326]{1,0:T(8,128)(2,1)S(1)}, bf16[96,1326]{1,0:T(8,128)(2,1)S(1)}, u32[]{:S(2)}, u32[]{:S(2)}) collective-permute-start(bf16[96,1326]{1,0:T(8,128)(2,1)S(1)} %slice.7), channel_id=1, source_target_pairs={{0,1},{1,0},{2,3},{3,2},{4,5},{5,4},{6,7},{7,6},{8,9},{9,8},{10,11... | collective-permute-start | bytes 763784 | tf_op jit(solution)/shard_map/ppermute | solution.py:402
  7.3 7.5 %collective-permute-start.2 = (bf16[16,1326]{1,0:T(8,128)(2,1)}, bf16[16,1326]{1,0:T(8,128)(2,1)S(1)}, u32[]{:S(2)}, u32[]{:S(2)}) collective-permute-start(bf16[16,1326]{1,0:T(8,128)(2,1)} %get-tuple-element.23), channel_id=1, source_target_pairs={{0,1},{1,0},{2,3},{3,2},{4,5},{5,4},{6,7},{7,6},{8,9},{9,8},{10,11... | collective-permute-start | bytes 127304 | tf_op jit(solution)/shard_map/ppermute | solution.py:402
  7.4 9.3 %collective-permute-start = (bf16[48,1326]{1,0:T(8,128)(2,1)S(1)}, bf16[48,1326]{1,0:T(8,128)(2,1)S(1)}, u32[]{:S(2)}, u32[]{:S(2)}) collective-permute-start(bf16[48,1326]{1,0:T(8,128)(2,1)S(1)} %slice.6), channel_id=1, source_target_pairs={{0,1},{1,0},{2,3},{3,2},{4,5},{5,4},{6,7},{7,6},{8,9},{9,8},{10,11... | collective-permute-start | bytes 381896 | tf_op jit(solution)/shard_map/ppermute | solution.py:402
  9.4 0.9 %copy-start = (f32[24,1408]{1,0:T(8,128)S(1)}, f32[24,1408]{1,0:T(8,128)}, u32[]{:S(2)}) copy-start(f32[24,1408]{1,0:T(8,128)} %get-tuple-element.18.info_ref) | copy-start | bytes 405508
  17.8 4.3 %collective-permute-start.3 = (f32[16,8,128]{2,1,0:T(8,128)S(1)}, f32[16,8,128]{2,1,0:T(8,128)S(1)}, u32[]{:S(2)}, u32[]{:S(2)}) collective-permute-start(f32[16,8,128]{2,1,0:T(8,128)S(1)} %get-tuple-element.29), channel_id=1, source_target_pairs={{0,1},{1,0},{2,3},{3,2},{4,5},{5,4},{6,7},{7,6},{8,9},{9,8},{10,11... | collective-permute-start | bytes 196616 | tf_op jit(solution)/shard_map/ppermute | solution.py:402
  22.1 1.3 %collective-permute-start.4 = (f32[8,8,128]{2,1,0:T(8,128)S(1)}, f32[8,8,128]{2,1,0:T(8,128)S(1)}, u32[]{:S(2)}, u32[]{:S(2)}) collective-permute-start(f32[8,8,128]{2,1,0:T(8,128)S(1)} %dynamic-slice_bitcast_fusion), channel_id=1, source_target_pairs={{0,2},{2,0},{4,6},{6,4},{8,10},{10,8},{12,14},{14,12},{16,18},{18,... | collective-permute-start | bytes 98312 | tf_op jit(solution)/shard_map/ppermute | solution.py:519
  23.4 4.1 %collective-permute-start.6 = (f32[8,8,128]{2,1,0:T(8,128)S(1)}, f32[8,8,128]{2,1,0:T(8,128)S(1)}, u32[]{:S(2)}, u32[]{:S(2)}) collective-permute-start(f32[8,8,128]{2,1,0:T(8,128)S(1)} %bitcast_add_fusion), channel_id=1, source_target_pairs={{0,8},{2,10},{4,12},{6,14},{8,0},{10,2},{12,4},{14,6},{16,24},{18,... | collective-permute-start | bytes 98312 | tf_op jit(solution)/shard_map/ppermute | solution.py:519
  23.4 4.9 %collective-permute-start.7 = (f32[8,8,128]{2,1,0:T(8,128)S(1)}, f32[8,8,128]{2,1,0:T(8,128)S(1)}, u32[]{:S(2)}, u32[]{:S(2)}) collective-permute-start(f32[8,8,128]{2,1,0:T(8,128)S(1)} %bitcast_add_fusion), channel_id=1, source_target_pairs={{0,12},{2,14},{4,8},{6,10},{8,4},{10,6},{12,0},{14,2},{16,28},{18,... | collective-permute-start | bytes 98312 | tf_op jit(solution)/shard_map/ppermute | solution.py:519
  25.1 3.9 %collective-permute-start.5 = (f32[8,8,128]{2,1,0:T(8,128)S(1)}, f32[8,8,128]{2,1,0:T(8,128)S(1)}, u32[]{:S(2)}, u32[]{:S(2)}) collective-permute-start(f32[8,8,128]{2,1,0:T(8,128)S(1)} %bitcast_add_fusion), channel_id=1, source_target_pairs={{0,4},{2,6},{4,0},{6,2},{8,12},{10,14},{12,8},{14,10},{16,20},{18,... | collective-permute-start | bytes 98312 | tf_op jit(solution)/shard_map/ppermute | solution.py:519
  29.1 4.9 %collective-permute-start.8 = (f32[8,8,128]{2,1,0:T(8,128)S(1)}, f32[8,8,128]{2,1,0:T(8,128)S(1)}, u32[]{:S(2)}, u32[]{:S(2)}) collective-permute-start(f32[8,8,128]{2,1,0:T(8,128)S(1)} %add_add_fusion), channel_id=1, source_target_pairs={{0,16},{2,18},{4,20},{6,22},{8,24},{10,26},{12,28},{14,30},{16,0},... | collective-permute-start | bytes 98312 | tf_op jit(solution)/shard_map/ppermute | solution.py:519
  34.0 1.2 %collective-permute-start.9 = (f32[8,8,128]{2,1,0:T(8,128)S(1)}, f32[8,8,128]{2,1,0:T(8,128)S(1)}, u32[]{:S(2)}, u32[]{:S(2)}) collective-permute-start(f32[8,8,128]{2,1,0:T(8,128)S(1)} %add.58.mine_ref), channel_id=1, source_target_pairs={{0,2},{2,0},{4,6},{6,4},{8,10},{10,8},{12,14},{14,12},{16,18},{18,... | collective-permute-start | bytes 98312 | tf_op jit(solution)/shard_map/ppermute | solution.py:519

commit v8 on v6

--- a/solution.py
+++ b/solution.py
@@ -225,13 +225,21 @@
 
     for start in range(0, padded, LANES):
         rows = slice(start, start + LANES)
+        column = jnp.broadcast_to(info_ref[rounds - 1 : rounds, rows], (LANES, LANES)).T
         for lane in range(0, padded, 2 * LANES):
             here = slice(lane, min(lane + 2 * LANES, padded))
             mask = product(holds[:, rows], lacks[:, here])
             if here.start <= start < here.stop:
                 mask = jnp.maximum(mask, 0.0)
             for at in range(rounds):
-                gap = product(ranks[at, :, rows], gaps[at, :, here])
+                if at < rounds - 1:
+                    gap = product(ranks[at, :, rows], gaps[at, :, here])
+                else:
+                    pieces = [
+                        (info_ref[at : at + 1, left : left + LANES] - column).astype(jnp.bfloat16)
+                        for left in range(here.start, here.stop, LANES)
+                    ]
+                    gap = jnp.concatenate(pieces, axis=1)
                 payoff_ref[at, rows, here] = jnp.maximum(jnp.minimum(gap, mask), -mask)
 
 

time: 37.5 us -> 36.3 us (0.968)
  waiting for transfers between devices: 12.2 us -> 9.6 us
  starting transfers between devices: 11.8 us -> 14.2 us
  Pallas kernels: 9 us -> 8.39 us
    ppermute x6, waiting for transfers between devices: 9.53 us -> 7.53 us  [swap(): lax.ppermute(array, 'board', [(at, at ^ step) for at in range(board_count)])]
    ppermute x6, starting transfers between devices: 5.7 us -> 7.48 us  [swap(): lax.ppermute(array, 'board', [(at, at ^ step) for at in range(board_count)])]
    ppermute x4, waiting for transfers between devices: 2.68 us -> 2.07 us  [shift(): lax.ppermute(array, 'seq', [(at, (at + step) % seq_count) for at in range...]
    ppermute x4, starting transfers between devices: 6.09 us -> 6.7 us  [shift(): lax.ppermute(array, 'seq', [(at, (at + step) % seq_count) for at in range...]
    pallas_call x1, Pallas kernels: 4.38 us -> 3.79 us  [body(): pl.pallas_call(functools.partial(build_kernel, rounds), out_shape=[jax.Sh...]
  transfers between devices with their start and end apart: 10 -> 10, of which waited for: 6 -> 6; matrix products, arithmetic and copies ran while one was open for 0% -> 0% of each run, Pallas kernels for 22% -> 21%
where the time goes in v8:
time: 36.3 us; the launch traced here: 36.4 us
  starting transfers between devices  14.2 us (39%)
  waiting for transfers between devices  9.6 us (26%)
  Pallas kernels  8.39 us (23%)
  local copies, waits for them, and re-layouts  2.15 us (6%)
  between operations  2.09 us (6%)
    ppermute x6, waiting for transfers between devices, swap(): lax.ppermute(array, 'board', [(at, at ^ step) for at in range(board_count)])  7.53 us
    ppermute x6, starting transfers between devices, swap(): lax.ppermute(array, 'board', [(at, at ^ step) for at in range(board_count)])  7.48 us
    ppermute x4, starting transfers between devices, shift(): lax.ppermute(array, 'seq', [(at, (at + step) % seq_count) for at in range...  6.7 us
    pallas_call x1, Pallas kernels, body(): pl.pallas_call(functools.partial(build_kernel, rounds), out_shape=[jax.Sh...  3.79 us
    ppermute x4, waiting for transfers between devices, shift(): lax.ppermute(array, 'seq', [(at, (at + step) % seq_count) for at in range...  2.07 us
    pallas_call x1, Pallas kernels, body(): pl.pallas_call(functools.partial(pack_kernel, rounds, seq_count), out_sha...  1.71 us
    pallas_call x1, Pallas kernels, body(): pl.pallas_call(functools.partial(head_kernel, rounds, seq_count, nodes, l...  1.25 us
    dynamic_slice x1, local copies, waits for them, and re-layouts, strategy_for(): rows = lax.dynamic_slice_in_dim(split, owner, 1, axis=1)  1.19 us
  transfers between devices with their start and end apart: 10, of which 6 were waited for; matrix products, arithmetic and copies ran while one was open for 0% of the time, Pallas kernels for 21%

profile of v8, /device:TPU:0, one launch (start us, length us, event | category | flops | bytes accessed | tf_op | source)
XLA Modules:
  0.0 36.4 jit_solution(4957396884456360343)
XLA Ops:
  0.7 1.2 %constant_dynamic-slice_fusion = (bf16[3,1,48,1326]{3,2,1,0:T(8,128)(2,1)S(1)}, bf16[3,1,48,1326]{3,2,1,0:T(8,128)(2,1)S(1)}) fusion(bf16[3,2,48,1326]{3,2,1,0:T(8,128)(2,1)} %bitcast.22, s32[]{:T(128)S(6)} %select_n.31, s32[]{:T(128)S(6)} %select_n.29), kind=kLoop, calls=%fused_computation.4 | loop fusion | bytes 1527560 | tf_op jit(solution)/shard_map/dynamic_slice | solution.py:418
  1.9 3.0 %collective-permute-start.1 = (bf16[96,1326]{1,0:T(8,128)(2,1)S(1)}, bf16[96,1326]{1,0:T(8,128)(2,1)S(1)}, u32[]{:S(2)}, u32[]{:S(2)}) collective-permute-start(bf16[96,1326]{1,0:T(8,128)(2,1)S(1)} %slice.7), channel_id=1, source_target_pairs={{0,1},{1,0},{2,3},{3,2},{4,5},{5,4},{6,7},{7,6},{8,9},{9,8},{10,11... | collective-permute-start | bytes 763784 | tf_op jit(solution)/shard_map/ppermute | solution.py:410
  5.5 1.7 %pack.1 = (bf16[16,1326]{1,0:T(8,128)(2,1)}, f32[24,1408]{1,0:T(8,128)}) custom-call(bf16[1,12,1326]{2,1,0:T(8,128)(2,1)} %reach_ref.1, s32[1,48]{1,0:T(1,128)} %bitcast.28, f32[1,48]{1,0:T(1,128)} %bitcast.29, s32[6,1,1326]{2,1,0:T(1,128)} %bitcast.26, s32[5,1,6]{2,1,0:T(1,128)} %bitcast.27, s32[1]{0:T(128)S(6)} %copy.14.count_ref), custom_call_target="tpu_custom_call" | custom-call | tf_op jit(solution)/shard_map/pack/pallas_call | solution.py:437
  7.3 0.1 collective-permute-start.2
  7.4 2.1 %collective-permute-start = (bf16[48,1326]{1,0:T(8,128)(2,1)S(1)}, bf16[48,1326]{1,0:T(8,128)(2,1)S(1)}, u32[]{:S(2)}, u32[]{:S(2)}) collective-permute-start(bf16[48,1326]{1,0:T(8,128)(2,1)S(1)} %slice.6), channel_id=1, source_target_pairs={{0,1},{1,0},{2,3},{3,2},{4,5},{5,4},{6,7},{7,6},{8,9},{9,8},{10,11... | collective-permute-start | bytes 381896 | tf_op jit(solution)/shard_map/ppermute | solution.py:410
  9.4 0.9 %copy-done = f32[24,1408]{1,0:T(8,128)S(1)} copy-done((f32[24,1408]{1,0:T(8,128)S(1)}, f32[24,1408]{1,0:T(8,128)}, u32[]{:S(2)}) %copy-start) | copy-done | bytes 135192
  10.3 3.8 %build.1 = (bf16[3,1408,1408]{2,1,0:T(8,128)(2,1)S(1)}, f32[24,1408]{1,0:T(8,128)S(1)}) custom-call(f32[24,1408]{1,0:T(8,128)S(1)} %copy-done), custom_call_target="tpu_custom_call" | custom-call | flops 59473920 | bytes 7929856 | tf_op jit(solution)/shard_map/build/pallas_call | solution.py:471
  14.1 0.0 collective-permute-done.2.refs_4_
  14.1 0.0 collective-permute-done.1.refs_3_
  14.2 1.3 %head.1 = (f32[24,1408]{1,0:T(8,128)S(1)}, bf16[2,96,128]{2,1,0:T(8,128)(2,1)S(1)}, f32[96,128]{1,0:T(8,128)S(1)}, f32[96,1326]{1,0:T(8,128)S(1)}) custom-call(bf16[3,1408,1408]{2,1,0:T(8,128)(2,1)S(1)} %get-tuple-element.19.refs_0_, f32[24,1408]{1,0:T(8,128)S(1)} %get-tuple-element.20.refs_1_, bf16[144,1326]{1,0:T(8,128)(2,1)S(1)} %bitcast.18, ...), custom_call_target="tpu_custom_call" | custom-call | flops 1141899264 | bytes 11894784 | tf_op jit(solution)/shard_map/head/pallas_call | solution.py:493
  15.4 0.2 tail.1
  15.6 1.6 %collective-permute-start.3 = (f32[16,8,128]{2,1,0:T(8,128)S(1)}, f32[16,8,128]{2,1,0:T(8,128)S(1)}, u32[]{:S(2)}, u32[]{:S(2)}) collective-permute-start(f32[16,8,128]{2,1,0:T(8,128)S(1)} %get-tuple-element.29), channel_id=1, source_target_pairs={{0,1},{1,0},{2,3},{3,2},{4,5},{5,4},{6,7},{7,6},{8,9},{9,8},{10,11... | collective-permute-start | bytes 196616 | tf_op jit(solution)/shard_map/ppermute | solution.py:410
  17.8 2.1 %collective-permute-done.3 = f32[16,8,128]{2,1,0:T(8,128)S(1)} collective-permute-done((f32[16,8,128]{2,1,0:T(8,128)S(1)}, f32[16,8,128]{2,1,0:T(8,128)S(1)}, u32[]{:S(2)}, u32[]{:S(2)}) %collective-permute-start.3) | collective-permute-done | bytes 65568 | tf_op jit(solution)/shard_map/ppermute | solution.py:410
  19.9 0.1 collective-permute-start.4
  20.0 1.2 %collective-permute-done.4 = f32[8,8,128]{2,1,0:T(8,128)S(1)} collective-permute-done((f32[8,8,128]{2,1,0:T(8,128)S(1)}, f32[8,8,128]{2,1,0:T(8,128)S(1)}, u32[]{:S(2)}, u32[]{:S(2)}) %collective-permute-start.4) | collective-permute-done | bytes 32800 | tf_op jit(solution)/shard_map/ppermute | solution.py:527
  21.2 3.2 %collective-permute-start.6 = (f32[8,8,128]{2,1,0:T(8,128)S(1)}, f32[8,8,128]{2,1,0:T(8,128)S(1)}, u32[]{:S(2)}, u32[]{:S(2)}) collective-permute-start(f32[8,8,128]{2,1,0:T(8,128)S(1)} %bitcast_add_fusion), channel_id=1, source_target_pairs={{0,8},{2,10},{4,12},{6,14},{8,0},{10,2},{12,4},{14,6},{16,24},{18,... | collective-permute-start | bytes 98312 | tf_op jit(solution)/shard_map/ppermute | solution.py:527
  24.4 1.5 %collective-permute-start.5 = (f32[8,8,128]{2,1,0:T(8,128)S(1)}, f32[8,8,128]{2,1,0:T(8,128)S(1)}, u32[]{:S(2)}, u32[]{:S(2)}) collective-permute-start(f32[8,8,128]{2,1,0:T(8,128)S(1)} %bitcast_add_fusion), channel_id=1, source_target_pairs={{0,4},{2,6},{4,0},{6,2},{8,12},{10,14},{12,8},{14,10},{16,20},{18,... | collective-permute-start | bytes 98312 | tf_op jit(solution)/shard_map/ppermute | solution.py:527
  26.0 0.4 %collective-permute-done.6 = f32[8,8,128]{2,1,0:T(8,128)S(1)} collective-permute-done((f32[8,8,128]{2,1,0:T(8,128)S(1)}, f32[8,8,128]{2,1,0:T(8,128)S(1)}, u32[]{:S(2)}, u32[]{:S(2)}) %collective-permute-start.6) | collective-permute-done | bytes 32800 | tf_op jit(solution)/shard_map/ppermute | solution.py:527
  26.4 2.9 %collective-permute-done.7 = f32[8,8,128]{2,1,0:T(8,128)S(1)} collective-permute-done((f32[8,8,128]{2,1,0:T(8,128)S(1)}, f32[8,8,128]{2,1,0:T(8,128)S(1)}, u32[]{:S(2)}, u32[]{:S(2)}) %collective-permute-start.7) | collective-permute-done | bytes 32800 | tf_op jit(solution)/shard_map/ppermute | solution.py:527
  29.3 2.6 %collective-permute-start.8 = (f32[8,8,128]{2,1,0:T(8,128)S(1)}, f32[8,8,128]{2,1,0:T(8,128)S(1)}, u32[]{:S(2)}, u32[]{:S(2)}) collective-permute-start(f32[8,8,128]{2,1,0:T(8,128)S(1)} %add_add_fusion), channel_id=1, source_target_pairs={{0,16},{2,18},{4,20},{6,22},{8,24},{10,26},{12,28},{14,30},{16,0},... | collective-permute-start | bytes 98312 | tf_op jit(solution)/shard_map/ppermute | solution.py:527
  31.9 2.6 %collective-permute-done.8 = f32[8,8,128]{2,1,0:T(8,128)S(1)} collective-permute-done((f32[8,8,128]{2,1,0:T(8,128)S(1)}, f32[8,8,128]{2,1,0:T(8,128)S(1)}, u32[]{:S(2)}, u32[]{:S(2)}) %collective-permute-start.8) | collective-permute-done | bytes 32800 | tf_op jit(solution)/shard_map/ppermute | solution.py:527
  34.5 0.7 %share.1 = f32[12,1,1326]{2,1,0:T(1,128)} custom-call(f32[16,8,128]{2,1,0:T(8,128)S(1)} %get-tuple-element.31.tiles_ref), custom_call_target="tpu_custom_call" | custom-call | tf_op jit(solution)/shard_map/share/pallas_call | solution.py:548
  35.2 0.5 %collective-permute-done.9.other_ref = f32[8,8,128]{2,1,0:T(8,128)S(1)} collective-permute-done((f32[8,8,128]{2,1,0:T(8,128)S(1)}, f32[8,8,128]{2,1,0:T(8,128)S(1)}, u32[]{:S(2)}, u32[]{:S(2)}) %collective-permute-start.9) | collective-permute-done | bytes 32800 | tf_op jit(solution)/shard_map/ppermute | solution.py:527
  35.7 0.7 %root.1 = f32[12,1326]{1,0:T(8,128)} custom-call(f32[8,8,128]{2,1,0:T(8,128)S(1)} %add.58.mine_ref, f32[8,8,128]{2,1,0:T(8,128)S(1)} %collective-permute-done.9.other_ref), custom_call_target="tpu_custom_call" | custom-call | tf_op jit(solution)/shard_map/root/pallas_call | solution.py:560
  (12 shorter events, 0.1 us)
Async XLA Ops:
  1.9 12.3 %collective-permute-start.1 = (bf16[96,1326]{1,0:T(8,128)(2,1)S(1)}, bf16[96,1326]{1,0:T(8,128)(2,1)S(1)}, u32[]{:S(2)}, u32[]{:S(2)}) collective-permute-start(bf16[96,1326]{1,0:T(8,128)(2,1)S(1)} %slice.7), channel_id=1, source_target_pairs={{0,1},{1,0},{2,3},{3,2},{4,5},{5,4},{6,7},{7,6},{8,9},{9,8},{10,11... | collective-permute-start | bytes 763784 | tf_op jit(solution)/shard_map/ppermute | solution.py:410
  7.3 6.9 %collective-permute-start.2 = (bf16[16,1326]{1,0:T(8,128)(2,1)}, bf16[16,1326]{1,0:T(8,128)(2,1)S(1)}, u32[]{:S(2)}, u32[]{:S(2)}) collective-permute-start(bf16[16,1326]{1,0:T(8,128)(2,1)} %get-tuple-element.23), channel_id=1, source_target_pairs={{0,1},{1,0},{2,3},{3,2},{4,5},{5,4},{6,7},{7,6},{8,9},{9,8},{10,11... | collective-permute-start | bytes 127304 | tf_op jit(solution)/shard_map/ppermute | solution.py:410
  7.4 8.1 %collective-permute-start = (bf16[48,1326]{1,0:T(8,128)(2,1)S(1)}, bf16[48,1326]{1,0:T(8,128)(2,1)S(1)}, u32[]{:S(2)}, u32[]{:S(2)}) collective-permute-start(bf16[48,1326]{1,0:T(8,128)(2,1)S(1)} %slice.6), channel_id=1, source_target_pairs={{0,1},{1,0},{2,3},{3,2},{4,5},{5,4},{6,7},{7,6},{8,9},{9,8},{10,11... | collective-permute-start | bytes 381896 | tf_op jit(solution)/shard_map/ppermute | solution.py:410
  9.4 0.9 %copy-start = (f32[24,1408]{1,0:T(8,128)S(1)}, f32[24,1408]{1,0:T(8,128)}, u32[]{:S(2)}) copy-start(f32[24,1408]{1,0:T(8,128)} %get-tuple-element.18.info_ref) | copy-start | bytes 405508
  15.6 4.3 %collective-permute-start.3 = (f32[16,8,128]{2,1,0:T(8,128)S(1)}, f32[16,8,128]{2,1,0:T(8,128)S(1)}, u32[]{:S(2)}, u32[]{:S(2)}) collective-permute-start(f32[16,8,128]{2,1,0:T(8,128)S(1)} %get-tuple-element.29), channel_id=1, source_target_pairs={{0,1},{1,0},{2,3},{3,2},{4,5},{5,4},{6,7},{7,6},{8,9},{9,8},{10,11... | collective-permute-start | bytes 196616 | tf_op jit(solution)/shard_map/ppermute | solution.py:410
  19.9 1.3 %collective-permute-start.4 = (f32[8,8,128]{2,1,0:T(8,128)S(1)}, f32[8,8,128]{2,1,0:T(8,128)S(1)}, u32[]{:S(2)}, u32[]{:S(2)}) collective-permute-start(f32[8,8,128]{2,1,0:T(8,128)S(1)} %dynamic-slice_bitcast_fusion), channel_id=1, source_target_pairs={{0,2},{2,0},{4,6},{6,4},{8,10},{10,8},{12,14},{14,12},{16,18},{18,... | collective-permute-start | bytes 98312 | tf_op jit(solution)/shard_map/ppermute | solution.py:527
  21.2 5.2 %collective-permute-start.6 = (f32[8,8,128]{2,1,0:T(8,128)S(1)}, f32[8,8,128]{2,1,0:T(8,128)S(1)}, u32[]{:S(2)}, u32[]{:S(2)}) collective-permute-start(f32[8,8,128]{2,1,0:T(8,128)S(1)} %bitcast_add_fusion), channel_id=1, source_target_pairs={{0,8},{2,10},{4,12},{6,14},{8,0},{10,2},{12,4},{14,6},{16,24},{18,... | collective-permute-start | bytes 98312 | tf_op jit(solution)/shard_map/ppermute | solution.py:527
  24.4 4.8 %collective-permute-start.7 = (f32[8,8,128]{2,1,0:T(8,128)S(1)}, f32[8,8,128]{2,1,0:T(8,128)S(1)}, u32[]{:S(2)}, u32[]{:S(2)}) collective-permute-start(f32[8,8,128]{2,1,0:T(8,128)S(1)} %bitcast_add_fusion), channel_id=1, source_target_pairs={{0,12},{2,14},{4,8},{6,10},{8,4},{10,6},{12,0},{14,2},{16,28},{18,... | collective-permute-start | bytes 98312 | tf_op jit(solution)/shard_map/ppermute | solution.py:527
  24.4 4.8 %collective-permute-start.5 = (f32[8,8,128]{2,1,0:T(8,128)S(1)}, f32[8,8,128]{2,1,0:T(8,128)S(1)}, u32[]{:S(2)}, u32[]{:S(2)}) collective-permute-start(f32[8,8,128]{2,1,0:T(8,128)S(1)} %bitcast_add_fusion), channel_id=1, source_target_pairs={{0,4},{2,6},{4,0},{6,2},{8,12},{10,14},{12,8},{14,10},{16,20},{18,... | collective-permute-start | bytes 98312 | tf_op jit(solution)/shard_map/ppermute | solution.py:527
  29.3 5.2 %collective-permute-start.8 = (f32[8,8,128]{2,1,0:T(8,128)S(1)}, f32[8,8,128]{2,1,0:T(8,128)S(1)}, u32[]{:S(2)}, u32[]{:S(2)}) collective-permute-start(f32[8,8,128]{2,1,0:T(8,128)S(1)} %add_add_fusion), channel_id=1, source_target_pairs={{0,16},{2,18},{4,20},{6,22},{8,24},{10,26},{12,28},{14,30},{16,0},... | collective-permute-start | bytes 98312 | tf_op jit(solution)/shard_map/ppermute | solution.py:527
  34.5 1.2 %collective-permute-start.9 = (f32[8,8,128]{2,1,0:T(8,128)S(1)}, f32[8,8,128]{2,1,0:T(8,128)S(1)}, u32[]{:S(2)}, u32[]{:S(2)}) collective-permute-start(f32[8,8,128]{2,1,0:T(8,128)S(1)} %add.58.mine_ref), channel_id=1, source_target_pairs={{0,2},{2,0},{4,6},{6,4},{8,10},{10,8},{12,14},{14,12},{16,18},{18,... | collective-permute-start | bytes 98312 | tf_op jit(solution)/shard_map/ppermute | solution.py:527

commit v9 on v8

--- a/solution.py
+++ b/solution.py
@@ -225,18 +225,23 @@
 
     for start in range(0, padded, LANES):
         rows = slice(start, start + LANES)
-        column = jnp.broadcast_to(info_ref[rounds - 1 : rounds, rows], (LANES, LANES)).T
+        columns = [
+            jnp.broadcast_to(info_ref[at : at + 1, rows], (LANES, LANES)).T
+            for at in range(1, rounds)
+        ]
         for lane in range(0, padded, 2 * LANES):
             here = slice(lane, min(lane + 2 * LANES, padded))
             mask = product(holds[:, rows], lacks[:, here])
             if here.start <= start < here.stop:
                 mask = jnp.maximum(mask, 0.0)
             for at in range(rounds):
-                if at < rounds - 1:
+                if at == 0:
                     gap = product(ranks[at, :, rows], gaps[at, :, here])
                 else:
                     pieces = [
-                        (info_ref[at : at + 1, left : left + LANES] - column).astype(jnp.bfloat16)
+                        (info_ref[at : at + 1, left : left + LANES] - columns[at - 1]).astype(
+                            jnp.bfloat16
+                        )
                         for left in range(here.start, here.stop, LANES)
                     ]
                     gap = jnp.concatenate(pieces, axis=1)

time: 36.3 us -> 35.2 us (0.970)
  starting transfers between devices: 14.2 us -> 13.1 us
    ppermute x6, starting transfers between devices: 7.48 us -> 6.22 us  [swap(): lax.ppermute(array, 'board', [(at, at ^ step) for at in range(board_count)])]
  transfers between devices with their start and end apart: 10 -> 10, of which waited for: 6 -> 8; matrix products, arithmetic and copies ran while one was open for 0% -> 0% of each run, Pallas kernels for 21% -> 21%
where the time goes in v9:
time: 35.2 us; the launch traced here: 35 us
  starting transfers between devices  13.1 us (37%)
  waiting for transfers between devices  9.49 us (27%)
  Pallas kernels  8.12 us (23%)
  local copies, waits for them, and re-layouts  2.15 us (6%)
  between operations  2.09 us (6%)
    ppermute x6, waiting for transfers between devices, swap(): lax.ppermute(array, 'board', [(at, at ^ step) for at in range(board_count)])  7.54 us
    ppermute x4, starting transfers between devices, shift(): lax.ppermute(array, 'seq', [(at, (at + step) % seq_count) for at in range...  6.9 us
    ppermute x6, starting transfers between devices, swap(): lax.ppermute(array, 'board', [(at, at ^ step) for at in range(board_count)])  6.22 us
    pallas_call x1, Pallas kernels, body(): pl.pallas_call(functools.partial(build_kernel, rounds), out_shape=[jax.Sh...  3.52 us
    ppermute x4, waiting for transfers between devices, shift(): lax.ppermute(array, 'seq', [(at, (at + step) % seq_count) for at in range...  1.94 us
    pallas_call x1, Pallas kernels, body(): pl.pallas_call(functools.partial(pack_kernel, rounds, seq_count), out_sha...  1.71 us
    pallas_call x1, Pallas kernels, body(): pl.pallas_call(functools.partial(head_kernel, rounds, seq_count, nodes, l...  1.26 us
    dynamic_slice x1, local copies, waits for them, and re-layouts, strategy_for(): rows = lax.dynamic_slice_in_dim(split, owner, 1, axis=1)  1.19 us
  transfers between devices with their start and end apart: 10, of which 8 were waited for; matrix products, arithmetic and copies ran while one was open for 0% of the time, Pallas kernels for 21%

profile of v9, /device:TPU:0, one launch (start us, length us, event | category | flops | bytes accessed | tf_op | source)
XLA Modules:
  0.0 35.0 jit_solution(16375537339311440248)
XLA Ops:
  0.7 1.2 %constant_dynamic-slice_fusion = (bf16[3,1,48,1326]{3,2,1,0:T(8,128)(2,1)S(1)}, bf16[3,1,48,1326]{3,2,1,0:T(8,128)(2,1)S(1)}) fusion(bf16[3,2,48,1326]{3,2,1,0:T(8,128)(2,1)} %bitcast.22, s32[]{:T(128)S(6)} %select_n.31, s32[]{:T(128)S(6)} %select_n.29), kind=kLoop, calls=%fused_computation.4 | loop fusion | bytes 1527560 | tf_op jit(solution)/shard_map/dynamic_slice | solution.py:423
  1.9 3.0 %collective-permute-start.1 = (bf16[96,1326]{1,0:T(8,128)(2,1)S(1)}, bf16[96,1326]{1,0:T(8,128)(2,1)S(1)}, u32[]{:S(2)}, u32[]{:S(2)}) collective-permute-start(bf16[96,1326]{1,0:T(8,128)(2,1)S(1)} %slice.7), channel_id=1, source_target_pairs={{0,1},{1,0},{2,3},{3,2},{4,5},{5,4},{6,7},{7,6},{8,9},{9,8},{10,11... | collective-permute-start | bytes 763784 | tf_op jit(solution)/shard_map/ppermute | solution.py:415
  5.5 1.7 %pack.1 = (bf16[16,1326]{1,0:T(8,128)(2,1)}, f32[24,1408]{1,0:T(8,128)}) custom-call(bf16[1,12,1326]{2,1,0:T(8,128)(2,1)} %reach_ref.1, s32[1,48]{1,0:T(1,128)} %bitcast.28, f32[1,48]{1,0:T(1,128)} %bitcast.29, s32[6,1,1326]{2,1,0:T(1,128)} %bitcast.26, s32[5,1,6]{2,1,0:T(1,128)} %bitcast.27, s32[1]{0:T(128)S(6)} %copy.14.count_ref), custom_call_target="tpu_custom_call" | custom-call | tf_op jit(solution)/shard_map/pack/pallas_call | solution.py:442
  7.3 0.1 collective-permute-start.2
  7.4 2.1 %collective-permute-start = (bf16[48,1326]{1,0:T(8,128)(2,1)S(1)}, bf16[48,1326]{1,0:T(8,128)(2,1)S(1)}, u32[]{:S(2)}, u32[]{:S(2)}) collective-permute-start(bf16[48,1326]{1,0:T(8,128)(2,1)S(1)} %slice.6), channel_id=1, source_target_pairs={{0,1},{1,0},{2,3},{3,2},{4,5},{5,4},{6,7},{7,6},{8,9},{9,8},{10,11... | collective-permute-start | bytes 381896 | tf_op jit(solution)/shard_map/ppermute | solution.py:415
  9.4 0.9 %copy-done = f32[24,1408]{1,0:T(8,128)S(1)} copy-done((f32[24,1408]{1,0:T(8,128)S(1)}, f32[24,1408]{1,0:T(8,128)}, u32[]{:S(2)}) %copy-start) | copy-done | bytes 135192
  10.3 3.5 %build.1 = (bf16[3,1408,1408]{2,1,0:T(8,128)(2,1)S(1)}, f32[24,1408]{1,0:T(8,128)S(1)}) custom-call(f32[24,1408]{1,0:T(8,128)S(1)} %copy-done), custom_call_target="tpu_custom_call" | custom-call | flops 59473920 | bytes 7929856 | tf_op jit(solution)/shard_map/build/pallas_call | solution.py:476
  13.9 1.3 %head.1 = (f32[24,1408]{1,0:T(8,128)S(1)}, bf16[2,96,128]{2,1,0:T(8,128)(2,1)S(1)}, f32[96,128]{1,0:T(8,128)S(1)}, f32[96,1326]{1,0:T(8,128)S(1)}) custom-call(bf16[3,1408,1408]{2,1,0:T(8,128)(2,1)S(1)} %get-tuple-element.19.refs_0_, f32[24,1408]{1,0:T(8,128)S(1)} %get-tuple-element.20.refs_1_, bf16[144,1326]{1,0:T(8,128)(2,1)S(1)} %bitcast.18, ...), custom_call_target="tpu_custom_call" | custom-call | flops 1141899264 | bytes 11894784 | tf_op jit(solution)/shard_map/head/pallas_call | solution.py:498
  15.2 0.1 collective-permute-done.refs_3_
  15.2 0.2 tail.1
  15.4 1.7 %collective-permute-start.3 = (f32[16,8,128]{2,1,0:T(8,128)S(1)}, f32[16,8,128]{2,1,0:T(8,128)S(1)}, u32[]{:S(2)}, u32[]{:S(2)}) collective-permute-start(f32[16,8,128]{2,1,0:T(8,128)S(1)} %get-tuple-element.29), channel_id=1, source_target_pairs={{0,1},{1,0},{2,3},{3,2},{4,5},{5,4},{6,7},{7,6},{8,9},{9,8},{10,11... | collective-permute-start | bytes 196616 | tf_op jit(solution)/shard_map/ppermute | solution.py:415
  17.8 1.9 %collective-permute-done.3 = f32[16,8,128]{2,1,0:T(8,128)S(1)} collective-permute-done((f32[16,8,128]{2,1,0:T(8,128)S(1)}, f32[16,8,128]{2,1,0:T(8,128)S(1)}, u32[]{:S(2)}, u32[]{:S(2)}) %collective-permute-start.3) | collective-permute-done | bytes 65568 | tf_op jit(solution)/shard_map/ppermute | solution.py:415
  19.8 1.2 %collective-permute-done.4 = f32[8,8,128]{2,1,0:T(8,128)S(1)} collective-permute-done((f32[8,8,128]{2,1,0:T(8,128)S(1)}, f32[8,8,128]{2,1,0:T(8,128)S(1)}, u32[]{:S(2)}, u32[]{:S(2)}) %collective-permute-start.4) | collective-permute-done | bytes 32800 | tf_op jit(solution)/shard_map/ppermute | solution.py:532
  21.0 1.8 %collective-permute-start.6 = (f32[8,8,128]{2,1,0:T(8,128)S(1)}, f32[8,8,128]{2,1,0:T(8,128)S(1)}, u32[]{:S(2)}, u32[]{:S(2)}) collective-permute-start(f32[8,8,128]{2,1,0:T(8,128)S(1)} %bitcast_add_fusion), channel_id=1, source_target_pairs={{0,8},{2,10},{4,12},{6,14},{8,0},{10,2},{12,4},{14,6},{16,24},{18,... | collective-permute-start | bytes 98312 | tf_op jit(solution)/shard_map/ppermute | solution.py:532
  22.8 1.4 %collective-permute-start.7 = (f32[8,8,128]{2,1,0:T(8,128)S(1)}, f32[8,8,128]{2,1,0:T(8,128)S(1)}, u32[]{:S(2)}, u32[]{:S(2)}) collective-permute-start(f32[8,8,128]{2,1,0:T(8,128)S(1)} %bitcast_add_fusion), channel_id=1, source_target_pairs={{0,12},{2,14},{4,8},{6,10},{8,4},{10,6},{12,0},{14,2},{16,28},{18,... | collective-permute-start | bytes 98312 | tf_op jit(solution)/shard_map/ppermute | solution.py:532
  24.2 0.3 collective-permute-start.5
  24.5 0.4 %collective-permute-done.6 = f32[8,8,128]{2,1,0:T(8,128)S(1)} collective-permute-done((f32[8,8,128]{2,1,0:T(8,128)S(1)}, f32[8,8,128]{2,1,0:T(8,128)S(1)}, u32[]{:S(2)}, u32[]{:S(2)}) %collective-permute-start.6) | collective-permute-done | bytes 32800 | tf_op jit(solution)/shard_map/ppermute | solution.py:532
  24.9 2.7 %collective-permute-done.7 = f32[8,8,128]{2,1,0:T(8,128)S(1)} collective-permute-done((f32[8,8,128]{2,1,0:T(8,128)S(1)}, f32[8,8,128]{2,1,0:T(8,128)S(1)}, u32[]{:S(2)}, u32[]{:S(2)}) %collective-permute-start.7) | collective-permute-done | bytes 32800 | tf_op jit(solution)/shard_map/ppermute | solution.py:532
  27.7 0.5 %collective-permute-done.5 = f32[8,8,128]{2,1,0:T(8,128)S(1)} collective-permute-done((f32[8,8,128]{2,1,0:T(8,128)S(1)}, f32[8,8,128]{2,1,0:T(8,128)S(1)}, u32[]{:S(2)}, u32[]{:S(2)}) %collective-permute-start.5) | collective-permute-done | bytes 32800 | tf_op jit(solution)/shard_map/ppermute | solution.py:532
  28.2 2.7 %collective-permute-start.8 = (f32[8,8,128]{2,1,0:T(8,128)S(1)}, f32[8,8,128]{2,1,0:T(8,128)S(1)}, u32[]{:S(2)}, u32[]{:S(2)}) collective-permute-start(f32[8,8,128]{2,1,0:T(8,128)S(1)} %add_add_fusion), channel_id=1, source_target_pairs={{0,16},{2,18},{4,20},{6,22},{8,24},{10,26},{12,28},{14,30},{16,0},... | collective-permute-start | bytes 98312 | tf_op jit(solution)/shard_map/ppermute | solution.py:532
  30.8 2.2 %collective-permute-done.8 = f32[8,8,128]{2,1,0:T(8,128)S(1)} collective-permute-done((f32[8,8,128]{2,1,0:T(8,128)S(1)}, f32[8,8,128]{2,1,0:T(8,128)S(1)}, u32[]{:S(2)}, u32[]{:S(2)}) %collective-permute-start.8) | collective-permute-done | bytes 32800 | tf_op jit(solution)/shard_map/ppermute | solution.py:532
  33.1 0.7 %share.1 = f32[12,1,1326]{2,1,0:T(1,128)} custom-call(f32[16,8,128]{2,1,0:T(8,128)S(1)} %get-tuple-element.31.tiles_ref), custom_call_target="tpu_custom_call" | custom-call | tf_op jit(solution)/shard_map/share/pallas_call | solution.py:553
  33.8 0.5 %collective-permute-done.9.other_ref = f32[8,8,128]{2,1,0:T(8,128)S(1)} collective-permute-done((f32[8,8,128]{2,1,0:T(8,128)S(1)}, f32[8,8,128]{2,1,0:T(8,128)S(1)}, u32[]{:S(2)}, u32[]{:S(2)}) %collective-permute-start.9) | collective-permute-done | bytes 32800 | tf_op jit(solution)/shard_map/ppermute | solution.py:532
  34.3 0.7 %root.1 = f32[12,1326]{1,0:T(8,128)} custom-call(f32[8,8,128]{2,1,0:T(8,128)S(1)} %add.58.mine_ref, f32[8,8,128]{2,1,0:T(8,128)S(1)} %collective-permute-done.9.other_ref), custom_call_target="tpu_custom_call" | custom-call | tf_op jit(solution)/shard_map/root/pallas_call | solution.py:565
  (12 shorter events, 0.2 us)
Async XLA Ops:
  1.9 12.0 %collective-permute-start.1 = (bf16[96,1326]{1,0:T(8,128)(2,1)S(1)}, bf16[96,1326]{1,0:T(8,128)(2,1)S(1)}, u32[]{:S(2)}, u32[]{:S(2)}) collective-permute-start(bf16[96,1326]{1,0:T(8,128)(2,1)S(1)} %slice.7), channel_id=1, source_target_pairs={{0,1},{1,0},{2,3},{3,2},{4,5},{5,4},{6,7},{7,6},{8,9},{9,8},{10,11... | collective-permute-start | bytes 763784 | tf_op jit(solution)/shard_map/ppermute | solution.py:415
  7.3 6.6 %collective-permute-start.2 = (bf16[16,1326]{1,0:T(8,128)(2,1)}, bf16[16,1326]{1,0:T(8,128)(2,1)S(1)}, u32[]{:S(2)}, u32[]{:S(2)}) collective-permute-start(bf16[16,1326]{1,0:T(8,128)(2,1)} %get-tuple-element.23), channel_id=1, source_target_pairs={{0,1},{1,0},{2,3},{3,2},{4,5},{5,4},{6,7},{7,6},{8,9},{9,8},{10,11... | collective-permute-start | bytes 127304 | tf_op jit(solution)/shard_map/ppermute | solution.py:415
  7.4 7.9 %collective-permute-start = (bf16[48,1326]{1,0:T(8,128)(2,1)S(1)}, bf16[48,1326]{1,0:T(8,128)(2,1)S(1)}, u32[]{:S(2)}, u32[]{:S(2)}) collective-permute-start(bf16[48,1326]{1,0:T(8,128)(2,1)S(1)} %slice.6), channel_id=1, source_target_pairs={{0,1},{1,0},{2,3},{3,2},{4,5},{5,4},{6,7},{7,6},{8,9},{9,8},{10,11... | collective-permute-start | bytes 381896 | tf_op jit(solution)/shard_map/ppermute | solution.py:415
  9.4 0.9 %copy-start = (f32[24,1408]{1,0:T(8,128)S(1)}, f32[24,1408]{1,0:T(8,128)}, u32[]{:S(2)}) copy-start(f32[24,1408]{1,0:T(8,128)} %get-tuple-element.18.info_ref) | copy-start | bytes 405508
  15.4 4.3 %collective-permute-start.3 = (f32[16,8,128]{2,1,0:T(8,128)S(1)}, f32[16,8,128]{2,1,0:T(8,128)S(1)}, u32[]{:S(2)}, u32[]{:S(2)}) collective-permute-start(f32[16,8,128]{2,1,0:T(8,128)S(1)} %get-tuple-element.29), channel_id=1, source_target_pairs={{0,1},{1,0},{2,3},{3,2},{4,5},{5,4},{6,7},{7,6},{8,9},{9,8},{10,11... | collective-permute-start | bytes 196616 | tf_op jit(solution)/shard_map/ppermute | solution.py:415
  19.7 1.3 %collective-permute-start.4 = (f32[8,8,128]{2,1,0:T(8,128)S(1)}, f32[8,8,128]{2,1,0:T(8,128)S(1)}, u32[]{:S(2)}, u32[]{:S(2)}) collective-permute-start(f32[8,8,128]{2,1,0:T(8,128)S(1)} %dynamic-slice_bitcast_fusion), channel_id=1, source_target_pairs={{0,2},{2,0},{4,6},{6,4},{8,10},{10,8},{12,14},{14,12},{16,18},{18,... | collective-permute-start | bytes 98312 | tf_op jit(solution)/shard_map/ppermute | solution.py:532
  21.0 3.9 %collective-permute-start.6 = (f32[8,8,128]{2,1,0:T(8,128)S(1)}, f32[8,8,128]{2,1,0:T(8,128)S(1)}, u32[]{:S(2)}, u32[]{:S(2)}) collective-permute-start(f32[8,8,128]{2,1,0:T(8,128)S(1)} %bitcast_add_fusion), channel_id=1, source_target_pairs={{0,8},{2,10},{4,12},{6,14},{8,0},{10,2},{12,4},{14,6},{16,24},{18,... | collective-permute-start | bytes 98312 | tf_op jit(solution)/shard_map/ppermute | solution.py:532
  22.8 4.8 %collective-permute-start.7 = (f32[8,8,128]{2,1,0:T(8,128)S(1)}, f32[8,8,128]{2,1,0:T(8,128)S(1)}, u32[]{:S(2)}, u32[]{:S(2)}) collective-permute-start(f32[8,8,128]{2,1,0:T(8,128)S(1)} %bitcast_add_fusion), channel_id=1, source_target_pairs={{0,12},{2,14},{4,8},{6,10},{8,4},{10,6},{12,0},{14,2},{16,28},{18,... | collective-permute-start | bytes 98312 | tf_op jit(solution)/shard_map/ppermute | solution.py:532
  24.2 3.9 %collective-permute-start.5 = (f32[8,8,128]{2,1,0:T(8,128)S(1)}, f32[8,8,128]{2,1,0:T(8,128)S(1)}, u32[]{:S(2)}, u32[]{:S(2)}) collective-permute-start(f32[8,8,128]{2,1,0:T(8,128)S(1)} %bitcast_add_fusion), channel_id=1, source_target_pairs={{0,4},{2,6},{4,0},{6,2},{8,12},{10,14},{12,8},{14,10},{16,20},{18,... | collective-permute-start | bytes 98312 | tf_op jit(solution)/shard_map/ppermute | solution.py:532
  28.2 4.9 %collective-permute-start.8 = (f32[8,8,128]{2,1,0:T(8,128)S(1)}, f32[8,8,128]{2,1,0:T(8,128)S(1)}, u32[]{:S(2)}, u32[]{:S(2)}) collective-permute-start(f32[8,8,128]{2,1,0:T(8,128)S(1)} %add_add_fusion), channel_id=1, source_target_pairs={{0,16},{2,18},{4,20},{6,22},{8,24},{10,26},{12,28},{14,30},{16,0},... | collective-permute-start | bytes 98312 | tf_op jit(solution)/shard_map/ppermute | solution.py:532
  33.1 1.2 %collective-permute-start.9 = (f32[8,8,128]{2,1,0:T(8,128)S(1)}, f32[8,8,128]{2,1,0:T(8,128)S(1)}, u32[]{:S(2)}, u32[]{:S(2)}) collective-permute-start(f32[8,8,128]{2,1,0:T(8,128)S(1)} %add.58.mine_ref), channel_id=1, source_target_pairs={{0,2},{2,0},{4,6},{6,4},{8,10},{10,8},{12,14},{14,12},{16,18},{18,... | collective-permute-start | bytes 98312 | tf_op jit(solution)/shard_map/ppermute | solution.py:532

commit v10 on v6

--- a/solution.py
+++ b/solution.py
@@ -199,7 +199,7 @@
     kept.wait()
 
 
-def build_kernel(rounds, info_ref, payoff_ref, kept_ref, ranks, gaps, holds, lacks):
+def build_kernel(rounds, info_ref, payoff_ref, kept_ref, holds, lacks):
     padded = payoff_ref.shape[-1]
     kept_ref[...] = info_ref[...]
 
@@ -208,16 +208,6 @@
     held = jnp.where((card == low) | (card == high), 1.0, 0.0)
     holds[...] = jnp.where(card == DECK, 1.0, held).astype(jnp.bfloat16)
     lacks[...] = jnp.where(card == DECK, 1.0, -held).astype(jnp.bfloat16)
-    row = lax.broadcasted_iota(jnp.int32, (ranks.shape[1], padded), 0)
-    for at in range(rounds):
-        rank = info_ref[at : at + 1, :]
-        top = jnp.floor(rank * (1.0 / LANES)) * LANES
-        rest = rank - top
-        sides = jnp.where(row % 2 == 0, top, rest)
-        ones = jnp.where(row < 4, 1.0, 0.0)
-        ranks[at] = jnp.where(row < 2, -sides, ones).astype(jnp.bfloat16)
-        gaps[at] = jnp.where(row < 2, ones, jnp.where(row < 4, sides, 0.0)).astype(jnp.bfloat16)
-
     def product(left, right):
         return lax.dot_general(
             left, right, (((0,), (0,)), ((), ())), preferred_element_type=jnp.float32
@@ -225,13 +215,21 @@
 
     for start in range(0, padded, LANES):
         rows = slice(start, start + LANES)
+        columns = [
+            jnp.broadcast_to(info_ref[at : at + 1, rows], (LANES, LANES)).T
+            for at in range(rounds)
+        ]
         for lane in range(0, padded, 2 * LANES):
             here = slice(lane, min(lane + 2 * LANES, padded))
             mask = product(holds[:, rows], lacks[:, here])
             if here.start <= start < here.stop:
                 mask = jnp.maximum(mask, 0.0)
             for at in range(rounds):
-                gap = product(ranks[at, :, rows], gaps[at, :, here])
+                pieces = [
+                    (info_ref[at : at + 1, left : left + LANES] - columns[at]).astype(jnp.bfloat16)
+                    for left in range(here.start, here.stop, LANES)
+                ]
+                gap = jnp.concatenate(pieces, axis=1)
                 payoff_ref[at, rows, here] = jnp.maximum(jnp.minimum(gap, mask), -mask)
 
 
@@ -469,8 +467,6 @@
         in_specs=[vmem],
         out_specs=[vmem] * 2,
         scratch_shapes=[
-            pltpu.VMEM((rounds, 16, padded), jnp.bfloat16),
-            pltpu.VMEM((rounds, 16, padded), jnp.bfloat16),
             pltpu.VMEM((round_up(DECK + 1, 16), padded), jnp.bfloat16),
             pltpu.VMEM((round_up(DECK + 1, 16), padded), jnp.bfloat16),
         ],

time: 37.5 us -> 35.6 us (0.949); the launches traced: 37.3 us -> 35 us
  waiting for transfers between devices: 12.2 us -> 9.66 us
  starting transfers between devices: 11.8 us -> 13.1 us
  Pallas kernels: 9 us -> 7.95 us
    ppermute x6, waiting for transfers between devices: 9.53 us -> 7.54 us  [swap(): lax.ppermute(array, 'board', [(at, at ^ step) for at in range(board_count)])]
    pallas_call x1, Pallas kernels: 4.38 us -> 3.34 us  [body(): pl.pallas_call(functools.partial(build_kernel, rounds), out_shape=[jax.Sh...]
    ppermute x4, starting transfers between devices: 6.09 us -> 6.9 us  [shift(): lax.ppermute(array, 'seq', [(at, (at + step) % seq_count) for at in range...]
    ppermute x4, waiting for transfers between devices: 2.68 us -> 2.12 us  [shift(): lax.ppermute(array, 'seq', [(at, (at + step) % seq_count) for at in range...]
    ppermute x6, starting transfers between devices: 5.7 us -> 6.22 us  [swap(): lax.ppermute(array, 'board', [(at, at ^ step) for at in range(board_count)])]
  transfers between devices with their start and end apart: 10 -> 10, of which waited for: 6 -> 8; matrix products, arithmetic and copies ran while one was open for 0% -> 0% of each run, Pallas kernels for 22% -> 20%
where the time goes in v10:
time: 35.6 us; the launch traced here: 35 us
  starting transfers between devices  13.1 us (37%)
  waiting for transfers between devices  9.66 us (27%)
  Pallas kernels  7.95 us (22%)
  local copies, waits for them, and re-layouts  2.15 us (6%)
  between operations  2.08 us (6%)
    ppermute x6, waiting for transfers between devices, swap(): lax.ppermute(array, 'board', [(at, at ^ step) for at in range(board_count)])  7.54 us
    ppermute x4, starting transfers between devices, shift(): lax.ppermute(array, 'seq', [(at, (at + step) % seq_count) for at in range...  6.9 us
    ppermute x6, starting transfers between devices, swap(): lax.ppermute(array, 'board', [(at, at ^ step) for at in range(board_count)])  6.22 us
    pallas_call x1, Pallas kernels, body(): pl.pallas_call(functools.partial(build_kernel, rounds), out_shape=[jax.Sh...  3.34 us
    ppermute x4, waiting for transfers between devices, shift(): lax.ppermute(array, 'seq', [(at, (at + step) % seq_count) for at in range...  2.12 us
    pallas_call x1, Pallas kernels, body(): pl.pallas_call(functools.partial(pack_kernel, rounds, seq_count), out_sha...  1.71 us
    pallas_call x1, Pallas kernels, body(): pl.pallas_call(functools.partial(head_kernel, rounds, seq_count, nodes, l...  1.26 us
    dynamic_slice x1, local copies, waits for them, and re-layouts, strategy_for(): rows = lax.dynamic_slice_in_dim(split, owner, 1, axis=1)  1.19 us
  transfers between devices with their start and end apart: 10, of which 8 were waited for; matrix products, arithmetic and copies ran while one was open for 0% of the time, Pallas kernels for 20%

profile of v10, /device:TPU:0, one launch (start us, length us, event | category | flops | bytes accessed | tf_op | source)
XLA Modules:
  0.0 35.0 jit_solution(14679251891086933231)
XLA Ops:
  0.7 1.2 %constant_dynamic-slice_fusion = (bf16[3,1,48,1326]{3,2,1,0:T(8,128)(2,1)S(1)}, bf16[3,1,48,1326]{3,2,1,0:T(8,128)(2,1)S(1)}) fusion(bf16[3,2,48,1326]{3,2,1,0:T(8,128)(2,1)} %bitcast.22, s32[]{:T(128)S(6)} %select_n.31, s32[]{:T(128)S(6)} %select_n.29), kind=kLoop, calls=%fused_computation.4 | loop fusion | bytes 1527560 | tf_op jit(solution)/shard_map/dynamic_slice | solution.py:408
  1.9 3.0 %collective-permute-start.1 = (bf16[96,1326]{1,0:T(8,128)(2,1)S(1)}, bf16[96,1326]{1,0:T(8,128)(2,1)S(1)}, u32[]{:S(2)}, u32[]{:S(2)}) collective-permute-start(bf16[96,1326]{1,0:T(8,128)(2,1)S(1)} %slice.7), channel_id=1, source_target_pairs={{0,1},{1,0},{2,3},{3,2},{4,5},{5,4},{6,7},{7,6},{8,9},{9,8},{10,11... | collective-permute-start | bytes 763784 | tf_op jit(solution)/shard_map/ppermute | solution.py:400
  5.5 1.7 %pack.1 = (bf16[16,1326]{1,0:T(8,128)(2,1)}, f32[24,1408]{1,0:T(8,128)}) custom-call(bf16[1,12,1326]{2,1,0:T(8,128)(2,1)} %reach_ref.1, s32[1,48]{1,0:T(1,128)} %bitcast.28, f32[1,48]{1,0:T(1,128)} %bitcast.29, s32[6,1,1326]{2,1,0:T(1,128)} %bitcast.26, s32[5,1,6]{2,1,0:T(1,128)} %bitcast.27, s32[1]{0:T(128)S(6)} %copy.14.count_ref), custom_call_target="tpu_custom_call" | custom-call | tf_op jit(solution)/shard_map/pack/pallas_call | solution.py:427
  7.3 0.1 collective-permute-start.2
  7.4 2.1 %collective-permute-start = (bf16[48,1326]{1,0:T(8,128)(2,1)S(1)}, bf16[48,1326]{1,0:T(8,128)(2,1)S(1)}, u32[]{:S(2)}, u32[]{:S(2)}) collective-permute-start(bf16[48,1326]{1,0:T(8,128)(2,1)S(1)} %slice.6), channel_id=1, source_target_pairs={{0,1},{1,0},{2,3},{3,2},{4,5},{5,4},{6,7},{7,6},{8,9},{9,8},{10,11... | collective-permute-start | bytes 381896 | tf_op jit(solution)/shard_map/ppermute | solution.py:400
  9.4 0.9 %copy-done = f32[24,1408]{1,0:T(8,128)S(1)} copy-done((f32[24,1408]{1,0:T(8,128)S(1)}, f32[24,1408]{1,0:T(8,128)}, u32[]{:S(2)}) %copy-start) | copy-done | bytes 135192
  10.3 3.3 %build.1 = (bf16[3,1408,1408]{2,1,0:T(8,128)(2,1)S(1)}, f32[24,1408]{1,0:T(8,128)S(1)}) custom-call(f32[24,1408]{1,0:T(8,128)S(1)} %copy-done), custom_call_target="tpu_custom_call" | custom-call | flops 59473920 | bytes 7929856 | tf_op jit(solution)/shard_map/build/pallas_call | solution.py:461
  13.7 1.3 %head.1 = (f32[24,1408]{1,0:T(8,128)S(1)}, bf16[2,96,128]{2,1,0:T(8,128)(2,1)S(1)}, f32[96,128]{1,0:T(8,128)S(1)}, f32[96,1326]{1,0:T(8,128)S(1)}) custom-call(bf16[3,1408,1408]{2,1,0:T(8,128)(2,1)S(1)} %get-tuple-element.19.refs_0_, f32[24,1408]{1,0:T(8,128)S(1)} %get-tuple-element.20.refs_1_, bf16[144,1326]{1,0:T(8,128)(2,1)S(1)} %bitcast.18, ...), custom_call_target="tpu_custom_call" | custom-call | flops 1141899264 | bytes 11894784 | tf_op jit(solution)/shard_map/head/pallas_call | solution.py:481
  15.0 0.3 collective-permute-done.refs_3_
  15.2 0.2 tail.1
  15.4 1.7 %collective-permute-start.3 = (f32[16,8,128]{2,1,0:T(8,128)S(1)}, f32[16,8,128]{2,1,0:T(8,128)S(1)}, u32[]{:S(2)}, u32[]{:S(2)}) collective-permute-start(f32[16,8,128]{2,1,0:T(8,128)S(1)} %get-tuple-element.29), channel_id=1, source_target_pairs={{0,1},{1,0},{2,3},{3,2},{4,5},{5,4},{6,7},{7,6},{8,9},{9,8},{10,11... | collective-permute-start | bytes 196616 | tf_op jit(solution)/shard_map/ppermute | solution.py:400
  17.8 1.9 %collective-permute-done.3 = f32[16,8,128]{2,1,0:T(8,128)S(1)} collective-permute-done((f32[16,8,128]{2,1,0:T(8,128)S(1)}, f32[16,8,128]{2,1,0:T(8,128)S(1)}, u32[]{:S(2)}, u32[]{:S(2)}) %collective-permute-start.3) | collective-permute-done | bytes 65568 | tf_op jit(solution)/shard_map/ppermute | solution.py:400
  19.8 1.2 %collective-permute-done.4 = f32[8,8,128]{2,1,0:T(8,128)S(1)} collective-permute-done((f32[8,8,128]{2,1,0:T(8,128)S(1)}, f32[8,8,128]{2,1,0:T(8,128)S(1)}, u32[]{:S(2)}, u32[]{:S(2)}) %collective-permute-start.4) | collective-permute-done | bytes 32800 | tf_op jit(solution)/shard_map/ppermute | solution.py:515
  21.0 1.8 %collective-permute-start.6 = (f32[8,8,128]{2,1,0:T(8,128)S(1)}, f32[8,8,128]{2,1,0:T(8,128)S(1)}, u32[]{:S(2)}, u32[]{:S(2)}) collective-permute-start(f32[8,8,128]{2,1,0:T(8,128)S(1)} %bitcast_add_fusion), channel_id=1, source_target_pairs={{0,8},{2,10},{4,12},{6,14},{8,0},{10,2},{12,4},{14,6},{16,24},{18,... | collective-permute-start | bytes 98312 | tf_op jit(solution)/shard_map/ppermute | solution.py:515
  22.8 1.4 %collective-permute-start.7 = (f32[8,8,128]{2,1,0:T(8,128)S(1)}, f32[8,8,128]{2,1,0:T(8,128)S(1)}, u32[]{:S(2)}, u32[]{:S(2)}) collective-permute-start(f32[8,8,128]{2,1,0:T(8,128)S(1)} %bitcast_add_fusion), channel_id=1, source_target_pairs={{0,12},{2,14},{4,8},{6,10},{8,4},{10,6},{12,0},{14,2},{16,28},{18,... | collective-permute-start | bytes 98312 | tf_op jit(solution)/shard_map/ppermute | solution.py:515
  24.2 0.3 collective-permute-start.5
  24.5 0.4 %collective-permute-done.6 = f32[8,8,128]{2,1,0:T(8,128)S(1)} collective-permute-done((f32[8,8,128]{2,1,0:T(8,128)S(1)}, f32[8,8,128]{2,1,0:T(8,128)S(1)}, u32[]{:S(2)}, u32[]{:S(2)}) %collective-permute-start.6) | collective-permute-done | bytes 32800 | tf_op jit(solution)/shard_map/ppermute | solution.py:515
  24.9 2.7 %collective-permute-done.7 = f32[8,8,128]{2,1,0:T(8,128)S(1)} collective-permute-done((f32[8,8,128]{2,1,0:T(8,128)S(1)}, f32[8,8,128]{2,1,0:T(8,128)S(1)}, u32[]{:S(2)}, u32[]{:S(2)}) %collective-permute-start.7) | collective-permute-done | bytes 32800 | tf_op jit(solution)/shard_map/ppermute | solution.py:515
  27.7 0.5 %collective-permute-done.5 = f32[8,8,128]{2,1,0:T(8,128)S(1)} collective-permute-done((f32[8,8,128]{2,1,0:T(8,128)S(1)}, f32[8,8,128]{2,1,0:T(8,128)S(1)}, u32[]{:S(2)}, u32[]{:S(2)}) %collective-permute-start.5) | collective-permute-done | bytes 32800 | tf_op jit(solution)/shard_map/ppermute | solution.py:515
  28.2 2.7 %collective-permute-start.8 = (f32[8,8,128]{2,1,0:T(8,128)S(1)}, f32[8,8,128]{2,1,0:T(8,128)S(1)}, u32[]{:S(2)}, u32[]{:S(2)}) collective-permute-start(f32[8,8,128]{2,1,0:T(8,128)S(1)} %add_add_fusion), channel_id=1, source_target_pairs={{0,16},{2,18},{4,20},{6,22},{8,24},{10,26},{12,28},{14,30},{16,0},... | collective-permute-start | bytes 98312 | tf_op jit(solution)/shard_map/ppermute | solution.py:515
  30.8 2.2 %collective-permute-done.8 = f32[8,8,128]{2,1,0:T(8,128)S(1)} collective-permute-done((f32[8,8,128]{2,1,0:T(8,128)S(1)}, f32[8,8,128]{2,1,0:T(8,128)S(1)}, u32[]{:S(2)}, u32[]{:S(2)}) %collective-permute-start.8) | collective-permute-done | bytes 32800 | tf_op jit(solution)/shard_map/ppermute | solution.py:515
  33.1 0.7 %share.1 = f32[12,1,1326]{2,1,0:T(1,128)} custom-call(f32[16,8,128]{2,1,0:T(8,128)S(1)} %get-tuple-element.31.tiles_ref), custom_call_target="tpu_custom_call" | custom-call | tf_op jit(solution)/shard_map/share/pallas_call | solution.py:536
  33.8 0.5 %collective-permute-done.9.other_ref = f32[8,8,128]{2,1,0:T(8,128)S(1)} collective-permute-done((f32[8,8,128]{2,1,0:T(8,128)S(1)}, f32[8,8,128]{2,1,0:T(8,128)S(1)}, u32[]{:S(2)}, u32[]{:S(2)}) %collective-permute-start.9) | collective-permute-done | bytes 32800 | tf_op jit(solution)/shard_map/ppermute | solution.py:515
  34.3 0.7 %root.1 = f32[12,1326]{1,0:T(8,128)} custom-call(f32[8,8,128]{2,1,0:T(8,128)S(1)} %add.58.mine_ref, f32[8,8,128]{2,1,0:T(8,128)S(1)} %collective-permute-done.9.other_ref), custom_call_target="tpu_custom_call" | custom-call | tf_op jit(solution)/shard_map/root/pallas_call | solution.py:548
  (12 shorter events, 0.2 us)
Async XLA Ops:
  1.9 11.8 %collective-permute-start.1 = (bf16[96,1326]{1,0:T(8,128)(2,1)S(1)}, bf16[96,1326]{1,0:T(8,128)(2,1)S(1)}, u32[]{:S(2)}, u32[]{:S(2)}) collective-permute-start(bf16[96,1326]{1,0:T(8,128)(2,1)S(1)} %slice.7), channel_id=1, source_target_pairs={{0,1},{1,0},{2,3},{3,2},{4,5},{5,4},{6,7},{7,6},{8,9},{9,8},{10,11... | collective-permute-start | bytes 763784 | tf_op jit(solution)/shard_map/ppermute | solution.py:400
  7.3 6.4 %collective-permute-start.2 = (bf16[16,1326]{1,0:T(8,128)(2,1)}, bf16[16,1326]{1,0:T(8,128)(2,1)S(1)}, u32[]{:S(2)}, u32[]{:S(2)}) collective-permute-start(bf16[16,1326]{1,0:T(8,128)(2,1)} %get-tuple-element.23), channel_id=1, source_target_pairs={{0,1},{1,0},{2,3},{3,2},{4,5},{5,4},{6,7},{7,6},{8,9},{9,8},{10,11... | collective-permute-start | bytes 127304 | tf_op jit(solution)/shard_map/ppermute | solution.py:400
  7.4 7.9 %collective-permute-start = (bf16[48,1326]{1,0:T(8,128)(2,1)S(1)}, bf16[48,1326]{1,0:T(8,128)(2,1)S(1)}, u32[]{:S(2)}, u32[]{:S(2)}) collective-permute-start(bf16[48,1326]{1,0:T(8,128)(2,1)S(1)} %slice.6), channel_id=1, source_target_pairs={{0,1},{1,0},{2,3},{3,2},{4,5},{5,4},{6,7},{7,6},{8,9},{9,8},{10,11... | collective-permute-start | bytes 381896 | tf_op jit(solution)/shard_map/ppermute | solution.py:400
  9.4 0.9 %copy-start = (f32[24,1408]{1,0:T(8,128)S(1)}, f32[24,1408]{1,0:T(8,128)}, u32[]{:S(2)}) copy-start(f32[24,1408]{1,0:T(8,128)} %get-tuple-element.18.info_ref) | copy-start | bytes 405508
  15.4 4.3 %collective-permute-start.3 = (f32[16,8,128]{2,1,0:T(8,128)S(1)}, f32[16,8,128]{2,1,0:T(8,128)S(1)}, u32[]{:S(2)}, u32[]{:S(2)}) collective-permute-start(f32[16,8,128]{2,1,0:T(8,128)S(1)} %get-tuple-element.29), channel_id=1, source_target_pairs={{0,1},{1,0},{2,3},{3,2},{4,5},{5,4},{6,7},{7,6},{8,9},{9,8},{10,11... | collective-permute-start | bytes 196616 | tf_op jit(solution)/shard_map/ppermute | solution.py:400
  19.7 1.3 %collective-permute-start.4 = (f32[8,8,128]{2,1,0:T(8,128)S(1)}, f32[8,8,128]{2,1,0:T(8,128)S(1)}, u32[]{:S(2)}, u32[]{:S(2)}) collective-permute-start(f32[8,8,128]{2,1,0:T(8,128)S(1)} %dynamic-slice_bitcast_fusion), channel_id=1, source_target_pairs={{0,2},{2,0},{4,6},{6,4},{8,10},{10,8},{12,14},{14,12},{16,18},{18,... | collective-permute-start | bytes 98312 | tf_op jit(solution)/shard_map/ppermute | solution.py:515
  21.0 3.9 %collective-permute-start.6 = (f32[8,8,128]{2,1,0:T(8,128)S(1)}, f32[8,8,128]{2,1,0:T(8,128)S(1)}, u32[]{:S(2)}, u32[]{:S(2)}) collective-permute-start(f32[8,8,128]{2,1,0:T(8,128)S(1)} %bitcast_add_fusion), channel_id=1, source_target_pairs={{0,8},{2,10},{4,12},{6,14},{8,0},{10,2},{12,4},{14,6},{16,24},{18,... | collective-permute-start | bytes 98312 | tf_op jit(solution)/shard_map/ppermute | solution.py:515
  22.8 4.8 %collective-permute-start.7 = (f32[8,8,128]{2,1,0:T(8,128)S(1)}, f32[8,8,128]{2,1,0:T(8,128)S(1)}, u32[]{:S(2)}, u32[]{:S(2)}) collective-permute-start(f32[8,8,128]{2,1,0:T(8,128)S(1)} %bitcast_add_fusion), channel_id=1, source_target_pairs={{0,12},{2,14},{4,8},{6,10},{8,4},{10,6},{12,0},{14,2},{16,28},{18,... | collective-permute-start | bytes 98312 | tf_op jit(solution)/shard_map/ppermute | solution.py:515
  24.2 3.9 %collective-permute-start.5 = (f32[8,8,128]{2,1,0:T(8,128)S(1)}, f32[8,8,128]{2,1,0:T(8,128)S(1)}, u32[]{:S(2)}, u32[]{:S(2)}) collective-permute-start(f32[8,8,128]{2,1,0:T(8,128)S(1)} %bitcast_add_fusion), channel_id=1, source_target_pairs={{0,4},{2,6},{4,0},{6,2},{8,12},{10,14},{12,8},{14,10},{16,20},{18,... | collective-permute-start | bytes 98312 | tf_op jit(solution)/shard_map/ppermute | solution.py:515
  28.2 4.9 %collective-permute-start.8 = (f32[8,8,128]{2,1,0:T(8,128)S(1)}, f32[8,8,128]{2,1,0:T(8,128)S(1)}, u32[]{:S(2)}, u32[]{:S(2)}) collective-permute-start(f32[8,8,128]{2,1,0:T(8,128)S(1)} %add_add_fusion), channel_id=1, source_target_pairs={{0,16},{2,18},{4,20},{6,22},{8,24},{10,26},{12,28},{14,30},{16,0},... | collective-permute-start | bytes 98312 | tf_op jit(solution)/shard_map/ppermute | solution.py:515
  33.1 1.2 %collective-permute-start.9 = (f32[8,8,128]{2,1,0:T(8,128)S(1)}, f32[8,8,128]{2,1,0:T(8,128)S(1)}, u32[]{:S(2)}, u32[]{:S(2)}) collective-permute-start(f32[8,8,128]{2,1,0:T(8,128)S(1)} %add.58.mine_ref), channel_id=1, source_target_pairs={{0,2},{2,0},{4,6},{6,4},{8,10},{10,8},{12,14},{14,12},{16,18},{18,... | collective-permute-start | bytes 98312 | tf_op jit(solution)/shard_map/ppermute | solution.py:515
